TPU v7x, 32 devices: a whole 2x2x4 slice. The times are simulated.
32 devices in a mesh: section: 2 (over y), head: 4 (over x, core), blk: 4 (over z).
Axes of the slice: x: 2, y: 2, z: 4, core: 2. Of those that a mesh axis runs over, the one named last changes fastest.
Arguments:
- tokens: bfloat16 [4, 1792, 768], P(None, ('head', 'blk')), may hold values from -6 to 6
- cotangent: float32 [4, 1792, 768], P(None, ('head', 'blk')), may hold values from -6 to 6
- doc_ids: int32 [4, 1792], P(None, ('head', 'blk')), may hold values from 0 to 10, as said below
- pad_mask: int32 [4, 1792], P(None, ('head', 'blk')), may hold values from 0 to 1, as said below
- w_query: bfloat16 [2, 768, 768], P('section', ('head', 'blk')), may hold values from -0.21875 to 0.21875
- w_key: bfloat16 [2, 768, 768], P('section', ('head', 'blk')), may hold values from -0.21875 to 0.21875
- w_value: bfloat16 [2, 768, 768], P('section', ('head', 'blk')), may hold values from -0.21875 to 0.21875
- w_out: bfloat16 [2, 768, 768], P('section', ('head', 'blk')), may hold values from -0.875 to 0.875
- b_query: bfloat16 [2, 768], P('section', ('head', 'blk')), may hold values from -1.5 to 1.5
- b_value: bfloat16 [2, 768], P('section', ('head', 'blk')), may hold values from -1.5 to 1.5
- b_out: bfloat16 [2, 768], P('section', ('head', 'blk')), may hold values from -1.5 to 1.5
- gain_attn: bfloat16 [2, 768], P('section', ('head', 'blk')), may hold values from 0.5 to 1.5
- bias_attn: bfloat16 [2, 768], P('section', ('head', 'blk')), may hold values from -1.5 to 1.5
- w_up: bfloat16 [2, 768, 3072], P('section', ('head', 'blk')), may hold values from -0.21875 to 0.21875
- b_up: bfloat16 [2, 3072], P('section', ('head', 'blk')), may hold values from -1.5 to 1.5
- w_down: bfloat16 [2, 3072, 768], P('section', ('head', 'blk')), may hold values from -0.109375 to 0.109375
- b_down: bfloat16 [2, 768], P('section', ('head', 'blk')), may hold values from -1.5 to 1.5
- gain_ffn: bfloat16 [2, 768], P('section', ('head', 'blk')), may hold values from 0.5 to 1.5
- bias_ffn: bfloat16 [2, 768], P('section', ('head', 'blk')), may hold values from -1.5 to 1.5
Outputs:
- layer_outputs: bfloat16 [2, 4, 1792, 768], P('section', None, ('head', 'blk'))
- input_grads: float32 [2, 4, 1792, 768], P('section', None, ('head', 'blk'))
- grad_w_query: float32 [2, 768, 768], P('section', ('head', 'blk'))
- grad_w_key: float32 [2, 768, 768], P('section', ('head', 'blk'))
- grad_w_value: float32 [2, 768, 768], P('section', ('head', 'blk'))
- grad_w_out: float32 [2, 768, 768], P('section', ('head', 'blk'))
- grad_b_query: float32 [2, 768], P('section', ('head', 'blk'))
- grad_b_value: float32 [2, 768], P('section', ('head', 'blk'))
- grad_b_out: float32 [2, 768], P('section', ('head', 'blk'))
- grad_gain_attn: float32 [2, 768], P('section', ('head', 'blk'))
- grad_bias_attn: float32 [2, 768], P('section', ('head', 'blk'))
- grad_w_up: float32 [2, 768, 3072], P('section', ('head', 'blk'))
- grad_b_up: float32 [2, 3072], P('section', ('head', 'blk'))
- grad_w_down: float32 [2, 3072, 768], P('section', ('head', 'blk'))
- grad_b_down: float32 [2, 768], P('section', ('head', 'blk'))
- grad_gain_ffn: float32 [2, 768], P('section', ('head', 'blk'))
- grad_bias_ffn: float32 [2, 768], P('section', ('head', 'blk'))
Inputs may be any that keep to these rules, and one draw needn't show every extreme that they name: `doc_ids`: document number of each token within its micro-batch: 0 at the first token, rising by one at the first token of each document and never falling; the padding belongs to the last document. Each micro-batch holds exactly 11 documents. `pad_mask`: 0 exactly on the last 1 to 223 tokens of each micro-batch (padding), 1 elsewhere; the last document holds at least one real token.
All inputs are finite; a program needn't handle non-finite values.
Results may differ from a plain program's by a relative error of at most 0.03.
Values may be sent and summed in bfloat16 or wider, within the bound.
No kernel may reach another device: no remote copies, remote signals or barrier semaphores. Data moves between devices by JAX's collectives and lax.ppermute only.
A program may use at most 320 MiB of HBM per device.

v0:
```python
import jax
import jax.numpy as jnp
from jax import lax
from jax.sharding import PartitionSpec as P

HEAD_DIM = 64


def shifted(value, axis, steps):
    count = lax.axis_size(axis)
    leading, last = (max(0, -steps), min(count, count - steps))
    return lax.ppermute(value, axis, [(source, source + steps) for source in range(leading, last)])


def layer_norm(value, gain, shift):
    centre = value - jnp.mean(value, axis=-1, keepdims=True)
    spread = jnp.mean(centre * centre, axis=-1, keepdims=True)
    return centre * lax.rsqrt(spread + 1e-05) * gain + shift


def gelu_exact(value):
    return jax.nn.gelu(value, approximate=False)


def split_pairs(portion, heads_here):
    half_width = portion.shape[1] // 2
    key_rows = portion[:, :half_width].reshape(portion.shape[0], heads_here, -1)
    value_rows = portion[:, half_width:].reshape(portion.shape[0], heads_here, -1)
    return (key_rows, value_rows)


def fold_keys(state_now, portion, queries, query_marks, key_marks):
    totals, running_max, weighted = state_now
    key_rows, value_rows = split_pairs(portion, queries.shape[1])
    scores = (
        jnp.einsum("qhc,khc->qhk", queries, key_rows, preferred_element_type=jnp.float32) * 0.125
    )
    allowed = (query_marks[:, None] == key_marks[None, :])[:, None, :]
    scores = jnp.where(allowed, scores, -1e30)
    new_max = jnp.maximum(running_max, jnp.max(scores, axis=-1))
    weights = jnp.where(allowed, jnp.exp(scores - new_max[..., None]), 0.0)
    totals = jnp.sum(weights, axis=-1)
    weighted = jnp.einsum(
        "qhk,khc->qhc", weights.astype(jnp.bfloat16), value_rows, preferred_element_type=jnp.float32
    )
    return (totals, new_max, weighted)


def key_group_grads(queries, grad_mixed, log_total, row_delta, query_marks, portion, marks):
    key_rows, value_rows = split_pairs(portion, queries.shape[1])
    scores = (
        jnp.einsum("qhc,khc->qhk", queries, key_rows, preferred_element_type=jnp.float32) * 0.125
    )
    allowed = (query_marks[:, None] == marks[None, :])[:, None, :]
    scores = jnp.where(allowed, scores, -1e30)
    probabilities = jnp.where(allowed, jnp.exp(scores - log_total[..., None]), 0.0)
    grad_prob = jnp.einsum(
        "qhc,khc->qhk", grad_mixed, value_rows, preferred_element_type=jnp.float32
    )
    grad_score = (probabilities * (grad_prob - row_delta[..., None])).astype(jnp.bfloat16)
    grad_query = (
        jnp.einsum("qhk,khc->qhc", grad_score, key_rows, preferred_element_type=jnp.float32) * 0.125
    )
    grad_key = (
        jnp.einsum("qhk,qhc->khc", grad_score, queries, preferred_element_type=jnp.float32) * 0.125
    )
    grad_value = jnp.einsum(
        "qhk,qhc->khc",
        probabilities.astype(jnp.bfloat16),
        grad_mixed,
        preferred_element_type=jnp.float32,
    )
    key_count = portion.shape[0]
    return (
        grad_query,
        jnp.concatenate(
            [grad_key.reshape(key_count, -1), grad_value.reshape(key_count, -1)], axis=1
        ),
    )


def body(
    tokens,
    cotangent,
    doc_ids,
    pad_mask,
    w_query,
    w_key,
    w_value,
    w_out,
    b_query,
    b_value,
    b_out,
    gain_attn,
    bias_attn,
    w_up,
    b_up,
    w_down,
    b_down,
    gain_ffn,
    bias_ffn,
):
    section_at = lax.axis_index("section")
    section_count = lax.axis_size("section")
    head_count = lax.axis_size("head")
    blk_count = lax.axis_size("blk")
    blk_at = lax.axis_index("blk")
    batches, tok_rows, model_width = tokens.shape
    head_width = model_width // head_count
    heads_here = head_width // HEAD_DIM
    row_count = head_count * tok_rows
    group_rows = row_count * min(4, blk_count)
    n_steps = batches + section_count - 1
    local_marks = jnp.where(pad_mask == 1, doc_ids, -1)
    all_ids, all_marks = (
        lax.all_gather(doc_ids, ("head", "blk"), axis=1, tiled=True),
        lax.all_gather(local_marks, ("head", "blk"), axis=1, tiled=True),
    )
    order_ids = (
        all_ids.reshape(batches, head_count, blk_count, tok_rows)
        .transpose(0, 2, 1, 3)
        .reshape(batches, -1)
    )
    order_marks = (
        all_marks.reshape(batches, head_count, blk_count, tok_rows)
        .transpose(0, 2, 1, 3)
        .reshape(batches, -1)
    )
    own_ids = lax.dynamic_slice_in_dim(order_ids, blk_at * row_count, row_count, 1)
    gathered = (
        lax.all_gather(w_query, ("head", "blk"), axis=1, tiled=True),
        lax.all_gather(w_key, ("head", "blk"), axis=1, tiled=True),
        lax.all_gather(w_value, ("head", "blk"), axis=1, tiled=True),
        lax.all_gather(w_out, ("head", "blk"), axis=1, tiled=True),
        lax.all_gather(b_query, ("head", "blk"), axis=1, tiled=True),
        lax.all_gather(b_value, ("head", "blk"), axis=1, tiled=True),
        lax.all_gather(b_out, ("head", "blk"), axis=1, tiled=True),
        lax.all_gather(gain_attn, ("head", "blk"), axis=1, tiled=True),
        lax.all_gather(bias_attn, ("head", "blk"), axis=1, tiled=True),
        lax.all_gather(w_up, ("head", "blk"), axis=1, tiled=True),
        lax.all_gather(b_up, ("head", "blk"), axis=1, tiled=True),
        lax.all_gather(w_down, ("head", "blk"), axis=1, tiled=True),
        lax.all_gather(b_down, ("head", "blk"), axis=1, tiled=True),
        lax.all_gather(gain_ffn, ("head", "blk"), axis=1, tiled=True),
        lax.all_gather(bias_ffn, ("head", "blk"), axis=1, tiled=True),
    )
    (
        query_full,
        key_full,
        value_full,
        out_full,
        query_shift,
        value_shift,
        out_shift,
        norm_gain,
        norm_shift,
        up_full,
        up_shift,
        down_full,
        down_shift,
        final_gain,
        final_shift,
    ) = [part[0] for part in gathered]
    joint_weight = jnp.concatenate(
        [
            query_full.reshape(model_width, head_count, head_width),
            key_full.reshape(model_width, head_count, head_width),
            value_full.reshape(model_width, head_count, head_width),
        ],
        axis=2,
    )
    joint_shift = jnp.concatenate(
        [
            query_shift.reshape(head_count, head_width).astype(jnp.float32),
            jnp.zeros((head_count, head_width), jnp.float32),
            value_shift.reshape(head_count, head_width).astype(jnp.float32),
        ],
        axis=1,
    )
    out_rows = out_full.reshape(head_count, head_width, model_width)
    out_bias = out_shift.astype(jnp.float32)
    gain_one = norm_gain.astype(jnp.float32)
    shift_one = norm_shift.astype(jnp.float32)
    up_bias = up_shift.astype(jnp.float32)
    down_bias = down_shift.astype(jnp.float32)
    gain_two = final_gain.astype(jnp.float32)
    shift_two = final_shift.astype(jnp.float32)
    received = jnp.zeros((tok_rows, model_width), jnp.bfloat16)
    outputs_all = jnp.zeros((batches, tok_rows, model_width), jnp.bfloat16)
    saved_list = []
    for step_at in range(n_steps):
        slot_at = step_at - section_at
        usable = (slot_at >= 0) & (slot_at < batches)
        picked = jnp.clip(slot_at, 0, batches - 1)
        own_rows = lax.dynamic_index_in_dim(tokens, picked, 0, keepdims=False)
        layer_in = jnp.where(section_at == 0, own_rows, received)
        forward_query_marks = own_ids[picked]
        forward_key_marks = order_marks[picked]
        joint_rows = jnp.einsum(
            "td,dgc->gtc", layer_in, joint_weight, preferred_element_type=jnp.float32
        )
        joint_rows = (joint_rows + joint_shift[:, None, :]).astype(jnp.bfloat16)
        arrived = lax.all_to_all(
            joint_rows.reshape(head_count, -1), "head", split_axis=0, concat_axis=0, tiled=True
        )
        arrived = arrived.reshape(row_count, 3 * head_width)
        forward_queries = arrived[:, :head_width].reshape(row_count, heads_here, HEAD_DIM)
        kv_pairs = arrived[:, head_width:]
        start_carry = (
            jnp.zeros((row_count, heads_here), jnp.float32),
            jnp.full((row_count, heads_here), -1e30, jnp.float32),
            jnp.zeros((row_count, heads_here, HEAD_DIM), jnp.float32),
        )
        forward_totals, running_max, weighted = fold_keys(
            start_carry,
            lax.all_gather(kv_pairs, "blk", axis=0, tiled=True),
            forward_queries,
            forward_query_marks,
            forward_key_marks,
        )
        forward_attended = weighted / forward_totals[..., None]
        forward_log_total = running_max + jnp.log(forward_totals)
        forward_returned = lax.all_to_all(
            forward_attended.astype(jnp.bfloat16).reshape(head_count, -1),
            "head",
            split_axis=0,
            concat_axis=0,
            tiled=True,
        )
        forward_returned = forward_returned.reshape(head_count, tok_rows, head_width)
        branch = (
            jnp.einsum(
                "gtc,gcd->td", forward_returned, out_rows, preferred_element_type=jnp.float32
            )
            + out_bias
        )
        forward_first_sum = layer_in.astype(jnp.float32) + branch
        middle = layer_norm(forward_first_sum, gain_one, shift_one)
        forward_middle_low = middle.astype(jnp.bfloat16)
        forward_hidden = (
            jnp.dot(forward_middle_low, up_full, preferred_element_type=jnp.float32) + up_bias
        )
        forward_active = gelu_exact(forward_hidden).astype(jnp.bfloat16)
        forward_second = (
            middle
            + jnp.dot(forward_active, down_full, preferred_element_type=jnp.float32)
            + down_bias
        )
        result = layer_norm(forward_second, gain_two, shift_two)
        forward_saved = (
            layer_in,
            forward_queries,
            kv_pairs,
            forward_attended,
            forward_log_total,
            forward_returned,
            forward_first_sum,
            forward_middle_low,
            forward_hidden,
            forward_active,
            forward_second,
        )
        result, saved = (result, forward_saved)
        outgoing = result.astype(jnp.bfloat16)
        current = lax.dynamic_index_in_dim(outputs_all, picked, 0, keepdims=False)
        outputs_all = lax.dynamic_update_index_in_dim(
            outputs_all, jnp.where(usable, outgoing, current), picked, 0
        )
        saved_list.append(saved)
        if step_at + 1 < n_steps:
            received = shifted(outgoing, "section", 1)
    stacked = jax.tree.map(lambda *parts: jnp.stack(parts), *saved_list)
    totals = tuple((jnp.zeros(part.shape[1:], jnp.float32) for part in gathered))
    grad_inputs = jnp.zeros((batches, tok_rows, model_width), jnp.float32)
    received_grad = jnp.zeros((tok_rows, model_width), jnp.bfloat16)
    for step_at in range(n_steps):
        slot_at = step_at - (section_count - 1 - section_at)
        usable = (slot_at >= 0) & (slot_at < batches)
        picked = jnp.clip(slot_at, 0, batches - 1)
        own_grad = lax.dynamic_index_in_dim(cotangent, picked, 0, keepdims=False)
        grad_top = jnp.where(
            section_at == section_count - 1, own_grad, received_grad.astype(jnp.float32)
        )
        forward_at = jnp.clip(picked + section_at, 0, n_steps - 1)
        saved = jax.tree.map(
            lambda part: lax.dynamic_index_in_dim(part, forward_at, 0, keepdims=False), stacked
        )
        query_marks = own_ids[picked]
        (
            backward_layer_in,
            queries,
            stored_pairs,
            attended,
            log_total,
            returned,
            first_sum,
            middle_low,
            hidden,
            active,
            second,
        ) = saved
        unused, pull_two = jax.vjp(layer_norm, second, gain_two, shift_two)
        grad_second, grad_gain_two, grad_shift_two = pull_two(grad_top)
        grad_down_low = grad_second.astype(jnp.bfloat16)
        grad_down_bias = jnp.sum(grad_down_low.astype(jnp.float32), axis=0)
        grad_down = jnp.einsum(
            "tf,td->fd", active, grad_down_low, preferred_element_type=jnp.float32
        )
        grad_active = jnp.einsum(
            "td,fd->tf", grad_down_low, down_full, preferred_element_type=jnp.float32
        )
        unused, pull_gelu = jax.vjp(gelu_exact, hidden)
        grad_hidden = pull_gelu(grad_active)[0].astype(jnp.bfloat16)
        grad_up_bias = jnp.sum(grad_hidden.astype(jnp.float32), axis=0)
        grad_up = jnp.einsum(
            "td,tf->df", middle_low, grad_hidden, preferred_element_type=jnp.float32
        )
        grad_middle = grad_second + jnp.einsum(
            "tf,df->td", grad_hidden, up_full, preferred_element_type=jnp.float32
        )
        unused, pull_one = jax.vjp(layer_norm, first_sum, gain_one, shift_one)
        grad_first, grad_gain_one, grad_shift_one = pull_one(grad_middle)
        grad_branch = grad_first.astype(jnp.bfloat16)
        grad_out_bias = jnp.sum(grad_branch.astype(jnp.float32), axis=0)
        grad_out = jnp.einsum(
            "gtc,td->gcd", returned, grad_branch, preferred_element_type=jnp.float32
        ).reshape(model_width, model_width)
        grad_returned = jnp.einsum(
            "td,gcd->gtc", grad_branch, out_rows, preferred_element_type=jnp.float32
        )
        grad_mixed = lax.all_to_all(
            grad_returned.astype(jnp.bfloat16).reshape(head_count, -1),
            "head",
            split_axis=0,
            concat_axis=0,
            tiled=True,
        )
        grad_mixed = grad_mixed.reshape(row_count, heads_here, HEAD_DIM)
        row_delta = jnp.sum(grad_mixed.astype(jnp.float32) * attended, axis=-1)
        all_pairs = lax.all_gather(stored_pairs, "blk", axis=0, tiled=True)
        group_count = all_pairs.shape[0] // group_rows
        grouped = all_pairs.reshape(group_count, group_rows, all_pairs.shape[1])
        grouped_marks = order_marks[picked].reshape(group_count, group_rows)

        def advance(grad_query, item):
            portion, marks = item
            part_query, part_terms = key_group_grads(
                queries, grad_mixed, log_total, row_delta, query_marks, portion, marks
            )
            return (grad_query + part_query, part_terms)

        grad_query, key_terms = lax.scan(
            advance,
            jnp.zeros((row_count, heads_here, HEAD_DIM), jnp.float32),
            (grouped, grouped_marks),
        )
        key_terms = key_terms.reshape(all_pairs.shape[0], all_pairs.shape[1])
        grad_pairs = lax.psum_scatter(
            key_terms.astype(jnp.bfloat16), "blk", scatter_dimension=0, tiled=True
        )
        grad_joint = jnp.concatenate(
            [grad_query.astype(jnp.bfloat16).reshape(row_count, head_width), grad_pairs], axis=1
        )
        grad_local = lax.all_to_all(
            grad_joint.reshape(head_count, -1), "head", split_axis=0, concat_axis=0, tiled=True
        )
        grad_local = grad_local.reshape(head_count, tok_rows, 3 * head_width)
        grad_joint_weight = jnp.einsum(
            "td,gtc->dgc", backward_layer_in, grad_local, preferred_element_type=jnp.float32
        )
        grad_joint_bias = jnp.sum(grad_local.astype(jnp.float32), axis=1)
        grad_input = grad_first + jnp.einsum(
            "gtc,dgc->td", grad_local, joint_weight, preferred_element_type=jnp.float32
        )
        grad_parts = (
            grad_joint_weight[:, :, :head_width].reshape(model_width, model_width),
            grad_joint_weight[:, :, head_width : 2 * head_width].reshape(model_width, model_width),
            grad_joint_weight[:, :, 2 * head_width :].reshape(model_width, model_width),
            grad_out,
            grad_joint_bias[:, :head_width].reshape(model_width),
            grad_joint_bias[:, 2 * head_width :].reshape(model_width),
            grad_out_bias,
            grad_gain_one,
            grad_shift_one,
            grad_up,
            grad_up_bias,
            grad_down,
            grad_down_bias,
            grad_gain_two,
            grad_shift_two,
        )
        grad_input, grad_parts = (grad_input, grad_parts)
        current = lax.dynamic_index_in_dim(grad_inputs, picked, 0, keepdims=False)
        grad_inputs = lax.dynamic_update_index_in_dim(
            grad_inputs, jnp.where(usable, grad_input, current), picked, 0
        )
        grad_parts = tuple((jnp.where(usable, part, 0.0) for part in grad_parts))
        totals = tuple((total + part for total, part in zip(totals, grad_parts)))
        if step_at + 1 < n_steps:
            received_grad = shifted(grad_input.astype(jnp.bfloat16), "section", -1)
    totals = (
        lax.psum_scatter(totals[0][None], ("head", "blk"), scatter_dimension=1, tiled=True),
        lax.psum_scatter(totals[1][None], ("head", "blk"), scatter_dimension=1, tiled=True),
        lax.psum_scatter(totals[2][None], ("head", "blk"), scatter_dimension=1, tiled=True),
        lax.psum_scatter(totals[3][None], ("head", "blk"), scatter_dimension=1, tiled=True),
        lax.psum_scatter(totals[4][None], ("head", "blk"), scatter_dimension=1, tiled=True),
        lax.psum_scatter(totals[5][None], ("head", "blk"), scatter_dimension=1, tiled=True),
        lax.psum_scatter(totals[6][None], ("head", "blk"), scatter_dimension=1, tiled=True),
        lax.psum_scatter(totals[7][None], ("head", "blk"), scatter_dimension=1, tiled=True),
        lax.psum_scatter(totals[8][None], ("head", "blk"), scatter_dimension=1, tiled=True),
        lax.psum_scatter(totals[9][None], ("head", "blk"), scatter_dimension=1, tiled=True),
        lax.psum_scatter(totals[10][None], ("head", "blk"), scatter_dimension=1, tiled=True),
        lax.psum_scatter(totals[11][None], ("head", "blk"), scatter_dimension=1, tiled=True),
        lax.psum_scatter(totals[12][None], ("head", "blk"), scatter_dimension=1, tiled=True),
        lax.psum_scatter(totals[13][None], ("head", "blk"), scatter_dimension=1, tiled=True),
        lax.psum_scatter(totals[14][None], ("head", "blk"), scatter_dimension=1, tiled=True),
    )
    return (
        outputs_all[None],
        grad_inputs[None],
        totals[0],
        totals[1],
        totals[2],
        totals[3],
        totals[4],
        totals[5],
        totals[6],
        totals[7],
        totals[8],
        totals[9],
        totals[10],
        totals[11],
        totals[12],
        totals[13],
        totals[14],
    )


def solution(mesh):
    placed = (
        P(None, ("head", "blk"), None),
        P(None, ("head", "blk"), None),
        P(None, ("head", "blk")),
        P(None, ("head", "blk")),
        P("section", ("head", "blk"), None),
        P("section", ("head", "blk"), None),
        P("section", ("head", "blk"), None),
        P("section", ("head", "blk"), None),
        P("section", ("head", "blk")),
        P("section", ("head", "blk")),
        P("section", ("head", "blk")),
        P("section", ("head", "blk")),
        P("section", ("head", "blk")),
        P("section", ("head", "blk"), None),
        P("section", ("head", "blk")),
        P("section", ("head", "blk"), None),
        P("section", ("head", "blk")),
        P("section", ("head", "blk")),
        P("section", ("head", "blk")),
    )
    return jax.shard_map(
        body,
        mesh=mesh,
        in_specs=placed,
        out_specs=(
            P("section", None, ("head", "blk"), None),
            P("section", None, ("head", "blk"), None),
            P("section", ("head", "blk"), None),
            P("section", ("head", "blk"), None),
            P("section", ("head", "blk"), None),
            P("section", ("head", "blk"), None),
            P("section", ("head", "blk")),
            P("section", ("head", "blk")),
            P("section", ("head", "blk")),
            P("section", ("head", "blk")),
            P("section", ("head", "blk")),
            P("section", ("head", "blk"), None),
            P("section", ("head", "blk")),
            P("section", ("head", "blk"), None),
            P("section", ("head", "blk")),
            P("section", ("head", "blk")),
            P("section", ("head", "blk")),
        ),
        check_vma=False,
    )
```

profile of v0, /device:TPU:0, one launch (start us, length us, event | category | flops | bytes accessed | tf_op | source)
XLA Modules:
  0.0 2631.5 jit_solution(396835379613935665)
XLA Ops:
  19.6 63.8 %all-reduce.9 = (bf16[3072]{0:T(1024)(128)(2,1)}, bf16[768]{0:T(1024)(128)(2,1)S(1)}, bf16[768]{0:T(1024)(128)(2,1)S(1)}, bf16[768]{0:T(1024)(128)(2,1)}, bf16[7...) all-reduce(bf16[3072]{0:T(1024)(128)(2,1)S(1)} %dynamic-update-slic, ...), channel_id=1, replica_groups=mesh['section'=2,'head'=4,'blk'=4] {'head','blk'}, use_global_device_ids=true, to_apply=%add.5 | all-reduce | flops 9216 | bytes 36864
  92.9 38.1 %all-gather.24.cloned.1.call-done = bf16[1,768,768]{2,1,0:T(8,128)(2,1)} async-done(((bf16[1,48,768]{2,1,0:T(8,128)(2,1)}), bf16[1,768,768]{2,1,0:T(8,128)(2,1)}) %all-gather.24.cloned.1.call-update) | async-done | bytes 1179664 | tf_op jit(solution)/shard_map/all_gather | solution.py:131
  161.7 30.9 %all-gather.6 = s32[16,112,4]{1,2,0:T(4,128)S(1)} all-gather(s32[1,112,4]{1,2,0:T(4,128)S(1)} %select_bitcast_fusion), channel_id=1, replica_groups=mesh['section'=2,'head'=4,'blk'=4] {'head','blk'}, dimensions={0}, use_global_device_ids=true | all-gather | bytes 30464 | tf_op jit(solution)/shard_map/all_gather | solution.py:117
  192.9 29.6 %all-gather.5 = s32[16,112,4]{1,2,0:T(4,128)S(1)} all-gather(s32[1,112,4]{1,2,0:T(4,128)S(1)} %bitcast.1683), channel_id=1, replica_groups=mesh['section'=2,'head'=4,'blk'=4] {'head','blk'}, dimensions={0}, use_global_device_ids=true | all-gather | bytes 30464 | tf_op jit(solution)/shard_map/all_gather | solution.py:116
  257.6 29.5 %all-gather.34.cloned.1.call-done = bf16[1,768,3072]{2,1,0:T(8,128)(2,1)} async-done(((bf16[1,48,3072]{2,1,0:T(8,128)(2,1)}), bf16[1,768,3072]{2,1,0:T(8,128)(2,1)}) %all-gather.34.cloned.1.call-update) | async-done | bytes 4718608 | tf_op jit(solution)/shard_map/all_gather | solution.py:140
  294.4 47.0 %all-gather.36.cloned.1.call-done = bf16[1,3072,768]{2,1,0:T(8,128)(2,1)} async-done(((bf16[1,192,768]{2,1,0:T(8,128)(2,1)}), bf16[1,3072,768]{2,1,0:T(8,128)(2,1)}) %all-gather.36.cloned.1.call-update) | async-done | bytes 4718608 | tf_op jit(solution)/shard_map/all_gather | solution.py:142
  381.1 33.4 %all-gather.38.cloned.1.call-done = bf16[1792,384]{1,0:T(8,128)(2,1)} async-done(((bf16[448,384]{1,0:T(8,128)(2,1)}), bf16[1792,384]{1,0:T(8,128)(2,1)}) %all-gather.38.cloned.1.call-update) | async-done | bytes 1376272 | tf_op jit(solution)/shard_map/all_gather | solution.py:216
  509.1 24.4 all-gather.40.cloned.1.call-done
  632.3 27.4 %all-gather.42.cloned.1.call-done = bf16[1792,384]{1,0:T(8,128)(2,1)} async-done(((bf16[448,384]{1,0:T(8,128)(2,1)}), bf16[1792,384]{1,0:T(8,128)(2,1)}) %all-gather.42.cloned.1.call-update) | async-done | bytes 1376272 | tf_op jit(solution)/shard_map/all_gather | solution.py:216
  777.6 23.4 all-gather.44.cloned.1.call-done
  943.0 25.0 reduce-scatter.39.cloned.1.call-done
  983.1 19.1 all-gather.48.cloned.1.call-done
  1100.0 26.8 %reduce-scatter.41.cloned.1.call-done = bf16[448,384]{1,0:T(8,128)(2,1)} async-done(((bf16[1792,384]{1,0:T(8,128)(2,1)}), bf16[448,384]{1,0:T(8,128)(2,1)}) %reduce-scatter.41.cloned.1.call-update) | async-done | bytes 344080 | tf_op jit(solution)/shard_map/reduce_scatter | solution.py:358
  1141.9 19.0 all-gather.50.cloned.1.call-done
  1262.2 24.7 reduce-scatter.43.cloned.1.call-done
  1302.1 19.0 all-gather.52.cloned.1.call-done
  1420.7 26.8 %reduce-scatter.45.cloned.1.call-done = bf16[448,384]{1,0:T(8,128)(2,1)} async-done(((bf16[1792,384]{1,0:T(8,128)(2,1)}), bf16[448,384]{1,0:T(8,128)(2,1)}) %reduce-scatter.45.cloned.1.call-update) | async-done | bytes 344080 | tf_op jit(solution)/shard_map/reduce_scatter | solution.py:358
  1462.7 18.9 all-gather.54.cloned.1.call-done
  1708.5 14.8 add_bitcast_fusion.1
  1745.8 14.6 add_bitcast_fusion
  1775.0 56.8 %reduce-scatter.73.cloned.1.call-done = f32[48,1]{1,0:T(8,128)} async-done(((f32[768,1]{1,0:T(8,128)}), f32[48,1]{1,0:T(8,128)}) %reduce-scatter.73.cloned.1.call-update) | async-done | bytes 208
  1833.1 57.1 %reduce-scatter.75.cloned.1.call-done = f32[48,1]{1,0:T(8,128)} async-done(((f32[768,1]{1,0:T(8,128)}), f32[48,1]{1,0:T(8,128)}) %reduce-scatter.75.cloned.1.call-update) | async-done | bytes 208
  1891.5 56.6 %reduce-scatter.77.cloned.1.call-done = f32[48,1]{1,0:T(8,128)} async-done(((f32[768,1]{1,0:T(8,128)}), f32[48,1]{1,0:T(8,128)}) %reduce-scatter.77.cloned.1.call-update) | async-done | bytes 208
  1949.5 61.3 %reduce-scatter.71.cloned.1.call-done = f32[192,1]{1,0:T(8,128)} async-done(((f32[3072,1]{1,0:T(8,128)}), f32[192,1]{1,0:T(8,128)}) %reduce-scatter.71.cloned.1.call-update) | async-done | bytes 784
  2015.7 53.1 %reduce-scatter.61.cloned.1.call-done = f32[48,1]{1,0:T(8,128)} async-done(((f32[768,1]{1,0:T(8,128)}), f32[48,1]{1,0:T(8,128)}) %reduce-scatter.61.cloned.1.call-update) | async-done | bytes 208
  2070.2 57.1 %reduce-scatter.63.cloned.1.call-done = f32[48,1]{1,0:T(8,128)} async-done(((f32[768,1]{1,0:T(8,128)}), f32[48,1]{1,0:T(8,128)}) %reduce-scatter.63.cloned.1.call-update) | async-done | bytes 208
  2128.6 65.1 %reduce-scatter.55.cloned.1.call-done = f32[1,48,768]{2,1,0:T(8,128)} async-done(((f32[1,768,768]{2,1,0:T(8,128)}), f32[1,48,768]{2,1,0:T(8,128)}) %reduce-scatter.55.cloned.1.call-update) | async-done | bytes 147472 | tf_op jit(solution)/shard_map/reduce_scatter | solution.py:405
  2193.6 66.8 %reduce-scatter.49.cloned.1.call-done = f32[1,48,768]{2,1,0:T(8,128)} async-done(((f32[1,768,768]{2,1,0:T(8,128)}), f32[1,48,768]{2,1,0:T(8,128)}) %reduce-scatter.49.cloned.1.call-update) | async-done | bytes 147472 | tf_op jit(solution)/shard_map/reduce_scatter | solution.py:402
  2260.4 66.2 %reduce-scatter.51.cloned.1.call-done = f32[1,48,768]{2,1,0:T(8,128)} async-done(((f32[1,768,768]{2,1,0:T(8,128)}), f32[1,48,768]{2,1,0:T(8,128)}) %reduce-scatter.51.cloned.1.call-update) | async-done | bytes 147472 | tf_op jit(solution)/shard_map/reduce_scatter | solution.py:403
  2326.6 66.8 %reduce-scatter.53.cloned.1.call-done = f32[1,48,768]{2,1,0:T(8,128)} async-done(((f32[1,768,768]{2,1,0:T(8,128)}), f32[1,48,768]{2,1,0:T(8,128)}) %reduce-scatter.53.cloned.1.call-update) | async-done | bytes 147472 | tf_op jit(solution)/shard_map/reduce_scatter | solution.py:404
  2393.5 115.1 %reduce-scatter.57.cloned.1.call-done = f32[1,48,3072]{2,1,0:T(8,128)} async-done(((f32[1,768,3072]{2,1,0:T(8,128)}), f32[1,48,3072]{2,1,0:T(8,128)}) %reduce-scatter.57.cloned.1.call-update) | async-done | bytes 589840 | tf_op jit(solution)/shard_map/reduce_scatter | solution.py:411
  2508.6 116.2 %reduce-scatter.59.cloned.1.call-done = f32[1,192,768]{2,1,0:T(8,128)} async-done(((f32[1,3072,768]{2,1,0:T(8,128)}), f32[1,192,768]{2,1,0:T(8,128)}) %reduce-scatter.59.cloned.1.call-update) | async-done | bytes 589840 | tf_op jit(solution)/shard_map/reduce_scatter | solution.py:413
  (1314 shorter events, 1216.5 us)
Async XLA Ops:
  7.2 76.5 %all-gather.28.cloned.1.call-start = ((), (), s32[]{:S(2)}) async-start(), calls=%async_computation.42 | async-start | bytes 1253376 | tf_op jit(solution)/shard_map/all_gather | solution.py:133
  7.9 83.4 %all-gather.26.cloned.1.call-start = ((), (), s32[]{:S(2)}) async-start(), calls=%async_computation.41 | async-start | bytes 1253376 | tf_op jit(solution)/shard_map/all_gather | solution.py:132
  8.7 122.3 %all-gather.24.cloned.1.call-start = ((), (), s32[]{:S(2)}) async-start(), calls=%async_computation.40 | async-start | bytes 1253376 | tf_op jit(solution)/shard_map/all_gather | solution.py:131
  9.4 216.2 %all-gather.30.cloned.1.call-start = ((), (), s32[]{:S(2)}) async-start(), calls=%async_computation.43 | async-start | bytes 1720320 | tf_op jit(solution)/shard_map/all_gather | solution.py:216
  159.7 95.9 %all-gather.32.cloned.1.call-start = ((), (), s32[]{:S(2)}) async-start(), calls=%async_computation.44 | async-start | bytes 1253376 | tf_op jit(solution)/shard_map/all_gather | solution.py:134
  160.3 126.8 %all-gather.34.cloned.1.call-start = ((), (), s32[]{:S(2)}) async-start(), calls=%async_computation.45 | async-start | bytes 5013504 | tf_op jit(solution)/shard_map/all_gather | solution.py:140
  160.9 180.5 %all-gather.36.cloned.1.call-start = ((), (), s32[]{:S(2)}) async-start(), calls=%async_computation.46 | async-start | bytes 5013504 | tf_op jit(solution)/shard_map/all_gather | solution.py:142
  249.0 165.4 %all-gather.38.cloned.1.call-start = ((), (), s32[]{:S(2)}) async-start(), calls=%async_computation.47 | async-start | bytes 1720320 | tf_op jit(solution)/shard_map/all_gather | solution.py:216
  768.0 68.6 %all-gather.46.cloned.1.call-start = ((), (), s32[]{:S(2)}) async-start(), calls=%async_computation.62 | async-start | bytes 1720320 | tf_op jit(solution)/shard_map/all_gather | solution.py:340
  894.5 73.5 %reduce-scatter.39.cloned.1.call-start = ((), (), s32[]{:S(2)}) async-start(), calls=%async_computation.51 | async-start | bytes 1720320 | tf_op jit(solution)/shard_map/reduce_scatter | solution.py:358
  936.2 66.1 %all-gather.48.cloned.1.call-start = ((), (), s32[]{:S(2)}) async-start(), calls=%async_computation.63 | async-start | bytes 1720320 | tf_op jit(solution)/shard_map/all_gather | solution.py:340
  1050.1 76.7 %reduce-scatter.41.cloned.1.call-start = ((), (), s32[]{:S(2)}) async-start(), calls=%async_computation.52 | async-start | bytes 1720320 | tf_op jit(solution)/shard_map/reduce_scatter | solution.py:358
  1095.2 65.7 %all-gather.50.cloned.1.call-start = ((), (), s32[]{:S(2)}) async-start(), calls=%async_computation.64 | async-start | bytes 1720320 | tf_op jit(solution)/shard_map/all_gather | solution.py:340
  1210.1 76.8 %reduce-scatter.43.cloned.1.call-start = ((), (), s32[]{:S(2)}) async-start(), calls=%async_computation.53 | async-start | bytes 1720320 | tf_op jit(solution)/shard_map/reduce_scatter | solution.py:358
  1255.3 65.8 %all-gather.52.cloned.1.call-start = ((), (), s32[]{:S(2)}) async-start(), calls=%async_computation.65 | async-start | bytes 1720320 | tf_op jit(solution)/shard_map/all_gather | solution.py:340
  1370.9 76.7 %reduce-scatter.45.cloned.1.call-start = ((), (), s32[]{:S(2)}) async-start(), calls=%async_computation.54 | async-start | bytes 1720320 | tf_op jit(solution)/shard_map/reduce_scatter | solution.py:358
  1528.3 75.3 %reduce-scatter.47.cloned.1.call-start = ((), (), s32[]{:S(2)}) async-start(), calls=%async_computation.55 | async-start | bytes 1720320 | tf_op jit(solution)/shard_map/reduce_scatter | solution.py:358
  1567.3 196.0 %reduce-scatter.65.cloned.1.call-start = ((), (), s32[]{:S(2)}) async-start(), calls=%async_computation.69 | async-start | bytes 417792
  1595.4 169.2 %reduce-scatter.67.cloned.1.call-start = ((), (), s32[]{:S(2)}) async-start(), calls=%async_computation.70 | async-start | bytes 417792
  1596.5 177.3 %reduce-scatter.69.cloned.1.call-start = ((), (), s32[]{:S(2)}) async-start(), calls=%async_computation.71 | async-start | bytes 417792
  1597.5 234.3 %reduce-scatter.73.cloned.1.call-start = ((), (), s32[]{:S(2)}) async-start(), calls=%async_computation.73 | async-start | bytes 417792
  1598.5 291.7 %reduce-scatter.75.cloned.1.call-start = ((), (), s32[]{:S(2)}) async-start(), calls=%async_computation.74 | async-start | bytes 417792
  1616.7 331.5 %reduce-scatter.77.cloned.1.call-start = ((), (), s32[]{:S(2)}) async-start(), calls=%async_computation.75 | async-start | bytes 417792
  1617.7 393.1 %reduce-scatter.71.cloned.1.call-start = ((), (), s32[]{:S(2)}) async-start(), calls=%async_computation.72 | async-start | bytes 1671168
  1619.5 449.4 %reduce-scatter.61.cloned.1.call-start = ((), (), s32[]{:S(2)}) async-start(), calls=%async_computation.67 | async-start | bytes 417792
  1630.9 496.4 %reduce-scatter.63.cloned.1.call-start = ((), (), s32[]{:S(2)}) async-start(), calls=%async_computation.68 | async-start | bytes 417792
  1633.9 559.8 %reduce-scatter.55.cloned.1.call-start = ((), (), s32[]{:S(2)}) async-start(), calls=%async_computation.59 | async-start | bytes 2506752 | tf_op jit(solution)/shard_map/reduce_scatter | solution.py:405
  1639.2 621.2 %reduce-scatter.49.cloned.1.call-start = ((), (), s32[]{:S(2)}) async-start(), calls=%async_computation.56 | async-start | bytes 2506752 | tf_op jit(solution)/shard_map/reduce_scatter | solution.py:402
  1665.0 661.6 %reduce-scatter.51.cloned.1.call-start = ((), (), s32[]{:S(2)}) async-start(), calls=%async_computation.57 | async-start | bytes 2506752 | tf_op jit(solution)/shard_map/reduce_scatter | solution.py:403
  1679.7 713.8 %reduce-scatter.53.cloned.1.call-start = ((), (), s32[]{:S(2)}) async-start(), calls=%async_computation.58 | async-start | bytes 2506752 | tf_op jit(solution)/shard_map/reduce_scatter | solution.py:404
  1686.1 822.5 %reduce-scatter.57.cloned.1.call-start = ((), (), s32[]{:S(2)}) async-start(), calls=%async_computation.60 | async-start | bytes 10027008 | tf_op jit(solution)/shard_map/reduce_scatter | solution.py:411
  1723.4 901.4 %reduce-scatter.59.cloned.1.call-start = ((), (), s32[]{:S(2)}) async-start(), calls=%async_computation.61 | async-start | bytes 10027008 | tf_op jit(solution)/shard_map/reduce_scatter | solution.py:413
  (319 other events, 4795.9 us)
Sparse Core Ops, SparseCore 0:
  10.3 41.1 all-gather.27
  53.8 37.4 all-gather.25
  93.6 37.2 all-gather.23
  159.8 33.3 all-gather.29
  195.4 37.2 all-gather.31
  234.8 52.2 all-gather.33
  289.4 51.9 all-gather.35
  381.1 33.3 all-gather.37
  500.6 32.8 all-gather.39
  626.9 32.8 all-gather.41
  768.1 32.8 all-gather.43
  802.4 32.7 all-gather.45
  936.3 31.6 reduce-scatter.38
  969.5 32.6 all-gather.47
  1128.2 32.6 all-gather.49
  1288.4 32.6 all-gather.51
  1448.9 32.6 all-gather.53
  1602.8 54.3 reduce-scatter.64
  1660.7 54.5 reduce-scatter.66
  1719.1 54.5 reduce-scatter.68
  1777.2 54.5 reduce-scatter.72
  1835.6 54.5 reduce-scatter.74
  1893.6 54.5 reduce-scatter.76
  1952.3 58.4 reduce-scatter.70
  2014.3 54.5 reduce-scatter.60
  2072.6 54.5 reduce-scatter.62
  2131.6 61.9 reduce-scatter.54
  2198.4 61.9 reduce-scatter.48
  2264.6 61.9 reduce-scatter.50
  2331.4 61.9 reduce-scatter.52
  2398.1 110.4 reduce-scatter.56
  2513.7 111.0 reduce-scatter.58
  (4 shorter events, 125.5 us)
where the time goes:
time: 2650 us; the launch traced here: 2630 us
  waiting for transfers between devices  1330 us (50%)
  matrix products  428 us (16%)
  local copies, waits for them, and re-layouts  362 us (14%)
  other arithmetic  253 us (10%)
  blocking collectives  147 us (6%)
  starting transfers between devices  89.7 us (3%)
    unnamed x45, waiting for transfers between devices  355 us
    unnamed x679, local copies, waits for them, and re-layouts  119 us
    reduce_scatter x1, waiting for transfers between devices, body(): lax.psum_scatter(totals[11][None], ('head', 'blk'), scatter_dimension=1,...  116 us
    reduce_scatter x1, waiting for transfers between devices, body(): lax.psum_scatter(totals[9][None], ('head', 'blk'), scatter_dimension=1, t...  115 us
    all_gather x5, waiting for transfers between devices, body(): lax.all_gather(kv_pairs, 'blk', axis=0, tiled=True)  109 us
    reduce_scatter x5, waiting for transfers between devices, body(): lax.psum_scatter(key_terms.astype(jnp.bfloat16), 'blk', scatter_dimension...  103 us
    all_gather x5, waiting for transfers between devices, body(): all_pairs = lax.all_gather(stored_pairs, 'blk', axis=0, tiled=True)  76.1 us
    reduce_scatter x1, waiting for transfers between devices, body(): lax.psum_scatter(totals[2][None], ('head', 'blk'), scatter_dimension=1, t...  66.8 us
  transfers between devices with their start and end apart: 62, of which 45 were waited for; matrix products, arithmetic and copies ran while one was open for 17% of the time, Pallas kernels for 0%

commit v1 on v0

v1 whole, which is shorter than its diff:
```python
import functools

import jax
import jax.numpy as jnp
from jax import lax
from jax.experimental import pallas as pl
from jax.experimental.pallas import tpu as pltpu
from jax.sharding import PartitionSpec as P

HEAD_DIM = 64
GROUP = ("head", "blk")
F32 = jnp.float32
BF16 = jnp.bfloat16
NT = (((1,), (1,)), ((), ()))
NN = (((1,), (0,)), ((), ()))
TN = (((0,), (0,)), ((), ()))
VMEM_LIMIT = 48 * 1024 * 1024


def dot(left, right, dims=NN):
    return lax.dot_general(left, right, dims, preferred_element_type=F32)


def head_lanes(value, head):
    lane = lax.broadcasted_iota(jnp.int32, value.shape, 1)
    return jnp.where(lane // HEAD_DIM == head, value, jnp.zeros_like(value))


def attention_forward_kernel(q_ref, kv_ref, qid_ref, mark_ref, out_ref, lse_ref, qm, acc, top, total):
    step = pl.program_id(0)
    heads = qm.shape[0]
    width = q_ref.shape[1]

    @pl.when(step == 0)
    def _():
        scaled = q_ref[...] * jnp.asarray(0.125, BF16)
        for head in range(heads):
            qm[head] = head_lanes(scaled, head)
        acc[...] = jnp.zeros_like(acc)
        top[...] = jnp.full_like(top, -1e30)
        total[...] = jnp.zeros_like(total)

    keys = kv_ref[:, :width]
    values = kv_ref[:, width:]
    allowed = mark_ref[...] == qid_ref[...]
    for head in range(heads):
        scores = jnp.where(allowed, dot(keys, qm[head], NT), -1e30)
        before = top[head : head + 1]
        after = jnp.maximum(before, jnp.max(scores, axis=0, keepdims=True))
        weights = jnp.exp(scores - after)
        fade = jnp.exp(before - after)
        top[head : head + 1] = after
        total[head : head + 1] = total[head : head + 1] * fade + jnp.sum(weights, axis=0, keepdims=True)
        rows = slice(head * HEAD_DIM, (head + 1) * HEAD_DIM)
        part = dot(values, weights.astype(BF16), TN)
        acc[rows] = acc[rows] * fade + part[rows]

    @pl.when(step == pl.num_programs(0) - 1)
    def _():
        scale = 1.0 / total[:heads]
        parts = [
            acc[head * HEAD_DIM : (head + 1) * HEAD_DIM] * scale[head : head + 1] for head in range(heads)
        ]
        out_ref[...] = jnp.concatenate(parts, axis=0).T
        lse_ref[...] = top[...] + jnp.log(jnp.maximum(total[...], 1e-30))


def attention_backward_kernel(
    q_ref, kv_ref, qid_ref, mark_ref, out_ref, lse_ref, do_ref, dq_ref, dkv_ref, qm, dom, acc, delta
):
    step = pl.program_id(0)
    heads = qm.shape[0]
    width = q_ref.shape[1]

    @pl.when(step == 0)
    def _():
        scaled = q_ref[...] * jnp.asarray(0.125, BF16)
        incoming = do_ref[...]
        for head in range(heads):
            qm[head] = head_lanes(scaled, head)
            dom[head] = head_lanes(incoming, head)
        product = incoming.astype(F32) * out_ref[...]
        row = lax.broadcasted_iota(jnp.int32, (8, width), 0)
        lane = lax.broadcasted_iota(jnp.int32, (8, width), 1)
        chooser = jnp.where(lane // HEAD_DIM == row, 1.0, 0.0).astype(F32)
        delta[...] = lax.dot_general(
            chooser, product, NT, preferred_element_type=F32, precision=lax.Precision.HIGHEST
        )
        acc[...] = jnp.zeros_like(acc)

    keys = kv_ref[:, :width]
    values = kv_ref[:, width:]
    allowed = mark_ref[...] == qid_ref[...]
    grad_keys = jnp.zeros(keys.shape, F32)
    grad_values = jnp.zeros(keys.shape, F32)
    for head in range(heads):
        scores = dot(keys, qm[head], NT)
        weights = jnp.where(allowed, jnp.exp(scores - lse_ref[head : head + 1]), 0.0)
        grad_weights = dot(values, dom[head], NT)
        grad_scores = (weights * (grad_weights - delta[head : head + 1])).astype(BF16)
        grad_values += dot(weights.astype(BF16), dom[head])
        grad_keys += dot(grad_scores, qm[head])
        rows = slice(head * HEAD_DIM, (head + 1) * HEAD_DIM)
        acc[rows] += dot(keys, grad_scores, TN)[rows]
    dkv_ref[:, :width] = grad_keys.astype(BF16)
    dkv_ref[:, width:] = grad_values.astype(BF16)

    @pl.when(step == pl.num_programs(0) - 1)
    def _():
        dq_ref[...] = (acc[...] * 0.125).T.astype(BF16)


def key_block(count):
    return 256 if count % 256 == 0 else count


def whole(shape):
    return pl.BlockSpec(shape, lambda step: (0,) * len(shape))


def attention_cost(rows, count, width, products):
    return pl.CostEstimate(
        flops=products * 2 * rows * count * width,
        bytes_accessed=rows * width * 12 + count * width * 8,
        transcendentals=rows * count * (width // HEAD_DIM),
    )


def attention_forward(queries, pairs, query_ids, marks):
    rows, width = queries.shape
    count = pairs.shape[0]
    heads = width // HEAD_DIM
    block = key_block(count)
    return pl.pallas_call(
        attention_forward_kernel,
        grid=(count // block,),
        in_specs=[
            whole((rows, width)),
            pl.BlockSpec((block, 2 * width), lambda step: (step, 0)),
            whole((1, rows)),
            pl.BlockSpec((block, 1), lambda step: (step, 0)),
        ],
        out_specs=[whole((rows, width)), whole((8, rows))],
        out_shape=[
            jax.ShapeDtypeStruct((rows, width), F32),
            jax.ShapeDtypeStruct((8, rows), F32),
        ],
        scratch_shapes=[
            pltpu.VMEM((heads, rows, width), BF16),
            pltpu.VMEM((width, rows), F32),
            pltpu.VMEM((8, rows), F32),
            pltpu.VMEM((8, rows), F32),
        ],
        compiler_params=pltpu.CompilerParams(vmem_limit_bytes=VMEM_LIMIT),
        cost_estimate=attention_cost(rows, count, width, 2),
        name="attention_forward",
    )(queries, pairs, query_ids, marks)


def attention_backward(queries, pairs, query_ids, marks, out, lse, grad_out):
    rows, width = queries.shape
    count = pairs.shape[0]
    heads = width // HEAD_DIM
    block = key_block(count)
    return pl.pallas_call(
        attention_backward_kernel,
        grid=(count // block,),
        in_specs=[
            whole((rows, width)),
            pl.BlockSpec((block, 2 * width), lambda step: (step, 0)),
            whole((1, rows)),
            pl.BlockSpec((block, 1), lambda step: (step, 0)),
            whole((rows, width)),
            whole((8, rows)),
            whole((rows, width)),
        ],
        out_specs=[
            whole((rows, width)),
            pl.BlockSpec((block, 2 * width), lambda step: (step, 0)),
        ],
        out_shape=[
            jax.ShapeDtypeStruct((rows, width), BF16),
            jax.ShapeDtypeStruct((count, 2 * width), BF16),
        ],
        scratch_shapes=[
            pltpu.VMEM((heads, rows, width), BF16),
            pltpu.VMEM((heads, rows, width), BF16),
            pltpu.VMEM((width, rows), F32),
            pltpu.VMEM((8, rows), F32),
        ],
        compiler_params=pltpu.CompilerParams(vmem_limit_bytes=VMEM_LIMIT),
        cost_estimate=attention_cost(rows, count, width, 5),
        name="attention_backward",
    )(queries, pairs, query_ids, marks, out, lse, grad_out)


def norm_forward(value, gain, shift):
    centre = value - jnp.mean(value, axis=-1, keepdims=True)
    inverse = lax.rsqrt(jnp.mean(centre * centre, axis=-1, keepdims=True) + 1e-05)
    unit = centre * inverse
    return unit * gain + shift, unit, inverse


def norm_backward(grad, unit, inverse, gain):
    scaled = grad * gain
    mean_one = jnp.mean(scaled, axis=-1, keepdims=True)
    mean_two = jnp.mean(scaled * unit, axis=-1, keepdims=True)
    return (
        inverse * (scaled - mean_one - unit * mean_two),
        jnp.sum(grad * unit, axis=0),
        jnp.sum(grad, axis=0),
    )


def body(
    tokens,
    cotangent,
    doc_ids,
    pad_mask,
    w_query,
    w_key,
    w_value,
    w_out,
    b_query,
    b_value,
    b_out,
    gain_attn,
    bias_attn,
    w_up,
    b_up,
    w_down,
    b_down,
    gain_ffn,
    bias_ffn,
):
    section = lax.axis_index("section")
    head_count = lax.axis_size("head")
    blk_count = lax.axis_size("blk")
    head_at = lax.axis_index("head")
    blk_at = lax.axis_index("blk")
    batches, rows, width = tokens.shape
    shard = width // (head_count * blk_count)
    hidden_width = w_up.shape[2]
    chunks = hidden_width // width
    half = blk_count // 2
    middles = blk_count // 4
    per_section = batches // 2
    members = 4
    part_width = width // members
    pair_width = 2 * part_width
    first_section = section == 0
    low_half = blk_at < half
    member = (head_at // 2) * 2 + blk_at % 2
    own_batch = section * per_section + blk_at // half
    other_batch = section * per_section + 1 - blk_at // half

    def across_section(value):
        return lax.ppermute(value, "section", [(0, 1), (1, 0)])

    def across_half(value):
        return lax.ppermute(value, "blk", [(at, (at + half) % blk_count) for at in range(blk_count)])

    def across_member(value, step):
        pairs = []
        for head in range(head_count):
            for blk in range(blk_count):
                there = (head ^ (step & 2)) * blk_count + (blk ^ (step & 1))
                pairs.append((head * blk_count + blk, there))
        return lax.ppermute(value, GROUP, pairs)

    def across_core(value):
        return lax.ppermute(value, "head", [(at, at ^ 1) for at in range(head_count)])

    def across_middle(value, step):
        pairs = []
        for at in range(blk_count):
            base, middle, low = at // half, (at % half) // 2, at % 2
            pairs.append((at, base * half + ((middle + step) % middles) * 2 + low))
        return lax.ppermute(value, "blk", pairs)

    def pick(value, at):
        return lax.dynamic_index_in_dim(value, at, 0, keepdims=False)

    def to_heads(groups):
        own = [pick(groups, member ^ step) for step in range(members)]
        return jnp.concatenate(
            [own[0]] + [across_member(own[step], step) for step in range(1, members)], axis=0
        )

    def to_tokens(value):
        parts = value.reshape(members, value.shape[0] // members, value.shape[1])
        back = jnp.stack(
            [parts[0]] + [across_member(parts[step], step) for step in range(1, members)], axis=0
        )
        return [pick(back, member ^ at) for at in range(members)]

    def all_keys(value):
        value = jnp.concatenate([value, across_core(value)], axis=0)
        return jnp.concatenate(
            [value] + [across_middle(value, step) for step in range(1, middles)], axis=0
        )

    def own_keys_sum(value):
        count = value.shape[0] // middles
        total = value[:count].astype(F32)
        for step in range(1, middles):
            back = across_middle(value[step * count : (step + 1) * count], middles - step)
            total = total + back.astype(F32)
        partner = across_core(total[count // 2 :].astype(BF16))
        return (total[: count // 2] + partner.astype(F32)).astype(BF16)

    def columns(value, size):
        return value.reshape(value.shape[0], members, size).transpose(1, 0, 2)

    def split_parts(value):
        return value[0].reshape(shard, members, part_width)

    pairs_local = jnp.concatenate([split_parts(w_key), split_parts(w_value)], axis=2)
    small_local = jnp.stack(
        [
            part.reshape(shard)
            for part in (b_query, b_value, b_out, gain_attn, bias_attn, b_down, gain_ffn, bias_ffn)
        ]
        + [b_up[0].reshape(chunks, shard)[at] for at in range(chunks)],
        axis=1,
    )
    small_count = small_local.shape[1]
    joint_width = 3 * width
    first_local = jnp.concatenate(
        [
            pairs_local.reshape(shard, 2 * width),
            w_query[0],
            jnp.pad(small_local, ((0, 0), (0, 128 - small_count))),
        ],
        axis=1,
    )
    up_local = (
        w_up[0]
        .reshape(shard, head_count * blk_count, chunks, shard)
        .transpose(0, 2, 1, 3)
        .reshape(shard, hidden_width)
    )
    down_local = jnp.concatenate(
        [w_down[0, at * shard : (at + 1) * shard] for at in range(chunks)], axis=1
    )
    rest_local = jnp.concatenate([w_out[0], up_local, down_local], axis=1)
    rest_other = across_section(rest_local)
    first_all = lax.all_gather(first_local, ("section",) + GROUP, axis=0, tiled=True)
    rest_all = [
        lax.all_gather(
            jnp.where(first_section, rest_local, rest_other), GROUP, axis=0, tiled=True
        ),
        lax.all_gather(
            jnp.where(first_section, rest_other, rest_local), GROUP, axis=0, tiled=True
        ),
    ]

    def both_blocks(value):
        return jnp.concatenate(
            [pick(value, own_batch), across_half(pick(value, other_batch))], axis=0
        )

    layer_in = both_blocks(tokens)
    grad_top = both_blocks(cotangent)
    marks_local = jnp.where(pad_mask == 1, doc_ids, -1)
    labels = both_blocks(jnp.stack([doc_ids, marks_local], axis=-1))
    labels = jnp.concatenate(
        [labels] + [across_member(labels, step) for step in range(1, members)], axis=0
    )
    query_ids = labels[:, 0].reshape(1, -1)
    key_marks = all_keys(labels)[:, 1].reshape(-1, 1)

    layers = []
    outputs = []
    for layer in range(2):
        joint = first_all[layer * width : (layer + 1) * width, :joint_width]
        small = first_all[layer * width : (layer + 1) * width, joint_width:].T.astype(F32)
        rest = rest_all[layer]
        out_weight = rest[:, :width]
        up_weight = rest[:, width : width + hidden_width]
        down_weight = [
            rest[:, width + hidden_width + at * width : width + hidden_width + (at + 1) * width]
            for at in range(chunks)
        ]
        q_shift, v_shift, out_shift, gain_one, shift_one, down_shift, gain_two, shift_two = [
            small[at] for at in range(8)
        ]
        up_shift = small[8 : 8 + chunks].reshape(hidden_width)
        pair_shift = jnp.concatenate(
            [jnp.zeros((members, part_width), F32), v_shift.reshape(members, part_width)], axis=1
        )
        joint_shift = jnp.concatenate([pair_shift.reshape(2 * width), q_shift])
        joint_rows = (dot(layer_in, joint) + joint_shift).astype(BF16)
        pairs = all_keys(to_heads(columns(joint_rows[:, : 2 * width], pair_width)))
        queries = to_heads(columns(joint_rows[:, 2 * width :], part_width))
        mixed, lse = attention_forward(queries, pairs, query_ids, key_marks)
        attended = jnp.concatenate(to_tokens(mixed.astype(BF16)), axis=1)
        first_sum = layer_in.astype(F32) + dot(attended, out_weight) + out_shift
        middle, unit_one, inverse_one = norm_forward(first_sum, gain_one, shift_one)
        middle_low = middle.astype(BF16)
        hidden = dot(middle_low, up_weight) + up_shift
        share = 0.5 * lax.erfc(hidden * (-(0.5**0.5)))
        slope = share + hidden * jnp.exp(hidden * hidden * -0.5) * 0.3989422804014327
        active = (hidden * share).astype(BF16)
        second = middle + down_shift
        for at in range(chunks):
            second = second + dot(active[:, at * width : (at + 1) * width], down_weight[at])
        result, unit_two, inverse_two = norm_forward(second, gain_two, shift_two)
        layers.append(
            (
                layer_in,
                joint,
                out_weight,
                up_weight,
                down_weight,
                gain_one,
                gain_two,
                pairs,
                queries,
                mixed,
                lse,
                attended,
                unit_one,
                inverse_one,
                middle_low,
                slope,
                active,
                unit_two,
                inverse_two,
            )
        )
        layer_in = result.astype(BF16)
        outputs.append(layer_in)

    def reduced(value):
        return lax.psum_scatter(value, GROUP, scatter_dimension=0, tiled=True)

    wide_sums = [None, None]
    last_sums = [None, None]
    grads = [None, None]
    for layer in (1, 0):
        (
            layer_in,
            joint,
            out_weight,
            up_weight,
            down_weight,
            gain_one,
            gain_two,
            pairs,
            queries,
            mixed,
            lse,
            attended,
            unit_one,
            inverse_one,
            middle_low,
            slope,
            active,
            unit_two,
            inverse_two,
        ) = layers[layer]
        grad_second, grad_gain_two, grad_shift_two = norm_backward(
            grad_top, unit_two, inverse_two, gain_two
        )
        grad_down_low = grad_second.astype(BF16)
        grad_active = jnp.concatenate(
            [dot(grad_down_low, down_weight[at], NT) for at in range(chunks)], axis=1
        )
        grad_hidden = (grad_active * slope).astype(BF16)
        grad_down = [
            dot(active[:, at * width : (at + 1) * width], grad_down_low, TN).astype(BF16)
            for at in range(chunks)
        ]
        grad_up = dot(middle_low, grad_hidden, TN).astype(BF16)
        wide_sums[layer] = reduced(jnp.concatenate([grad_up] + grad_down, axis=1))
        grad_middle = grad_second + dot(grad_hidden, up_weight, NT)
        grad_first, grad_gain_one, grad_shift_one = norm_backward(
            grad_middle, unit_one, inverse_one, gain_one
        )
        grad_branch = grad_first.astype(BF16)
        grad_out = dot(attended, grad_branch, TN).astype(BF16)
        grad_returned = dot(grad_branch, out_weight, NT).astype(BF16)
        grad_mixed = to_heads(columns(grad_returned, part_width))
        grad_queries, grad_pairs = attention_backward(
            queries, pairs, query_ids, key_marks, mixed, lse, grad_mixed
        )
        pair_parts = to_tokens(own_keys_sum(grad_pairs))
        query_parts = to_tokens(grad_queries)
        grad_joint = jnp.concatenate(pair_parts + query_parts, axis=1)
        grad_joint_weight = dot(layer_in, grad_joint, TN).astype(BF16)
        grad_input = grad_first + dot(grad_joint, joint, NT)
        joint_sum = jnp.sum(grad_joint.astype(F32), axis=0)
        small = jnp.stack(
            [
                joint_sum[2 * width :],
                joint_sum[: 2 * width].reshape(members, 2, part_width)[:, 1].reshape(width),
                jnp.sum(grad_branch.astype(F32), axis=0),
                grad_gain_one,
                grad_shift_one,
                jnp.sum(grad_down_low.astype(F32), axis=0),
                grad_gain_two,
                grad_shift_two,
            ],
            axis=0,
        )
        hidden_sum = jnp.sum(grad_hidden.astype(F32), axis=0).reshape(chunks, width)
        small = jnp.concatenate([small, hidden_sum], axis=0).astype(BF16)
        small = jnp.pad(small.T, ((0, 0), (0, 128 - small_count)))
        last_sums[layer] = reduced(
            jnp.concatenate([grad_joint_weight, grad_out, small], axis=1)
        )
        grads[layer] = grad_input
        grad_top = grad_input.astype(BF16).astype(F32)

    def settle(first, second):
        sent = jnp.where(first_section, second, first)
        kept = jnp.where(first_section, first, second)
        return kept.astype(F32) + across_section(sent).astype(F32)

    wide = settle(wide_sums[0], wide_sums[1])
    last = settle(last_sums[0], last_sums[1])
    grad_up = (
        wide[:, :hidden_width]
        .reshape(shard, chunks, head_count * blk_count, shard)
        .transpose(0, 2, 1, 3)
        .reshape(shard, hidden_width)
    )
    grad_down = jnp.concatenate(
        [
            wide[:, hidden_width + at * width : hidden_width + (at + 1) * width]
            for at in range(chunks)
        ],
        axis=0,
    )
    grad_pairs = last[:, : 2 * width].reshape(shard, members, 2, part_width)
    grad_key = grad_pairs[:, :, 0].reshape(shard, width)
    grad_value = grad_pairs[:, :, 1].reshape(shard, width)
    grad_query = last[:, 2 * width : 3 * width]
    grad_out = last[:, 3 * width : 4 * width]
    small = last[:, 4 * width :].T

    def placed_rows(first, second):
        def halves(value):
            got = across_half(value[rows:])
            own = value[:rows]
            return jnp.stack([jnp.where(low_half, own, got), jnp.where(low_half, got, own)], axis=0)

        first, second = halves(first), halves(second)
        got = across_section(jnp.where(first_section, second, first))
        kept = jnp.where(first_section, first, second)
        return jnp.where(
            first_section,
            jnp.concatenate([kept, got], axis=0),
            jnp.concatenate([got, kept], axis=0),
        )

    outputs_all = placed_rows(outputs[0], outputs[1])
    grad_inputs = placed_rows(grads[0], grads[1])
    return (
        outputs_all[None],
        grad_inputs[None],
        grad_query[None],
        grad_key[None],
        grad_value[None],
        grad_out[None],
        small[0][None],
        small[1][None],
        small[2][None],
        small[3][None],
        small[4][None],
        grad_up[None],
        small[8 : 8 + chunks].reshape(1, chunks * shard),
        grad_down[None],
        small[5][None],
        small[6][None],
        small[7][None],
    )


def solution(mesh):
    rows = P(None, GROUP, None)
    marks = P(None, GROUP)
    matrix = P("section", GROUP, None)
    vector = P("section", GROUP)
    result = P("section", None, GROUP, None)
    return jax.shard_map(
        body,
        mesh=mesh,
        in_specs=(rows, rows, marks, marks)
        + (matrix,) * 4
        + (vector,) * 5
        + (matrix, vector, matrix, vector, vector, vector),
        out_specs=(result, result)
        + (matrix,) * 4
        + (vector,) * 5
        + (matrix, vector, matrix, vector, vector, vector),
        check_vma=False,
    )
```

time: 2650 us -> 849 us (0.32)
  waiting for transfers between devices: 1330 us -> 467 us
  matrix products: 428 us -> 96.9 us
  local copies, waits for them, and re-layouts: 362 us -> 90 us
  other arithmetic: 253 us -> 34.9 us
  blocking collectives: 147 us -> 0 us
  Pallas kernels: 0 us -> 66.2 us
    reduce_scatter x11 -> x4, waiting for transfers between devices: 600 us -> 220 us  [reduced(): return lax.psum_scatter(value, GROUP, scatter_dimension=0, tiled=True)]
    unnamed x45 -> x7, waiting for transfers between devices: 355 us -> 0.78 us
    dot_general x95 -> x42, matrix products: 428 us -> 96.9 us  [dot(): return lax.dot_general(left, right, dims, preferred_element_type=F32)]
    all_gather x16 -> x3, waiting for transfers between devices: 305 us -> 43.4 us  [the longest x1 42.4 us: body(): lax.all_gather(first_local, ('section',) + GROUP, axis=0, tiled=True)]
    ppermute x8 -> x56, waiting for transfers between devices: 35.5 us -> 203 us  [the longest x39 106 us: across_member(): return lax.ppermute(value, GROUP, pairs)]
    all_to_all x40 -> x0, other arithmetic: 128 us -> none  [the longest x10 46.6 us: body(): lax.all_to_all(grad_joint.reshape(head_count, -1), 'head', split_axis=0,...]
    unnamed x679 -> x214, local copies, waits for them, and re-layouts: 119 us -> 31.2 us
    pallas_call x0 -> x4, Pallas kernels: none -> 66.2 us  [the longest x2 36.6 us: attention_backward(): pl.pallas_call(attention_backward_kernel, grid=(count // block,), in_spec...]
  transfers between devices with their start and end apart: 62 -> 63, of which waited for: 45 -> 43; matrix products, arithmetic and copies ran while one was open for 17% -> 20% of each run, Pallas kernels for 0% -> 6%
where the time goes in v1:
time: 849 us; the launch traced here: 839 us
  waiting for transfers between devices  467 us (55%)
  matrix products  96.9 us (11%)
  local copies, waits for them, and re-layouts  90 us (11%)
  starting transfers between devices  67.6 us (8%)
  Pallas kernels  66.2 us (8%)
  other arithmetic  34.9 us (4%)
  between operations  16.4 us (2%)
    reduce_scatter x4, waiting for transfers between devices, reduced(): return lax.psum_scatter(value, GROUP, scatter_dimension=0, tiled=True)  220 us
    ppermute x39, waiting for transfers between devices, across_member(): return lax.ppermute(value, GROUP, pairs)  106 us
    dot_general x42, matrix products, dot(): return lax.dot_general(left, right, dims, preferred_element_type=F32)  96.9 us
    ppermute x7, waiting for transfers between devices, across_half(): lax.ppermute(value, 'blk', [(at, (at + half) % blk_count) for at in range...  62.5 us
    ppermute x39, starting transfers between devices, across_member(): return lax.ppermute(value, GROUP, pairs)  49.3 us
    all_gather x1, waiting for transfers between devices, body(): lax.all_gather(first_local, ('section',) + GROUP, axis=0, tiled=True)  42.4 us
    pallas_call x2, Pallas kernels, attention_backward(): pl.pallas_call(attention_backward_kernel, grid=(count // block,), in_spec...  36.6 us
    ppermute x5, waiting for transfers between devices, across_section(): return lax.ppermute(value, 'section', [(0, 1), (1, 0)])  32.8 us
  transfers between devices with their start and end apart: 63, of which 43 were waited for; matrix products, arithmetic and copies ran while one was open for 20% of the time, Pallas kernels for 6%

profile of v1, /device:TPU:0, one launch (start us, length us, event | category | flops | bytes accessed | tf_op | source)
XLA Modules:
  0.0 839.1 jit_solution(9846414904871666064)
XLA Ops:
  19.5 16.6 %collective-permute-done.16 = bf16[48,6912]{1,0:T(8,128)(2,1)S(1)} collective-permute-done((bf16[48,6912]{1,0:T(8,128)(2,1)S(1)}, bf16[48,6912]{1,0:T(8,128)(2,1)S(1)}, u32[]{:S(2)}, u32[]{:S(2)}) %collective-permute-start.16) | collective-permute-done | bytes 663584 | tf_op jit(solution)/shard_map/ppermute | solution.py:258
  51.5 42.4 %all-gather.4.cloned.1.call-done = bf16[1536,2432]{1,0:T(8,128)(2,1)} async-done(((bf16[48,2432]{1,0:T(8,128)(2,1)}), bf16[1536,2432]{1,0:T(8,128)(2,1)}) %all-gather.4.cloned.1.call-update) | async-done | bytes 7471120 | tf_op jit(solution)/shard_map/all_gather | solution.py:348
  111.1 9.2 %collective-permute-done.4 = bf16[224,384]{1,0:T(8,128)(2,1)} collective-permute-done((bf16[224,384]{1,0:T(8,128)(2,1)}, bf16[224,384]{1,0:T(8,128)(2,1)}, u32[]{:S(2)}, u32[]{:S(2)}) %collective-permute-start.4) | collective-permute-done | bytes 172064 | tf_op jit(solution)/shard_map/ppermute | solution.py:269
  120.3 12.5 %collective-permute-done.6 = bf16[224,384]{1,0:T(8,128)(2,1)} collective-permute-done((bf16[224,384]{1,0:T(8,128)(2,1)}, bf16[224,384]{1,0:T(8,128)(2,1)}, u32[]{:S(2)}, u32[]{:S(2)}) %collective-permute-start.6) | collective-permute-done | bytes 172064 | tf_op jit(solution)/shard_map/ppermute | solution.py:269
  150.4 4.3 collective-permute-done.3
  159.1 14.9 %attention_forward.2 = (f32[896,192]{1,0:T(8,128)S(1)}, f32[8,896]{1,0:T(8,128)S(1)}) custom-call(bf16[896,192]{1,0:T(8,128)(2,1)S(1)} %pad_maximum_fusion.7.q_ref, bf16[1792,384]{1,0:T(8,128)(2,1)S(1)} %constant_dynamic-update-slice_fusion.kv_ref, s32[1,896]{1,0:T(1,128)S(1)} %slice_bitcast_fusion.9.qid_ref, s32[1792,1]{1,0:T(8,128)S(1)} %copy.222.mark_ref), custom_call_target="tpu_custom_call" | custom-call | flops 1233125376 | bytes 4816896 | tf_op jit(solution)/shard_map/attention_forward/pallas_call | solution.py:134
  180.9 9.3 %collective-permute-done.13 = bf16[224,192]{1,0:T(8,128)(2,1)S(1)} collective-permute-done((bf16[224,192]{1,0:T(8,128)(2,1)S(1)}, bf16[224,192]{1,0:T(8,128)(2,1)S(1)}, u32[]{:S(2)}, u32[]{:S(2)}) %collective-permute-start.13) | collective-permute-done | bytes 86048 | tf_op jit(solution)/shard_map/ppermute | solution.py:269
  190.1 6.0 collective-permute-done.15
  199.5 10.6 %multiply_convert_fusion.1 = (bf16[224,3072]{1,0:T(8,128)(2,1)S(1)}, f32[224,3072]{1,0:T(8,128)}, f32[224,3072]{1,0:T(8,128)}) fusion(f32[3072]{0:T(1024)S(1)} %copy-done.84, bf16[768,6912]{1,0:T(8,128)(2,1)} %all-gather.6.cloned.1.call-done, f32[224,768]{1,0:T(8,128)S(1)} %get-tuple-element.254, f32[768]{0:T(1024)S(1)} %copy-done.80, ...), kind=kOutput, calls=%fused_computation.54 | convolution fusion | flops 1102553088 | bytes 12308224 | tf_op jit(solution)/shard_map/dot_general | solution.py:21
  228.4 6.6 collective-permute-done.21
  235.1 4.5 collective-permute-done.23
  256.0 8.2 collective-permute-done.18
  264.2 7.2 collective-permute-done.20
  276.8 14.7 %attention_forward.3 = (f32[896,192]{1,0:T(8,128)S(1)}, f32[8,896]{1,0:T(8,128)S(1)}) custom-call(bf16[896,192]{1,0:T(8,128)(2,1)S(1)} %pad_maximum_fusion.9.q_ref, bf16[1792,384]{1,0:T(8,128)(2,1)S(1)} %constant_dynamic-update-slice_fusion.6.kv_ref, s32[1,896]{1,0:T(1,128)S(1)} %slice_bitcast_fusion.9.qid_ref, s32[1792,1]{1,0:T(8,128)S(1)} %copy.222.mark_ref), custom_call_target="tpu_custom_call" | custom-call | flops 1233125376 | bytes 4816896 | tf_op jit(solution)/shard_map/attention_forward/pallas_call | solution.py:134
  306.9 9.0 %multiply_convert_fusion = (bf16[224,3072]{1,0:T(8,128)(2,1)S(1)}, f32[224,3072]{1,0:T(8,128)S(1)}, f32[224,3072]{1,0:T(8,128)S(1)}) fusion(f32[3072]{0:T(1024)S(1)} %add.359, bf16[768,6912]{1,0:T(8,128)(2,1)} %all-gather.8.cloned.1.call-done, f32[224,768]{1,0:T(8,128)S(1)} %get-tuple-element.259, f32[768]{0:T(1024)S(1)} %copy-done.81, ...), kind=kOutput, calls=%fused_computation.41 | convolution fusion | flops 1102553088 | bytes 12308224 | tf_op jit(solution)/shard_map/dot_general | solution.py:21
  338.2 18.4 %attention_backward.2 = (bf16[896,192]{1,0:T(8,128)(2,1)S(1)}, bf16[1792,384]{1,0:T(8,128)(2,1)S(1)}) custom-call(bf16[896,192]{1,0:T(8,128)(2,1)S(1)} %copy-done.5, bf16[1792,384]{1,0:T(8,128)(2,1)S(1)} %copy-done.12, s32[1,896]{1,0:T(1,128)S(1)} %slice_bitcast_fusion.9.qid_ref, s32[1792,1]{1,0:T(8,128)S(1)} %copy.222.mark_ref, f32[896,192]{1,0:T(8,128)S(1)} %copy-done.1, ...), custom_call_target="tpu_custom_call" | custom-call | flops 3082813440 | bytes 4816896 | tf_op jit(solution)/shard_map/attention_backward/pallas_call | solution.py:165
  375.4 4.0 collective-permute-done.36
  385.7 4.6 fusion.157
  391.2 5.5 fusion.5
  406.3 5.1 multiply_reduce_fusion.2
  425.0 18.2 %attention_backward.3 = (bf16[896,192]{1,0:T(8,128)(2,1)S(1)}, bf16[1792,384]{1,0:T(8,128)(2,1)S(1)}) custom-call(bf16[896,192]{1,0:T(8,128)(2,1)S(1)} %copy-done.3, bf16[1792,384]{1,0:T(8,128)(2,1)S(1)} %copy-done.10, s32[1,896]{1,0:T(1,128)S(1)} %slice_bitcast_fusion.9.qid_ref, s32[1792,1]{1,0:T(8,128)S(1)} %copy.222.mark_ref, ...), custom_call_target="tpu_custom_call" | custom-call | flops 3082813440 | bytes 4816896 | tf_op jit(solution)/shard_map/attention_backward/pallas_call | solution.py:165
  460.6 6.9 collective-permute-done.47
  487.3 3.9 fusion.3
  501.8 11.2 %collective-permute-done.17 = bf16[112,768]{1,0:T(8,128)(2,1)S(1)} collective-permute-done((bf16[112,768]{1,0:T(8,128)(2,1)S(1)}, bf16[112,768]{1,0:T(8,128)(2,1)S(1)}, u32[]{:S(2)}, u32[]{:S(2)}) %collective-permute-start.17) | collective-permute-done | bytes 172064 | tf_op jit(solution)/shard_map/ppermute | solution.py:261
  513.0 11.7 %collective-permute-done.28 = bf16[112,768]{1,0:T(8,128)(2,1)S(1)} collective-permute-done((bf16[112,768]{1,0:T(8,128)(2,1)S(1)}, bf16[112,768]{1,0:T(8,128)(2,1)S(1)}, u32[]{:S(2)}, u32[]{:S(2)}) %collective-permute-start.28) | collective-permute-done | bytes 172064 | tf_op jit(solution)/shard_map/ppermute | solution.py:261
  532.6 27.3 %collective-permute-done.52 = f32[112,768]{1,0:T(8,128)S(1)} collective-permute-done((f32[112,768]{1,0:T(8,128)S(1)}, f32[112,768]{1,0:T(8,128)S(1)}, u32[]{:S(2)}, u32[]{:S(2)}) %collective-permute-start.52) | collective-permute-done | bytes 344096 | tf_op jit(solution)/shard_map/ppermute | solution.py:261
  559.9 10.9 %collective-permute-done.51 = f32[112,768]{1,0:T(8,128)S(1)} collective-permute-done((f32[112,768]{1,0:T(8,128)S(1)}, f32[112,768]{1,0:T(8,128)S(1)}, u32[]{:S(2)}, u32[]{:S(2)}) %collective-permute-start.51) | collective-permute-done | bytes 344096 | tf_op jit(solution)/shard_map/ppermute | solution.py:261
  571.8 7.3 reduce-scatter.5.cloned.1.call-done
  582.7 6.7 collective-permute-done.53
  596.2 96.8 %reduce-scatter.11.cloned.1.call-done = bf16[48,6144]{1,0:T(8,128)(2,1)} async-done(((bf16[768,6144]{1,0:T(8,128)(2,1)}), bf16[48,6144]{1,0:T(8,128)(2,1)}) %reduce-scatter.11.cloned.1.call-update) | async-done | bytes 589840 | tf_op jit(solution)/shard_map/reduce_scatter | solution.py:436
  693.1 115.8 %reduce-scatter.9.cloned.1.call-done = bf16[48,6144]{1,0:T(8,128)(2,1)} async-done(((bf16[768,6144]{1,0:T(8,128)(2,1)}), bf16[48,6144]{1,0:T(8,128)(2,1)}) %reduce-scatter.9.cloned.1.call-update) | async-done | bytes 589840 | tf_op jit(solution)/shard_map/reduce_scatter | solution.py:436
  817.9 7.2 collective-permute-done.55
  (563 shorter events, 285.3 us)
Async XLA Ops:
  7.2 86.7 %all-gather.4.cloned.1.call-start = ((), (), s32[]{:S(2)}) async-start(), calls=%async_computation.4 | async-start | bytes 7704576 | tf_op jit(solution)/shard_map/all_gather | solution.py:348
  12.9 184.4 %all-gather.6.cloned.1.call-start = ((), (), s32[]{:S(2)}) async-start(), calls=%async_computation.5 | async-start | bytes 11280384 | tf_op jit(solution)/shard_map/all_gather | solution.py:350
  16.4 19.6 %collective-permute-start.16 = (bf16[48,6912]{1,0:T(8,128)(2,1)S(1)}, bf16[48,6912]{1,0:T(8,128)(2,1)S(1)}, u32[]{:S(2)}, u32[]{:S(2)}) collective-permute-start(bf16[48,6912]{1,0:T(8,128)(2,1)S(1)} %bitcast_dynamic-update-slice_fusion), channel_id=1, source_target_pairs={{0,16},{16,0},{1,17},{17,1},{2,18},{18,2},{3,19},{19,3},{4,20},{20... | collective-permute-start | bytes 1990664 | tf_op jit(solution)/shard_map/ppermute | solution.py:258
  37.2 267.3 %all-gather.8.cloned.1.call-start = ((), (), s32[]{:S(2)}) async-start(), calls=%async_computation.6 | async-start | bytes 11280384 | tf_op jit(solution)/shard_map/all_gather | solution.py:353
  38.0 533.8 %reduce-scatter.7.cloned.1.call-start = ((), (), s32[]{:S(2)}) async-start(), calls=%async_computation.8 | async-start | bytes 5222400 | tf_op jit(solution)/shard_map/reduce_scatter | solution.py:436
  41.0 56.2 %collective-permute-start = (bf16[112,768]{1,0:T(8,128)(2,1)S(1)}, bf16[112,768]{1,0:T(8,128)(2,1)S(1)}, u32[]{:S(2)}, u32[]{:S(2)}) collective-permute-start(bf16[112,768]{1,0:T(8,128)(2,1)S(1)} %get-tuple-element.184), channel_id=1, source_target_pairs={{0,2},{1,3},{2,0},{3,1},{4,6},{5,7},{6,4},{7,5},{8,10},{9,11},{10,... | collective-permute-start | bytes 516104 | tf_op jit(solution)/shard_map/ppermute | solution.py:261
  104.3 16.0 %collective-permute-start.4 = (bf16[224,384]{1,0:T(8,128)(2,1)}, bf16[224,384]{1,0:T(8,128)(2,1)}, u32[]{:S(2)}, u32[]{:S(2)}) collective-permute-start(bf16[224,384]{1,0:T(8,128)(2,1)} %bitcast.233), channel_id=1, source_target_pairs={{0,1},{1,0},{2,3},{3,2},{4,5},{5,4},{6,7},{7,6},{8,9},{9,8},{10,11... | collective-permute-start | bytes 516104 | tf_op jit(solution)/shard_map/ppermute | solution.py:269
  106.5 13.8 %collective-permute-start.5 = (bf16[224,384]{1,0:T(8,128)(2,1)}, bf16[224,384]{1,0:T(8,128)(2,1)}, u32[]{:S(2)}, u32[]{:S(2)}) collective-permute-start(bf16[224,384]{1,0:T(8,128)(2,1)} %bitcast.232), channel_id=1, source_target_pairs={{0,8},{1,9},{2,10},{3,11},{4,12},{5,13},{6,14},{7,15},{8,0},{9,1},... | collective-permute-start | bytes 516104 | tf_op jit(solution)/shard_map/ppermute | solution.py:269
  108.6 24.2 %collective-permute-start.6 = (bf16[224,384]{1,0:T(8,128)(2,1)}, bf16[224,384]{1,0:T(8,128)(2,1)}, u32[]{:S(2)}, u32[]{:S(2)}) collective-permute-start(bf16[224,384]{1,0:T(8,128)(2,1)} %bitcast.231), channel_id=1, source_target_pairs={{0,9},{1,8},{2,11},{3,10},{4,13},{5,12},{6,15},{7,14},{8,1},{9,0},... | collective-permute-start | bytes 516104 | tf_op jit(solution)/shard_map/ppermute | solution.py:269
  134.8 23.1 %collective-permute-start.7 = (bf16[896,384]{1,0:T(8,128)(2,1)}, bf16[896,384]{1,0:T(8,128)(2,1)}, u32[]{:S(2)}, u32[]{:S(2)}) collective-permute-start(bf16[896,384]{1,0:T(8,128)(2,1)} %pad_maximum_fusion), channel_id=1, source_target_pairs={{0,4},{4,0},{8,12},{12,8},{1,5},{5,1},{9,13},{13,9},{2,6},{6,2},{1... | collective-permute-start | bytes 2064392 | tf_op jit(solution)/shard_map/ppermute | solution.py:272
  137.6 12.8 %collective-permute-start.1 = (bf16[224,192]{1,0:T(8,128)(2,1)}, bf16[224,192]{1,0:T(8,128)(2,1)S(1)}, u32[]{:S(2)}, u32[]{:S(2)}) collective-permute-start(bf16[224,192]{1,0:T(8,128)(2,1)} %bitcast.18), channel_id=1, source_target_pairs={{0,1},{1,0},{2,3},{3,2},{4,5},{5,4},{6,7},{7,6},{8,9},{9,8},{10,11... | collective-permute-start | bytes 258056 | tf_op jit(solution)/shard_map/ppermute | solution.py:269
  139.1 15.7 %collective-permute-start.3 = (bf16[224,192]{1,0:T(8,128)(2,1)}, bf16[224,192]{1,0:T(8,128)(2,1)S(1)}, u32[]{:S(2)}, u32[]{:S(2)}) collective-permute-start(bf16[224,192]{1,0:T(8,128)(2,1)} %bitcast.20), channel_id=1, source_target_pairs={{0,9},{1,8},{2,11},{3,10},{4,13},{5,12},{6,15},{7,14},{8,1},{9,0},... | collective-permute-start | bytes 258056 | tf_op jit(solution)/shard_map/ppermute | solution.py:269
  174.2 15.9 %collective-permute-start.13 = (bf16[224,192]{1,0:T(8,128)(2,1)S(1)}, bf16[224,192]{1,0:T(8,128)(2,1)S(1)}, u32[]{:S(2)}, u32[]{:S(2)}) collective-permute-start(bf16[224,192]{1,0:T(8,128)(2,1)S(1)} %get-tuple-element.222), channel_id=1, source_target_pairs={{0,1},{1,0},{2,3},{3,2},{4,5},{5,4},{6,7},{7,6},{8,9},{9,8},{10,11... | collective-permute-start | bytes 258056 | tf_op jit(solution)/shard_map/ppermute | solution.py:269
  177.3 12.9 %collective-permute-start.14 = (bf16[224,192]{1,0:T(8,128)(2,1)S(1)}, bf16[224,192]{1,0:T(8,128)(2,1)S(1)}, u32[]{:S(2)}, u32[]{:S(2)}) collective-permute-start(bf16[224,192]{1,0:T(8,128)(2,1)S(1)} %get-tuple-element.221), channel_id=1, source_target_pairs={{0,8},{1,9},{2,10},{3,11},{4,12},{5,13},{6,14},{7,15},{8,0},{9,1},... | collective-permute-start | bytes 258056 | tf_op jit(solution)/shard_map/ppermute | solution.py:269
  179.5 16.7 %collective-permute-start.15 = (bf16[224,192]{1,0:T(8,128)(2,1)S(1)}, bf16[224,192]{1,0:T(8,128)(2,1)S(1)}, u32[]{:S(2)}, u32[]{:S(2)}) collective-permute-start(bf16[224,192]{1,0:T(8,128)(2,1)S(1)} %get-tuple-element.220), channel_id=1, source_target_pairs={{0,9},{1,8},{2,11},{3,10},{4,13},{5,12},{6,15},{7,14},{8,1},{9,0},... | collective-permute-start | bytes 258056 | tf_op jit(solution)/shard_map/ppermute | solution.py:269
  240.5 35.1 %collective-permute-start.24 = (bf16[896,384]{1,0:T(8,128)(2,1)}, bf16[896,384]{1,0:T(8,128)(2,1)}, u32[]{:S(2)}, u32[]{:S(2)}) collective-permute-start(bf16[896,384]{1,0:T(8,128)(2,1)} %pad_maximum_fusion.1), channel_id=1, source_target_pairs={{0,4},{4,0},{8,12},{12,8},{1,5},{5,1},{9,13},{13,9},{2,6},{6,2},{1... | collective-permute-start | bytes 2064392 | tf_op jit(solution)/shard_map/ppermute | solution.py:272
  247.6 16.6 %collective-permute-start.18 = (bf16[224,192]{1,0:T(8,128)(2,1)}, bf16[224,192]{1,0:T(8,128)(2,1)}, u32[]{:S(2)}, u32[]{:S(2)}) collective-permute-start(bf16[224,192]{1,0:T(8,128)(2,1)} %bitcast.272), channel_id=1, source_target_pairs={{0,1},{1,0},{2,3},{3,2},{4,5},{5,4},{6,7},{7,6},{8,9},{9,8},{10,11... | collective-permute-start | bytes 258056 | tf_op jit(solution)/shard_map/ppermute | solution.py:269
  249.9 14.3 %collective-permute-start.19 = (bf16[224,192]{1,0:T(8,128)(2,1)}, bf16[224,192]{1,0:T(8,128)(2,1)}, u32[]{:S(2)}, u32[]{:S(2)}) collective-permute-start(bf16[224,192]{1,0:T(8,128)(2,1)} %bitcast.275), channel_id=1, source_target_pairs={{0,8},{1,9},{2,10},{3,11},{4,12},{5,13},{6,14},{7,15},{8,0},{9,1},... | collective-permute-start | bytes 258056 | tf_op jit(solution)/shard_map/ppermute | solution.py:269
  251.7 19.7 %collective-permute-start.20 = (bf16[224,192]{1,0:T(8,128)(2,1)}, bf16[224,192]{1,0:T(8,128)(2,1)}, u32[]{:S(2)}, u32[]{:S(2)}) collective-permute-start(bf16[224,192]{1,0:T(8,128)(2,1)} %bitcast.277), channel_id=1, source_target_pairs={{0,9},{1,8},{2,11},{3,10},{4,13},{5,12},{6,15},{7,14},{8,1},{9,0},... | collective-permute-start | bytes 258056 | tf_op jit(solution)/shard_map/ppermute | solution.py:269
  297.6 20.6 %collective-permute-start.30 = (f32[112,768]{1,0:T(8,128)}, f32[112,768]{1,0:T(8,128)S(1)}, u32[]{:S(2)}, u32[]{:S(2)}) collective-permute-start(f32[112,768]{1,0:T(8,128)} %get-tuple-element.142), channel_id=1, source_target_pairs={{0,2},{1,3},{2,0},{3,1},{4,6},{5,7},{6,4},{7,5},{8,10},{9,11},{10,... | collective-permute-start | bytes 1032200 | tf_op jit(solution)/shard_map/ppermute | solution.py:261
  396.7 182.4 %reduce-scatter.5.cloned.1.call-start = ((), (), s32[]{:S(2)}) async-start(), calls=%async_computation.7 | async-start | bytes 5222400 | tf_op jit(solution)/shard_map/reduce_scatter | solution.py:436
  454.4 13.1 %collective-permute-start.47 = (bf16[224,384]{1,0:T(8,128)(2,1)S(1)}, bf16[224,384]{1,0:T(8,128)(2,1)S(1)}, u32[]{:S(2)}, u32[]{:S(2)}) collective-permute-start(bf16[224,384]{1,0:T(8,128)(2,1)S(1)} %get-tuple-element.162), channel_id=1, source_target_pairs={{0,9},{1,8},{2,11},{3,10},{4,13},{5,12},{6,15},{7,14},{8,1},{9,0},... | collective-permute-start | bytes 516104 | tf_op jit(solution)/shard_map/ppermute | solution.py:269
  474.0 219.1 %reduce-scatter.11.cloned.1.call-start = ((), (), s32[]{:S(2)}) async-start(), calls=%async_computation.10 | async-start | bytes 10027008 | tf_op jit(solution)/shard_map/reduce_scatter | solution.py:436
  485.8 323.1 %reduce-scatter.9.cloned.1.call-start = ((), (), s32[]{:S(2)}) async-start(), calls=%async_computation.9 | async-start | bytes 10027008 | tf_op jit(solution)/shard_map/reduce_scatter | solution.py:436
  498.7 14.3 %collective-permute-start.17 = (bf16[112,768]{1,0:T(8,128)(2,1)S(1)}, bf16[112,768]{1,0:T(8,128)(2,1)S(1)}, u32[]{:S(2)}, u32[]{:S(2)}) collective-permute-start(bf16[112,768]{1,0:T(8,128)(2,1)S(1)} %slice.588), channel_id=1, source_target_pairs={{0,2},{1,3},{2,0},{3,1},{4,6},{5,7},{6,4},{7,5},{8,10},{9,11},{10,... | collective-permute-start | bytes 516104 | tf_op jit(solution)/shard_map/ppermute | solution.py:261
  499.6 25.2 %collective-permute-start.28 = (bf16[112,768]{1,0:T(8,128)(2,1)S(1)}, bf16[112,768]{1,0:T(8,128)(2,1)S(1)}, u32[]{:S(2)}, u32[]{:S(2)}) collective-permute-start(bf16[112,768]{1,0:T(8,128)(2,1)S(1)} %slice.617), channel_id=1, source_target_pairs={{0,2},{1,3},{2,0},{3,1},{4,6},{5,7},{6,4},{7,5},{8,10},{9,11},{10,... | collective-permute-start | bytes 516104 | tf_op jit(solution)/shard_map/ppermute | solution.py:261
  524.8 35.0 %collective-permute-start.52 = (f32[112,768]{1,0:T(8,128)S(1)}, f32[112,768]{1,0:T(8,128)S(1)}, u32[]{:S(2)}, u32[]{:S(2)}) collective-permute-start(f32[112,768]{1,0:T(8,128)S(1)} %slice.629), channel_id=1, source_target_pairs={{0,2},{1,3},{2,0},{3,1},{4,6},{5,7},{6,4},{7,5},{8,10},{9,11},{10,... | collective-permute-start | bytes 1032200 | tf_op jit(solution)/shard_map/ppermute | solution.py:261
  528.2 42.6 %collective-permute-start.51 = (f32[112,768]{1,0:T(8,128)S(1)}, f32[112,768]{1,0:T(8,128)S(1)}, u32[]{:S(2)}, u32[]{:S(2)}) collective-permute-start(f32[112,768]{1,0:T(8,128)S(1)} %slice.627), channel_id=1, source_target_pairs={{0,2},{1,3},{2,0},{3,1},{4,6},{5,7},{6,4},{7,5},{8,10},{9,11},{10,... | collective-permute-start | bytes 1032200 | tf_op jit(solution)/shard_map/ppermute | solution.py:261
  531.3 49.4 %collective-permute-start.29 = (bf16[2,112,768]{2,1,0:T(8,128)(2,1)S(1)}, bf16[2,112,768]{2,1,0:T(8,128)(2,1)}, u32[]{:S(2)}, u32[]{:S(2)}) collective-permute-start(bf16[2,112,768]{2,1,0:T(8,128)(2,1)S(1)} %get-tuple-element.174), channel_id=1, source_target_pairs={{0,16},{16,0},{1,17},{17,1},{2,18},{18,2},{3,19},{19,3},{4,20},{20... | collective-permute-start | bytes 1032200 | tf_op jit(solution)/shard_map/ppermute | solution.py:258
  570.9 18.4 %collective-permute-start.53 = (f32[2,112,768]{2,1,0:T(8,128)S(1)}, f32[2,112,768]{2,1,0:T(8,128)S(1)}, u32[]{:S(2)}, u32[]{:S(2)}) collective-permute-start(f32[2,112,768]{2,1,0:T(8,128)S(1)} %get-tuple-element.145), channel_id=1, source_target_pairs={{0,16},{16,0},{1,17},{17,1},{2,18},{18,2},{3,19},{19,3},{4,20},{20... | collective-permute-start | bytes 2064392 | tf_op jit(solution)/shard_map/ppermute | solution.py:258
  580.2 12.8 %collective-permute-start.54 = (bf16[48,3200]{1,0:T(8,128)(2,1)S(1)}, bf16[48,3200]{1,0:T(8,128)(2,1)S(1)}, u32[]{:S(2)}, u32[]{:S(2)}) collective-permute-start(bf16[48,3200]{1,0:T(8,128)(2,1)S(1)} %broadcast_select_fusion.4), channel_id=1, source_target_pairs={{0,16},{16,0},{1,17},{17,1},{2,18},{18,2},{3,19},{19,3},{4,20},{20... | collective-permute-start | bytes 921608 | tf_op jit(solution)/shard_map/ppermute | solution.py:258
  810.1 15.1 %collective-permute-start.55 = (bf16[48,6144]{1,0:T(8,128)(2,1)S(1)}, bf16[48,6144]{1,0:T(8,128)(2,1)S(1)}, u32[]{:S(2)}, u32[]{:S(2)}) collective-permute-start(bf16[48,6144]{1,0:T(8,128)(2,1)S(1)} %broadcast_select_fusion.2), channel_id=1, source_target_pairs={{0,16},{16,0},{1,17},{17,1},{2,18},{18,2},{3,19},{19,3},{4,20},{20... | collective-permute-start | bytes 1769480 | tf_op jit(solution)/shard_map/ppermute | solution.py:258
  (124 other events, 1170.6 us)
Sparse Core Ops, SparseCore 0:
  13.1 80.8 all-gather.3
  96.2 101.0 all-gather.5
  199.7 98.8 all-gather.7
  396.8 79.8 reduce-scatter.6
  481.0 98.0 reduce-scatter.4
  583.1 109.9 reduce-scatter.10
  697.7 111.1 reduce-scatter.8

commit v2 on v1

--- a/solution.py
+++ b/solution.py
@@ -278,6 +278,72 @@
             pairs.append((at, base * half + ((middle + step) % middles) * 2 + low))
         return lax.ppermute(value, "blk", pairs)
 
+    direct = head_count == 4 and blk_count == 4
+    core_at = head_at % 2
+    side_at = head_at // 2
+
+    def across_side(value):
+        return lax.ppermute(value, "head", [(at, at ^ 2) for at in range(head_count)])
+
+    def add(left, right):
+        return (left.astype(F32) + right.astype(F32)).astype(BF16)
+
+    def side_sum(value):
+        kept = lax.dynamic_index_in_dim(value, side_at, 1, keepdims=False)
+        sent = lax.dynamic_index_in_dim(value, 1 - side_at, 1, keepdims=False)
+        return add(kept, across_side(sent))
+
+    def line_sum(value, axis):
+        def entry(at):
+            return lax.dynamic_index_in_dim(value, jnp.clip(at, 0, blk_count - 1), axis, keepdims=False)
+
+        right = [(at, at + 1) for at in range(blk_count - 1)]
+        left = [(at + 1, at) for at in range(blk_count - 1)]
+        from_left = from_right = None
+        for step in range(1, blk_count):
+            to_right = entry(blk_at + blk_count - step)
+            to_left = entry(blk_at - blk_count + step)
+            if step > 1:
+                to_right = add(to_right, from_left)
+                to_left = add(to_left, from_right)
+            from_left = lax.ppermute(to_right, "blk", right)
+            from_right = lax.ppermute(to_left, "blk", left)
+        return entry(blk_at).astype(F32) + from_left.astype(F32) + from_right.astype(F32)
+
+    def chip_sum(kept, sent, side_first):
+        value = add(kept, across_core(sent))
+        if side_first:
+            return line_sum(side_sum(value), 1)
+        return side_sum(line_sum(value, 2).astype(BF16))
+
+    def halves(value, axis):
+        shape = value.shape
+        lead = shape[axis] // width
+        split = value.reshape(shape[:axis] + (lead, 2, 2, width // 4) + shape[axis + 1 :])
+        first = lax.index_in_dim(split, 0, axis + 2, keepdims=False)
+        second = lax.index_in_dim(split, 1, axis + 2, keepdims=False)
+        flat = shape[:axis] + (shape[axis] // 2,) + shape[axis + 1 :]
+        return (
+            jnp.where(core_at == 0, first, second).reshape(flat),
+            jnp.where(core_at == 0, second, first).reshape(flat),
+        )
+
+    def scattered(kept, sent, side_first):
+        shape = (-1, 2, blk_count, shard, kept.shape[-1])
+        return chip_sum(kept.reshape(shape), sent.reshape(shape), side_first)
+
+    def weight_grad(left, right):
+        if not direct:
+            return (dot(left, right, TN).astype(BF16),)
+        kept, sent = halves(left, 1)
+        return (dot(kept, right, TN).astype(BF16), dot(sent, right, TN).astype(BF16))
+
+    def reduced(parts, side_first):
+        if not direct:
+            value = parts[0].reshape(-1, width, parts[0].shape[-1])
+            return lax.psum_scatter(value, GROUP, scatter_dimension=1, tiled=True)
+        return scattered(parts[0], parts[1], side_first)
+
     def pick(value, at):
         return lax.dynamic_index_in_dim(value, at, 0, keepdims=False)
 
@@ -432,11 +498,7 @@
         layer_in = result.astype(BF16)
         outputs.append(layer_in)
 
-    def reduced(value):
-        return lax.psum_scatter(value, GROUP, scatter_dimension=0, tiled=True)
-
-    wide_sums = [None, None]
-    last_sums = [None, None]
+    sums = [None, None]
     grads = [None, None]
     for layer in (1, 0):
         (
@@ -468,18 +530,20 @@
             [dot(grad_down_low, down_weight[at], NT) for at in range(chunks)], axis=1
         )
         grad_hidden = (grad_active * slope).astype(BF16)
-        grad_down = [
-            dot(active[:, at * width : (at + 1) * width], grad_down_low, TN).astype(BF16)
-            for at in range(chunks)
-        ]
-        grad_up = dot(middle_low, grad_hidden, TN).astype(BF16)
-        wide_sums[layer] = reduced(jnp.concatenate([grad_up] + grad_down, axis=1))
+        up_parts = weight_grad(middle_low, grad_hidden)
+        down_parts = weight_grad(active, grad_down_low)
+        grad_hidden, up_parts, down_parts = lax.optimization_barrier(
+            (grad_hidden, up_parts, down_parts)
+        )
+        up_sum = reduced(up_parts, True)
+        down_sum = reduced(down_parts, False)
         grad_middle = grad_second + dot(grad_hidden, up_weight, NT)
         grad_first, grad_gain_one, grad_shift_one = norm_backward(
             grad_middle, unit_one, inverse_one, gain_one
         )
         grad_branch = grad_first.astype(BF16)
-        grad_out = dot(attended, grad_branch, TN).astype(BF16)
+        out_parts = weight_grad(attended, grad_branch)
+        out_sum = reduced(out_parts, False)
         grad_returned = dot(grad_branch, out_weight, NT).astype(BF16)
         grad_mixed = to_heads(columns(grad_returned, part_width))
         grad_queries, grad_pairs = attention_backward(
@@ -488,7 +552,7 @@
         pair_parts = to_tokens(own_keys_sum(grad_pairs))
         query_parts = to_tokens(grad_queries)
         grad_joint = jnp.concatenate(pair_parts + query_parts, axis=1)
-        grad_joint_weight = dot(layer_in, grad_joint, TN).astype(BF16)
+        joint_parts = weight_grad(layer_in, grad_joint)
         grad_input = grad_first + dot(grad_joint, joint, NT)
         joint_sum = jnp.sum(grad_joint.astype(F32), axis=0)
         small = jnp.stack(
@@ -507,38 +571,34 @@
         hidden_sum = jnp.sum(grad_hidden.astype(F32), axis=0).reshape(chunks, width)
         small = jnp.concatenate([small, hidden_sum], axis=0).astype(BF16)
         small = jnp.pad(small.T, ((0, 0), (0, 128 - small_count)))
-        last_sums[layer] = reduced(
-            jnp.concatenate([grad_joint_weight, grad_out, small], axis=1)
-        )
+        joint_sum = reduced(joint_parts, True)
+        small_sum = reduced(halves(small, 0) if direct else (small,), False)
+        sums[layer] = [up_sum, down_sum, out_sum, joint_sum, small_sum]
         grads[layer] = grad_input
         grad_top = grad_input.astype(BF16).astype(F32)
 
     def settle(first, second):
-        sent = jnp.where(first_section, second, first)
-        kept = jnp.where(first_section, first, second)
-        return kept.astype(F32) + across_section(sent).astype(F32)
-
-    wide = settle(wide_sums[0], wide_sums[1])
-    last = settle(last_sums[0], last_sums[1])
+        to_first = lax.ppermute(first.astype(BF16), "section", [(1, 0)])
+        to_second = lax.ppermute(second.astype(BF16), "section", [(0, 1)])
+        return jnp.where(
+            first_section,
+            first.astype(F32) + to_first.astype(F32),
+            second.astype(F32) + to_second.astype(F32),
+        )
+
+    wide, down, out, last, small = [settle(first, second) for first, second in zip(*sums)]
     grad_up = (
-        wide[:, :hidden_width]
-        .reshape(shard, chunks, head_count * blk_count, shard)
+        wide.reshape(shard, chunks, head_count * blk_count, shard)
         .transpose(0, 2, 1, 3)
         .reshape(shard, hidden_width)
     )
-    grad_down = jnp.concatenate(
-        [
-            wide[:, hidden_width + at * width : hidden_width + (at + 1) * width]
-            for at in range(chunks)
-        ],
-        axis=0,
-    )
-    grad_pairs = last[:, : 2 * width].reshape(shard, members, 2, part_width)
+    grad_down = down.reshape(chunks * shard, width)
+    grad_pairs = last[0, :, : 2 * width].reshape(shard, members, 2, part_width)
     grad_key = grad_pairs[:, :, 0].reshape(shard, width)
     grad_value = grad_pairs[:, :, 1].reshape(shard, width)
-    grad_query = last[:, 2 * width : 3 * width]
-    grad_out = last[:, 3 * width : 4 * width]
-    small = last[:, 4 * width :].T
+    grad_query = last[0, :, 2 * width :]
+    grad_out = out[0]
+    small = small[0].T
 
     def placed_rows(first, second):
         def halves(value):

time: 849 us -> 1010 us (1.19)
  starting transfers between devices: 67.6 us -> 274 us
  waiting for transfers between devices: 467 us -> 327 us
  local copies, waits for them, and re-layouts: 90 us -> 139 us
  other arithmetic: 34.9 us -> 72.4 us
    reduce_scatter x4 -> x0, waiting for transfers between devices: 220 us -> none  [reduced(): return lax.psum_scatter(value, GROUP, scatter_dimension=0, tiled=True)]
    ppermute x0 -> x80, starting transfers between devices: none -> 197 us  [the longest x30 127 us: line_sum(): from_left = lax.ppermute(to_right, 'blk', right)]
    ppermute x0 -> x80, waiting for transfers between devices: none -> 152 us  [the longest x30 73.8 us: line_sum(): from_right = lax.ppermute(to_left, 'blk', left)]
    ppermute x7, waiting for transfers between devices: 62.5 us -> 19.9 us  [across_half(): lax.ppermute(value, 'blk', [(at, (at + half) % blk_count) for at in range...]
    convert_element_type x0 -> x64, other arithmetic: none -> 28.9 us  [the longest x50 21.4 us: add(): return (left.astype(F32) + right.astype(F32)).astype(BF16)]
    all_gather x1, waiting for transfers between devices: 42.4 us -> 22.8 us  [body(): lax.all_gather(first_local, ('section',) + GROUP, axis=0, tiled=True)]
    another operation x22 -> x23, local copies, waits for them, and re-layouts: 15.6 us -> 29.8 us
    ppermute x39, waiting for transfers between devices: 106 us -> 93.2 us  [across_member(): return lax.ppermute(value, GROUP, pairs)]
  transfers between devices with their start and end apart: 63 -> 147, of which waited for: 43 -> 68; matrix products, arithmetic and copies ran while one was open for 20% -> 27% of each run, Pallas kernels for 6% -> 7%
where the time goes in v2:
time: 1010 us; the launch traced here: 1000 us
  waiting for transfers between devices  327 us (32%)
  starting transfers between devices  274 us (27%)
  local copies, waits for them, and re-layouts  139 us (14%)
  matrix products  103 us (10%)
  other arithmetic  72.4 us (7%)
  Pallas kernels  66 us (7%)
  between operations  17.6 us (2%)
    ppermute x30, starting transfers between devices, line_sum(): from_left = lax.ppermute(to_right, 'blk', right)  127 us
    dot_general x44, matrix products, dot(): return lax.dot_general(left, right, dims, preferred_element_type=F32)  103 us
    ppermute x39, waiting for transfers between devices, across_member(): return lax.ppermute(value, GROUP, pairs)  93.2 us
    ppermute x30, waiting for transfers between devices, line_sum(): from_right = lax.ppermute(to_left, 'blk', left)  73.8 us
    ppermute x39, starting transfers between devices, across_member(): return lax.ppermute(value, GROUP, pairs)  48 us
    ppermute x30, starting transfers between devices, line_sum(): from_right = lax.ppermute(to_left, 'blk', left)  39 us
    pallas_call x2, Pallas kernels, attention_backward(): pl.pallas_call(attention_backward_kernel, grid=(count // block,), in_spec...  36.5 us
    ppermute x30, waiting for transfers between devices, line_sum(): from_left = lax.ppermute(to_right, 'blk', right)  34.9 us
  transfers between devices with their start and end apart: 147, of which 68 were waited for; matrix products, arithmetic and copies ran while one was open for 27% of the time, Pallas kernels for 7%

profile of v2, /device:TPU:0, one launch (start us, length us, event | category | flops | bytes accessed | tf_op | source)
XLA Modules:
  0.0 1000.2 jit_solution(12005254446372744717)
XLA Ops:
  19.5 16.6 %collective-permute-done.16 = bf16[48,6912]{1,0:T(8,128)(2,1)S(1)} collective-permute-done((bf16[48,6912]{1,0:T(8,128)(2,1)S(1)}, bf16[48,6912]{1,0:T(8,128)(2,1)S(1)}, u32[]{:S(2)}, u32[]{:S(2)}) %collective-permute-start.16) | collective-permute-done | bytes 663584 | tf_op jit(solution)/shard_map/ppermute | solution.py:258
  45.8 19.9 %collective-permute-done.8 = s32[112,2]{0,1:T(2,128)S(1)} collective-permute-done((s32[112,2]{0,1:T(2,128)S(1)}, s32[112,2]{0,1:T(2,128)S(1)}, u32[]{:S(2)}, u32[]{:S(2)}) %collective-permute-start.8) | collective-permute-done | bytes 928 | tf_op jit(solution)/shard_map/ppermute | solution.py:261
  69.5 5.6 collective-permute-done.11
  79.7 22.8 %all-gather.4.cloned.1.call-done = bf16[1536,2432]{1,0:T(8,128)(2,1)} async-done(((bf16[48,2432]{1,0:T(8,128)(2,1)}), bf16[1536,2432]{1,0:T(8,128)(2,1)}) %all-gather.4.cloned.1.call-update) | async-done | bytes 7471120 | tf_op jit(solution)/shard_map/all_gather | solution.py:414
  114.6 12.3 %collective-permute-done.4 = bf16[224,384]{1,0:T(8,128)(2,1)S(1)} collective-permute-done((bf16[224,384]{1,0:T(8,128)(2,1)S(1)}, bf16[224,384]{1,0:T(8,128)(2,1)S(1)}, u32[]{:S(2)}, u32[]{:S(2)}) %collective-permute-start.4) | collective-permute-done | bytes 172064 | tf_op jit(solution)/shard_map/ppermute | solution.py:269
  126.9 11.1 %collective-permute-done.6 = bf16[224,384]{1,0:T(8,128)(2,1)S(1)} collective-permute-done((bf16[224,384]{1,0:T(8,128)(2,1)S(1)}, bf16[224,384]{1,0:T(8,128)(2,1)S(1)}, u32[]{:S(2)}, u32[]{:S(2)}) %collective-permute-start.6) | collective-permute-done | bytes 172064 | tf_op jit(solution)/shard_map/ppermute | solution.py:269
  153.0 7.8 collective-permute-done.1
  165.6 14.9 %attention_forward.2 = (f32[896,192]{1,0:T(8,128)S(1)}, f32[8,896]{1,0:T(8,128)S(1)}) custom-call(bf16[896,192]{1,0:T(8,128)(2,1)S(1)} %pad_maximum_fusion.7.q_ref, bf16[1792,384]{1,0:T(8,128)(2,1)S(1)} %copy-done.3, s32[1,896]{1,0:T(1,128)S(1)} %slice_bitcast_fusion.6.qid_ref, s32[1792,1]{1,0:T(8,128)S(1)} %copy.309.mark_ref), custom_call_target="tpu_custom_call" | custom-call | flops 1233125376 | bytes 4816896 | tf_op jit(solution)/shard_map/attention_forward/pallas_call | solution.py:134
  184.2 11.3 %collective-permute-done.15 = bf16[224,192]{1,0:T(8,128)(2,1)S(1)} collective-permute-done((bf16[224,192]{1,0:T(8,128)(2,1)S(1)}, bf16[224,192]{1,0:T(8,128)(2,1)S(1)}, u32[]{:S(2)}, u32[]{:S(2)}) %collective-permute-start.15) | collective-permute-done | bytes 86048 | tf_op jit(solution)/shard_map/ppermute | solution.py:269
  196.9 6.7 all-gather.6.cloned.1.call-done
  205.9 9.9 multiply_convert_fusion.1
  248.9 12.8 %collective-permute-done.21 = bf16[224,384]{1,0:T(8,128)(2,1)S(1)} collective-permute-done((bf16[224,384]{1,0:T(8,128)(2,1)S(1)}, bf16[224,384]{1,0:T(8,128)(2,1)S(1)}, u32[]{:S(2)}, u32[]{:S(2)}) %collective-permute-start.21) | collective-permute-done | bytes 172064 | tf_op jit(solution)/shard_map/ppermute | solution.py:269
  265.7 11.2 %collective-permute-done.23 = bf16[224,384]{1,0:T(8,128)(2,1)S(1)} collective-permute-done((bf16[224,384]{1,0:T(8,128)(2,1)S(1)}, bf16[224,384]{1,0:T(8,128)(2,1)S(1)}, u32[]{:S(2)}, u32[]{:S(2)}) %collective-permute-start.23) | collective-permute-done | bytes 172064 | tf_op jit(solution)/shard_map/ppermute | solution.py:269
  291.3 14.7 %attention_forward.3 = (f32[896,192]{1,0:T(8,128)S(1)}, f32[8,896]{1,0:T(8,128)S(1)}) custom-call(bf16[896,192]{1,0:T(8,128)(2,1)S(1)} %pad_maximum_fusion.9.q_ref, bf16[1792,384]{1,0:T(8,128)(2,1)S(1)} %copy-done.5, s32[1,896]{1,0:T(1,128)S(1)} %slice_bitcast_fusion.6.qid_ref, s32[1792,1]{1,0:T(8,128)S(1)} %copy.309.mark_ref), custom_call_target="tpu_custom_call" | custom-call | flops 1233125376 | bytes 4816896 | tf_op jit(solution)/shard_map/attention_forward/pallas_call | solution.py:134
  328.6 10.2 %multiply_convert_fusion = (bf16[224,3072]{1,0:T(8,128)(2,1)}, f32[224,3072]{1,0:T(8,128)}, f32[224,3072]{1,0:T(8,128)}) fusion(f32[3072]{0:T(1024)} %add.805, bf16[224,768]{1,0:T(8,128)(2,1)} %fusion.126, bf16[768,6912]{1,0:T(8,128)(2,1)} %all-gather.8.cloned.1.call-done), kind=kOutput, calls=%fused_computation.54 | convolution fusion | flops 1101692928 | bytes 11956224 | tf_op jit(solution)/shard_map/dot_general | solution.py:21
  405.8 18.2 %attention_backward.2 = (bf16[896,192]{1,0:T(8,128)(2,1)S(1)}, bf16[1792,384]{1,0:T(8,128)(2,1)S(1)}) custom-call(bf16[896,192]{1,0:T(8,128)(2,1)S(1)} %copy-done.1, bf16[1792,384]{1,0:T(8,128)(2,1)S(1)} %copy-done.6, s32[1,896]{1,0:T(1,128)S(1)} %slice_bitcast_fusion.6.qid_ref, s32[1792,1]{1,0:T(8,128)S(1)} %copy.309.mark_ref, ...), custom_call_target="tpu_custom_call" | custom-call | flops 3082813440 | bytes 4816896 | tf_op jit(solution)/shard_map/attention_backward/pallas_call | solution.py:165
  537.7 18.3 %attention_backward.3 = (bf16[896,192]{1,0:T(8,128)(2,1)S(1)}, bf16[1792,384]{1,0:T(8,128)(2,1)S(1)}) custom-call(bf16[896,192]{1,0:T(8,128)(2,1)S(1)} %pad_maximum_fusion.7.q_ref, bf16[1792,384]{1,0:T(8,128)(2,1)S(1)} %copy-done.4, s32[1,896]{1,0:T(1,128)S(1)} %slice_bitcast_fusion.6.qid_ref, s32[1792,1]{1,0:T(8,128)S(1)} %copy.309.mark_ref, ...), custom_call_target="tpu_custom_call" | custom-call | flops 3082813440 | bytes 4816896 | tf_op jit(solution)/shard_map/attention_backward/pallas_call | solution.py:165
  586.1 11.3 %collective-permute-done.87 = bf16[1,2,48,768]{3,2,1,0:T(8,128)(2,1)S(1)} collective-permute-done((bf16[1,2,48,768]{3,2,1,0:T(8,128)(2,1)S(1)}, bf16[1,2,48,768]{3,2,1,0:T(8,128)(2,1)S(1)}, u32[]{:S(2)}, u32[]{:S(2)}) %collective-permute-start.87) | collective-permute-done | bytes 147488 | tf_op jit(solution)/shard_map/ppermute | solution.py:310
  670.7 6.4 collective-permute-done.77
  686.6 5.6 collective-permute-start.51
  722.2 10.4 %collective-permute-done.53 = f32[2,112,768]{2,1,0:T(8,128)S(1)} collective-permute-done((f32[2,112,768]{2,1,0:T(8,128)S(1)}, f32[2,112,768]{2,1,0:T(8,128)S(1)}, u32[]{:S(2)}, u32[]{:S(2)}) %collective-permute-start.53) | collective-permute-done | bytes 688160 | tf_op jit(solution)/shard_map/ppermute | solution.py:258
  743.6 7.0 collective-permute-done.139
  763.2 17.2 %collective-permute-done.64 = bf16[1,4,48,2304]{3,2,1,0:T(8,128)(2,1)S(1)} collective-permute-done((bf16[1,4,48,2304]{3,2,1,0:T(8,128)(2,1)S(1)}, bf16[1,4,48,2304]{3,2,1,0:T(8,128)(2,1)S(1)}, u32[]{:S(2)}, u32[]{:S(2)}) %collective-permute-start.64) | collective-permute-done | bytes 884768 | tf_op jit(solution)/shard_map/ppermute | solution.py:286
  822.7 7.7 collective-permute-done.69
  831.8 7.2 collective-permute-done.123
  858.2 5.6 collective-permute-start.121
  879.9 5.2 collective-permute-start.56
  891.8 5.3 collective-permute-start.57
  904.7 5.7 collective-permute-done.142
  915.5 5.9 collective-permute-done.60
  939.0 7.2 collective-permute-done.114
  949.6 5.4 collective-permute-done.62
  (905 shorter events, 645.4 us)
Async XLA Ops:
  7.2 95.4 %all-gather.4.cloned.1.call-start = ((), (), s32[]{:S(2)}) async-start(), calls=%async_computation | async-start | bytes 7704576 | tf_op jit(solution)/shard_map/all_gather | solution.py:414
  12.9 190.7 %all-gather.6.cloned.1.call-start = ((), (), s32[]{:S(2)}) async-start(), calls=%async_computation.1 | async-start | bytes 11280384 | tf_op jit(solution)/shard_map/all_gather | solution.py:416
  37.2 285.7 %all-gather.8.cloned.1.call-start = ((), (), s32[]{:S(2)}) async-start(), calls=%async_computation.2 | async-start | bytes 11280384 | tf_op jit(solution)/shard_map/all_gather | solution.py:419
  39.1 37.8 %collective-permute-start = (bf16[112,768]{1,0:T(8,128)(2,1)S(1)}, bf16[112,768]{1,0:T(8,128)(2,1)}, u32[]{:S(2)}, u32[]{:S(2)}) collective-permute-start(bf16[112,768]{1,0:T(8,128)(2,1)S(1)} %get-tuple-element.226), channel_id=1, source_target_pairs={{0,2},{1,3},{2,0},{3,1},{4,6},{5,7},{6,4},{7,5},{8,10},{9,11},{10,... | collective-permute-start | bytes 516104 | tf_op jit(solution)/shard_map/ppermute | solution.py:261
  42.9 36.1 %collective-permute-start.30 = (f32[112,768]{1,0:T(8,128)S(1)}, f32[112,768]{1,0:T(8,128)S(1)}, u32[]{:S(2)}, u32[]{:S(2)}) collective-permute-start(f32[112,768]{1,0:T(8,128)S(1)} %get-tuple-element.172), channel_id=1, source_target_pairs={{0,2},{1,3},{2,0},{3,1},{4,6},{5,7},{6,4},{7,5},{8,10},{9,11},{10,... | collective-permute-start | bytes 1032200 | tf_op jit(solution)/shard_map/ppermute | solution.py:261
  235.7 42.3 %collective-permute-start.20 = (bf16[224,192]{1,0:T(8,128)(2,1)}, bf16[224,192]{1,0:T(8,128)(2,1)}, u32[]{:S(2)}, u32[]{:S(2)}) collective-permute-start(bf16[224,192]{1,0:T(8,128)(2,1)} %bitcast.51), channel_id=1, source_target_pairs={{0,9},{1,8},{2,11},{3,10},{4,13},{5,12},{6,15},{7,14},{8,1},{9,0},... | collective-permute-start | bytes 258056 | tf_op jit(solution)/shard_map/ppermute | solution.py:269
  237.3 40.7 %collective-permute-start.19 = (bf16[224,192]{1,0:T(8,128)(2,1)}, bf16[224,192]{1,0:T(8,128)(2,1)}, u32[]{:S(2)}, u32[]{:S(2)}) collective-permute-start(bf16[224,192]{1,0:T(8,128)(2,1)} %bitcast.50), channel_id=1, source_target_pairs={{0,8},{1,9},{2,10},{3,11},{4,12},{5,13},{6,14},{7,15},{8,0},{9,1},... | collective-permute-start | bytes 258056 | tf_op jit(solution)/shard_map/ppermute | solution.py:269
  244.9 32.0 %collective-permute-start.23 = (bf16[224,384]{1,0:T(8,128)(2,1)S(1)}, bf16[224,384]{1,0:T(8,128)(2,1)S(1)}, u32[]{:S(2)}, u32[]{:S(2)}) collective-permute-start(bf16[224,384]{1,0:T(8,128)(2,1)S(1)} %bitcast.669), channel_id=1, source_target_pairs={{0,9},{1,8},{2,11},{3,10},{4,13},{5,12},{6,15},{7,14},{8,1},{9,0},... | collective-permute-start | bytes 516104 | tf_op jit(solution)/shard_map/ppermute | solution.py:269
  261.7 48.3 %collective-permute-start.17 = (bf16[112,768]{1,0:T(8,128)(2,1)}, bf16[112,768]{1,0:T(8,128)(2,1)}, u32[]{:S(2)}, u32[]{:S(2)}) collective-permute-start(bf16[112,768]{1,0:T(8,128)(2,1)} %slice.632), channel_id=1, source_target_pairs={{0,2},{1,3},{2,0},{3,1},{4,6},{5,7},{6,4},{7,5},{8,10},{9,11},{10,... | collective-permute-start | bytes 516104 | tf_op jit(solution)/shard_map/ppermute | solution.py:261
  351.2 74.7 %collective-permute-start.28 = (bf16[112,768]{1,0:T(8,128)(2,1)}, bf16[112,768]{1,0:T(8,128)(2,1)}, u32[]{:S(2)}, u32[]{:S(2)}) collective-permute-start(bf16[112,768]{1,0:T(8,128)(2,1)} %slice.661), channel_id=1, source_target_pairs={{0,2},{1,3},{2,0},{3,1},{4,6},{5,7},{6,4},{7,5},{8,10},{9,11},{10,... | collective-permute-start | bytes 516104 | tf_op jit(solution)/shard_map/ppermute | solution.py:261
  392.9 42.2 %collective-permute-start.81 = (bf16[1,2,4,48,768]{4,3,1,2,0:T(8,128)(2,1)}, bf16[1,2,4,48,768]{4,3,1,2,0:T(8,128)(2,1)}, u32[]{:S(2)}, u32[]{:S(2)}) collective-permute-start(bf16[1,2,4,48,768]{4,3,1,2,0:T(8,128)(2,1)} %copy.278), channel_id=1, source_target_pairs={{0,4},{4,0},{8,12},{12,8},{1,5},{5,1},{9,13},{13,9},{2,6},{6,2},{1... | collective-permute-start | bytes 1769480 | tf_op jit(solution)/shard_map/ppermute | solution.py:272
  401.8 310.1 %collective-permute-start.117 = (bf16[1,2,4,48,3072]{4,3,2,1,0:T(8,128)(2,1)}, bf16[1,2,4,48,3072]{4,3,2,1,0:T(8,128)(2,1)}, u32[]{:S(2)}, u32[]{:S(2)}) collective-permute-start(bf16[1,2,4,48,3072]{4,3,2,1,0:T(8,128)(2,1)} %bitcast.598), channel_id=1, source_target_pairs={{0,4},{4,0},{8,12},{12,8},{1,5},{5,1},{9,13},{13,9},{2,6},{6,2},{1... | collective-permute-start | bytes 7077896 | tf_op jit(solution)/shard_map/ppermute | solution.py:272
  431.2 283.9 %collective-permute-start.135 = (bf16[4,2,4,48,768]{4,3,2,1,0:T(8,128)(2,1)}, bf16[4,2,4,48,768]{4,3,2,1,0:T(8,128)(2,1)}, u32[]{:S(2)}, u32[]{:S(2)}) collective-permute-start(bf16[4,2,4,48,768]{4,3,2,1,0:T(8,128)(2,1)} %bitcast.251), channel_id=1, source_target_pairs={{0,4},{4,0},{8,12},{12,8},{1,5},{5,1},{9,13},{13,9},{2,6},{6,2},{1... | collective-permute-start | bytes 7077896 | tf_op jit(solution)/shard_map/ppermute | solution.py:272
  501.4 28.8 %collective-permute-start.43 = (bf16[224,192]{1,0:T(8,128)(2,1)}, bf16[224,192]{1,0:T(8,128)(2,1)}, u32[]{:S(2)}, u32[]{:S(2)}) collective-permute-start(bf16[224,192]{1,0:T(8,128)(2,1)} %bitcast.695), channel_id=1, source_target_pairs={{0,9},{1,8},{2,11},{3,10},{4,13},{5,12},{6,15},{7,14},{8,1},{9,0},... | collective-permute-start | bytes 258056 | tf_op jit(solution)/shard_map/ppermute | solution.py:269
  530.2 35.5 %collective-permute-start.86 = (bf16[1,2,48,768]{3,2,1,0:T(8,128)(2,1)S(1)}, bf16[1,2,48,768]{3,2,1,0:T(8,128)(2,1)S(1)}, u32[]{:S(2)}, u32[]{:S(2)}) collective-permute-start(bf16[1,2,48,768]{3,2,1,0:T(8,128)(2,1)S(1)} %copy-done.91), channel_id=1, source_target_pairs={{1,0},{2,1},{3,2},{5,4},{6,5},{7,6},{9,8},{10,9},{11,10},{13,12},{... | collective-permute-start | bytes 442376 | tf_op jit(solution)/shard_map/ppermute | solution.py:310
  616.3 101.4 %collective-permute-start.63 = (bf16[1,2,4,48,2304]{4,3,2,1,0:T(8,128)(2,1)}, bf16[1,2,4,48,2304]{4,3,2,1,0:T(8,128)(2,1)}, u32[]{:S(2)}, u32[]{:S(2)}) collective-permute-start(bf16[1,2,4,48,2304]{4,3,2,1,0:T(8,128)(2,1)} %bitcast.149), channel_id=1, source_target_pairs={{0,4},{4,0},{8,12},{12,8},{1,5},{5,1},{9,13},{13,9},{2,6},{6,2},{1... | collective-permute-start | bytes 5308424 | tf_op jit(solution)/shard_map/ppermute | solution.py:272
  707.7 28.4 %collective-permute-start.108 = (bf16[1,2,4,48,3072]{4,3,2,1,0:T(8,128)(2,1)S(1)}, bf16[1,2,4,48,3072]{4,3,2,1,0:T(8,128)(2,1)S(1)}, u32[]{:S(2)}, u32[]{:S(2)}) collective-permute-start(bf16[1,2,4,48,3072]{4,3,2,1,0:T(8,128)(2,1)S(1)} %bitcast.599), channel_id=1, source_target_pairs={{0,4},{4,0},{8,12},{12,8},{1,5},{5,1},{9,13},{13,9},{2,6},{6,2},{1... | collective-permute-start | bytes 7077896 | tf_op jit(solution)/shard_map/ppermute | solution.py:272
  711.9 70.1 %collective-permute-start.54 = (bf16[1,2,4,48,2304]{4,3,2,1,0:T(8,128)(2,1)}, bf16[1,2,4,48,2304]{4,3,2,1,0:T(8,128)(2,1)S(1)}, u32[]{:S(2)}, u32[]{:S(2)}) collective-permute-start(bf16[1,2,4,48,2304]{4,3,2,1,0:T(8,128)(2,1)} %bitcast.613), channel_id=1, source_target_pairs={{0,4},{4,0},{8,12},{12,8},{1,5},{5,1},{9,13},{13,9},{2,6},{6,2},{1... | collective-permute-start | bytes 5308424 | tf_op jit(solution)/shard_map/ppermute | solution.py:272
  732.5 28.9 %collective-permute-start.118 = (bf16[1,4,48,3072]{3,2,1,0:T(8,128)(2,1)S(1)}, bf16[1,4,48,3072]{3,2,1,0:T(8,128)(2,1)S(1)}, u32[]{:S(2)}, u32[]{:S(2)}) collective-permute-start(bf16[1,4,48,3072]{3,2,1,0:T(8,128)(2,1)S(1)} %dynamic-slice_bitcast_fusion), channel_id=1, source_target_pairs={{0,8},{4,12},{8,0},{12,4},{1,9},{5,13},{9,1},{13,5},{2,10},{6,14},... | collective-permute-start | bytes 3538952 | tf_op jit(solution)/shard_map/ppermute | solution.py:286
  736.2 44.2 %collective-permute-start.64 = (bf16[1,4,48,2304]{3,2,1,0:T(8,128)(2,1)S(1)}, bf16[1,4,48,2304]{3,2,1,0:T(8,128)(2,1)S(1)}, u32[]{:S(2)}, u32[]{:S(2)}) collective-permute-start(bf16[1,4,48,2304]{3,2,1,0:T(8,128)(2,1)S(1)} %dynamic-slice_bitcast_fusion.2), channel_id=1, source_target_pairs={{0,8},{4,12},{8,0},{12,4},{1,9},{5,13},{9,1},{13,5},{2,10},{6,14},... | collective-permute-start | bytes 2654216 | tf_op jit(solution)/shard_map/ppermute | solution.py:286
  750.7 93.4 %collective-permute-start.109 = (bf16[1,4,48,3072]{3,2,1,0:T(8,128)(2,1)S(1)}, bf16[1,4,48,3072]{3,2,1,0:T(8,128)(2,1)S(1)}, u32[]{:S(2)}, u32[]{:S(2)}) collective-permute-start(bf16[1,4,48,3072]{3,2,1,0:T(8,128)(2,1)S(1)} %dynamic-slice_bitcast_fusion.1), channel_id=1, source_target_pairs={{0,8},{4,12},{8,0},{12,4},{1,9},{5,13},{9,1},{13,5},{2,10},{6,14},... | collective-permute-start | bytes 3538952 | tf_op jit(solution)/shard_map/ppermute | solution.py:286
  753.9 46.3 %collective-permute-start.127 = (bf16[4,2,48,768]{3,2,0,1:T(8,128)(2,1)S(1)}, bf16[4,2,48,768]{3,2,0,1:T(8,128)(2,1)S(1)}, u32[]{:S(2)}, u32[]{:S(2)}) collective-permute-start(bf16[4,2,48,768]{3,2,0,1:T(8,128)(2,1)S(1)} %get-tuple-element.161), channel_id=1, source_target_pairs={{0,1},{1,2},{2,3},{4,5},{5,6},{6,7},{8,9},{9,10},{10,11},{12,13},{... | collective-permute-start | bytes 1769480 | tf_op jit(solution)/shard_map/ppermute | solution.py:309
  761.4 87.6 %collective-permute-start.130 = (bf16[4,2,48,768]{3,2,0,1:T(8,128)(2,1)S(1)}, bf16[4,2,48,768]{3,2,0,1:T(8,128)(2,1)S(1)}, u32[]{:S(2)}, u32[]{:S(2)}) collective-permute-start(bf16[4,2,48,768]{3,2,0,1:T(8,128)(2,1)S(1)} %get-tuple-element.162), channel_id=1, source_target_pairs={{1,0},{2,1},{3,2},{5,4},{6,5},{7,6},{9,8},{10,9},{11,10},{13,12},{... | collective-permute-start | bytes 1769480 | tf_op jit(solution)/shard_map/ppermute | solution.py:310
  780.4 34.8 %collective-permute-start.140 = (bf16[4,2,48,768]{3,2,1,0:T(8,128)(2,1)S(1)}, bf16[4,2,48,768]{3,2,1,0:T(8,128)(2,1)S(1)}, u32[]{:S(2)}, u32[]{:S(2)}) collective-permute-start(bf16[4,2,48,768]{3,2,1,0:T(8,128)(2,1)S(1)} %get-tuple-element.164), channel_id=1, source_target_pairs={{1,0},{2,1},{3,2},{5,4},{6,5},{7,6},{9,8},{10,9},{11,10},{13,12},{... | collective-permute-start | bytes 1769480 | tf_op jit(solution)/shard_map/ppermute | solution.py:310
  815.2 57.2 %collective-permute-start.138 = (bf16[4,2,48,768]{3,2,1,0:T(8,128)(2,1)S(1)}, bf16[4,2,48,768]{3,2,1,0:T(8,128)(2,1)S(1)}, u32[]{:S(2)}, u32[]{:S(2)}) collective-permute-start(bf16[4,2,48,768]{3,2,1,0:T(8,128)(2,1)S(1)} %get-tuple-element.163), channel_id=1, source_target_pairs={{0,1},{1,2},{2,3},{4,5},{5,6},{6,7},{8,9},{9,10},{10,11},{12,13},{... | collective-permute-start | bytes 1769480 | tf_op jit(solution)/shard_map/ppermute | solution.py:309
  819.5 50.5 %collective-permute-start.55 = (bf16[1,4,48,2304]{3,2,1,0:T(8,128)(2,1)S(1)}, bf16[1,4,48,2304]{3,2,1,0:T(8,128)(2,1)S(1)}, u32[]{:S(2)}, u32[]{:S(2)}) collective-permute-start(bf16[1,4,48,2304]{3,2,1,0:T(8,128)(2,1)S(1)} %dynamic-slice_bitcast_fusion.3), channel_id=1, source_target_pairs={{0,8},{4,12},{8,0},{12,4},{1,9},{5,13},{9,1},{13,5},{2,10},{6,14},... | collective-permute-start | bytes 2654216 | tf_op jit(solution)/shard_map/ppermute | solution.py:286
  870.1 78.2 %collective-permute-start.71 = (bf16[1,48,2304]{2,1,0:T(8,128)(2,1)S(1)}, bf16[1,48,2304]{2,1,0:T(8,128)(2,1)S(1)}, u32[]{:S(2)}, u32[]{:S(2)}) collective-permute-start(bf16[1,48,2304]{2,1,0:T(8,128)(2,1)S(1)} %fusion.174), channel_id=1, source_target_pairs={{0,16},{1,17},{2,18},{3,19},{4,20},{5,21},{6,22},{7,23},{8,24},{9,... | collective-permute-start | bytes 663560 | tf_op jit(solution)/shard_map/ppermute | solution.py:582
  877.0 48.2 %collective-permute-start.113 = (bf16[1,48,3072]{2,1,0:T(8,128)(2,1)S(1)}, bf16[1,48,3072]{2,1,0:T(8,128)(2,1)S(1)}, u32[]{:S(2)}, u32[]{:S(2)}) collective-permute-start(bf16[1,48,3072]{2,1,0:T(8,128)(2,1)S(1)} %get-tuple-element.181), channel_id=1, source_target_pairs={{1,0},{2,1},{3,2},{5,4},{6,5},{7,6},{9,8},{10,9},{11,10},{13,12},{... | collective-permute-start | bytes 884744 | tf_op jit(solution)/shard_map/ppermute | solution.py:310
  878.6 34.7 %collective-permute-start.131 = (bf16[4,2,48,768]{3,2,0,1:T(8,128)(2,1)S(1)}, bf16[4,2,48,768]{3,2,0,1:T(8,128)(2,1)S(1)}, u32[]{:S(2)}, u32[]{:S(2)}) collective-permute-start(bf16[4,2,48,768]{3,2,0,1:T(8,128)(2,1)S(1)} %get-tuple-element.160), channel_id=1, source_target_pairs={{1,0},{2,1},{3,2},{5,4},{6,5},{7,6},{9,8},{10,9},{11,10},{13,12},{... | collective-permute-start | bytes 1769480 | tf_op jit(solution)/shard_map/ppermute | solution.py:310
  899.9 63.6 %collective-permute-start.129 = (bf16[4,2,48,768]{3,2,0,1:T(8,128)(2,1)}, bf16[4,2,48,768]{3,2,0,1:T(8,128)(2,1)}, u32[]{:S(2)}, u32[]{:S(2)}) collective-permute-start(bf16[4,2,48,768]{3,2,0,1:T(8,128)(2,1)} %get-tuple-element.159), channel_id=1, source_target_pairs={{0,1},{1,2},{2,3},{4,5},{5,6},{6,7},{8,9},{9,10},{10,11},{12,13},{... | collective-permute-start | bytes 1769480 | tf_op jit(solution)/shard_map/ppermute | solution.py:309
  910.3 72.9 %collective-permute-start.125 = (bf16[1,48,3072]{2,1,0:T(8,128)(2,1)}, bf16[1,48,3072]{2,1,0:T(8,128)(2,1)}, u32[]{:S(2)}, u32[]{:S(2)}) collective-permute-start(bf16[1,48,3072]{2,1,0:T(8,128)(2,1)} %fusion.152), channel_id=1, source_target_pairs={{0,16},{1,17},{2,18},{3,19},{4,20},{5,21},{6,22},{7,23},{8,24},{9,... | collective-permute-start | bytes 884744 | tf_op jit(solution)/shard_map/ppermute | solution.py:582
  934.3 55.5 %collective-permute-start.143 = (bf16[4,48,768]{2,1,0:T(8,128)(2,1)}, bf16[4,48,768]{2,1,0:T(8,128)(2,1)}, u32[]{:S(2)}, u32[]{:S(2)}) collective-permute-start(bf16[4,48,768]{2,1,0:T(8,128)(2,1)} %fusion.127), channel_id=1, source_target_pairs={{0,16},{1,17},{2,18},{3,19},{4,20},{5,21},{6,22},{7,23},{8,24},{9,... | collective-permute-start | bytes 884744 | tf_op jit(solution)/shard_map/ppermute | solution.py:582
  (239 other events, 2784.7 us)
Sparse Core Ops, SparseCore 0:
  13.0 89.4 all-gather.3
  104.9 98.6 all-gather.5
  205.9 97.1 all-gather.7

commit v3 on v1

--- a/solution.py
+++ b/solution.py
@@ -120,7 +120,7 @@
 
 def attention_cost(rows, count, width, products):
     return pl.CostEstimate(
-        flops=products * 2 * rows * count * width,
+        flops=16 * products * 2 * rows * count * width,
         bytes_accessed=rows * width * 12 + count * width * 8,
         transcendentals=rows * count * (width // HEAD_DIM),
     )
@@ -278,6 +278,48 @@
             pairs.append((at, base * half + ((middle + step) % middles) * 2 + low))
         return lax.ppermute(value, "blk", pairs)
 
+    direct = head_count == 4 and blk_count == 4
+    core_at = head_at % 2
+    side_at = head_at // 2
+
+    def across_side(value):
+        return lax.ppermute(value, "head", [(at, at ^ 2) for at in range(head_count)])
+
+    def add(*values):
+        return sum(value.astype(F32) for value in values).astype(BF16)
+
+    def tied(*values):
+        return lax.optimization_barrier(values)
+
+    def halves(value, axis):
+        shape = value.shape
+        lead = shape[axis] // width
+        split = value.reshape(shape[:axis] + (lead, 2, 2, width // 4) + shape[axis + 1 :])
+        first = lax.index_in_dim(split, 0, axis + 2, keepdims=False)
+        second = lax.index_in_dim(split, 1, axis + 2, keepdims=False)
+        flat = shape[:axis] + (shape[axis] // 2,) + shape[axis + 1 :]
+        return (
+            jnp.where(core_at == 0, first, second).reshape(flat),
+            jnp.where(core_at == 0, second, first).reshape(flat),
+        )
+
+    def weight_grad(left, right):
+        return [dot(part, right, TN).astype(BF16) for part in halves(left, 1)]
+
+    def chip_parts(parts):
+        return [parts[0], across_core(parts[1])]
+
+    def side_sum(parts):
+        views = [part.reshape(-1, 2, blk_count, shard, part.shape[1]) for part in parts]
+
+        def at(which):
+            return [lax.dynamic_index_in_dim(view, which, 1, keepdims=False) for view in views]
+
+        return add(*at(side_at), across_side(add(*at(1 - side_at))))
+
+    def line_sum(value):
+        return lax.psum_scatter(value, "blk", scatter_dimension=0, tiled=True)[0]
+
     def pick(value, at):
         return lax.dynamic_index_in_dim(value, at, 0, keepdims=False)
 
@@ -473,13 +515,16 @@
             for at in range(chunks)
         ]
         grad_up = dot(middle_low, grad_hidden, TN).astype(BF16)
-        wide_sums[layer] = reduced(jnp.concatenate([grad_up] + grad_down, axis=1))
+        parts = [grad_up] + grad_down + ([last] if layer == 0 else [])
+        grad_hidden, wide = tied(grad_hidden, jnp.concatenate(parts, axis=1))
+        if layer == 0:
+            wide, wide_sums[1] = tied(wide, wide_sums[1])
+        wide_sums[layer] = reduced(wide)
         grad_middle = grad_second + dot(grad_hidden, up_weight, NT)
         grad_first, grad_gain_one, grad_shift_one = norm_backward(
             grad_middle, unit_one, inverse_one, gain_one
         )
         grad_branch = grad_first.astype(BF16)
-        grad_out = dot(attended, grad_branch, TN).astype(BF16)
         grad_returned = dot(grad_branch, out_weight, NT).astype(BF16)
         grad_mixed = to_heads(columns(grad_returned, part_width))
         grad_queries, grad_pairs = attention_backward(
@@ -488,7 +533,6 @@
         pair_parts = to_tokens(own_keys_sum(grad_pairs))
         query_parts = to_tokens(grad_queries)
         grad_joint = jnp.concatenate(pair_parts + query_parts, axis=1)
-        grad_joint_weight = dot(layer_in, grad_joint, TN).astype(BF16)
         grad_input = grad_first + dot(grad_joint, joint, NT)
         joint_sum = jnp.sum(grad_joint.astype(F32), axis=0)
         small = jnp.stack(
@@ -507,17 +551,45 @@
         hidden_sum = jnp.sum(grad_hidden.astype(F32), axis=0).reshape(chunks, width)
         small = jnp.concatenate([small, hidden_sum], axis=0).astype(BF16)
         small = jnp.pad(small.T, ((0, 0), (0, 128 - small_count)))
-        last_sums[layer] = reduced(
-            jnp.concatenate([grad_joint_weight, grad_out, small], axis=1)
-        )
+        if direct and layer == 0:
+            last_side = side_sum(
+                chip_parts(
+                    [
+                        jnp.concatenate(group, axis=1)
+                        for group in zip(
+                            weight_grad(layer_in, grad_joint),
+                            weight_grad(attended, grad_branch),
+                            halves(small, 0),
+                        )
+                    ]
+                )
+            )[0]
+        else:
+            last = jnp.concatenate(
+                [
+                    dot(layer_in, grad_joint, TN).astype(BF16),
+                    dot(attended, grad_branch, TN).astype(BF16),
+                    small,
+                ],
+                axis=1,
+            )
         grads[layer] = grad_input
         grad_top = grad_input.astype(BF16).astype(F32)
 
     def settle(first, second):
-        sent = jnp.where(first_section, second, first)
-        kept = jnp.where(first_section, first, second)
-        return kept.astype(F32) + across_section(sent).astype(F32)
-
+        to_first = lax.ppermute(first, "section", [(1, 0)])
+        to_second = lax.ppermute(second, "section", [(0, 1)])
+        return jnp.where(first_section, first, second).astype(F32) + jnp.where(
+            first_section, to_first, to_second
+        ).astype(F32)
+
+    if direct:
+        last_side, wide_sums[0] = tied(last_side, wide_sums[0])
+        last_sums[0] = line_sum(last_side)
+    else:
+        last_sums[0] = reduced(last)
+    last_sums[1] = wide_sums[0][:, 2 * hidden_width :]
+    wide_sums[0] = wide_sums[0][:, : 2 * hidden_width]
     wide = settle(wide_sums[0], wide_sums[1])
     last = settle(last_sums[0], last_sums[1])
     grad_up = (

time: 849 us -> 742 us (0.87)
  waiting for transfers between devices: 467 us -> 343 us
  other arithmetic: 34.9 us -> 47 us
    reduce_scatter x4 -> x2, waiting for transfers between devices: 220 us -> 3.97 us  [reduced(): return lax.psum_scatter(value, GROUP, scatter_dimension=0, tiled=True)]
    ppermute x39, waiting for transfers between devices: 106 us -> 182 us  [across_member(): return lax.ppermute(value, GROUP, pairs)]
    unnamed x214 -> x246, local copies, waits for them, and re-layouts: 31.2 us -> 15.8 us
    ppermute x0 -> x5, waiting for transfers between devices: none -> 12.3 us  [the longest x2 7.2 us: settle(): to_first = lax.ppermute(first, 'section', [(1, 0)])]
    ppermute x0 -> x5, starting transfers between devices: none -> 10.6 us  [the longest x2 6.94 us: settle(): to_second = lax.ppermute(second, 'section', [(0, 1)])]
    dot_general x42 -> x44, matrix products: 96.9 us -> 101 us  [dot(): return lax.dot_general(left, right, dims, preferred_element_type=F32)]
    ppermute x5 -> x3, waiting for transfers between devices: 32.8 us -> 34.4 us  [across_section(): return lax.ppermute(value, 'section', [(0, 1), (1, 0)])]
  transfers between devices with their start and end apart: 63 -> 66, of which waited for: 43 -> 41; matrix products, arithmetic and copies ran while one was open for 20% -> 27% of each run, Pallas kernels for 6% -> 9%
where the time goes in v3:
time: 742 us; the launch traced here: 731 us
  waiting for transfers between devices  343 us (46%)
  matrix products  101 us (14%)
  local copies, waits for them, and re-layouts  88.6 us (12%)
  starting transfers between devices  69.2 us (9%)
  Pallas kernels  66.2 us (9%)
  other arithmetic  47 us (6%)
  between operations  16.6 us (2%)
    ppermute x39, waiting for transfers between devices, across_member(): return lax.ppermute(value, GROUP, pairs)  182 us
    dot_general x44, matrix products, dot(): return lax.dot_general(left, right, dims, preferred_element_type=F32)  101 us
    ppermute x7, waiting for transfers between devices, across_half(): lax.ppermute(value, 'blk', [(at, (at + half) % blk_count) for at in range...  62.3 us
    ppermute x39, starting transfers between devices, across_member(): return lax.ppermute(value, GROUP, pairs)  46 us
    all_gather x1, waiting for transfers between devices, body(): lax.all_gather(first_local, ('section',) + GROUP, axis=0, tiled=True)  42.4 us
    pallas_call x2, Pallas kernels, attention_backward(): pl.pallas_call(attention_backward_kernel, grid=(count // block,), in_spec...  36.7 us
    ppermute x3, waiting for transfers between devices, across_section(): return lax.ppermute(value, 'section', [(0, 1), (1, 0)])  34.4 us
    pallas_call x2, Pallas kernels, attention_forward(): pl.pallas_call(attention_forward_kernel, grid=(count // block,), in_specs...  29.5 us
  transfers between devices with their start and end apart: 66, of which 41 were waited for; matrix products, arithmetic and copies ran while one was open for 27% of the time, Pallas kernels for 9%

profile of v3, /device:TPU:0, one launch (start us, length us, event | category | flops | bytes accessed | tf_op | source)
XLA Modules:
  0.0 731.2 jit_solution(2607026859614423167)
XLA Ops:
  19.5 16.6 %collective-permute-done.16 = bf16[48,6912]{1,0:T(8,128)(2,1)S(1)} collective-permute-done((bf16[48,6912]{1,0:T(8,128)(2,1)S(1)}, bf16[48,6912]{1,0:T(8,128)(2,1)S(1)}, u32[]{:S(2)}, u32[]{:S(2)}) %collective-permute-start.16) | collective-permute-done | bytes 663584 | tf_op jit(solution)/shard_map/ppermute | solution.py:258
  51.5 42.4 %all-gather.4.cloned.1.call-done = bf16[1536,2432]{1,0:T(8,128)(2,1)} async-done(((bf16[48,2432]{1,0:T(8,128)(2,1)}), bf16[1536,2432]{1,0:T(8,128)(2,1)}) %all-gather.4.cloned.1.call-update) | async-done | bytes 7471120 | tf_op jit(solution)/shard_map/all_gather | solution.py:390
  108.2 12.5 %collective-permute-done.4 = bf16[224,384]{1,0:T(8,128)(2,1)S(1)} collective-permute-done((bf16[224,384]{1,0:T(8,128)(2,1)S(1)}, bf16[224,384]{1,0:T(8,128)(2,1)S(1)}, u32[]{:S(2)}, u32[]{:S(2)}) %collective-permute-start.4) | collective-permute-done | bytes 172064 | tf_op jit(solution)/shard_map/ppermute | solution.py:269
  120.7 12.4 %collective-permute-done.6 = bf16[224,384]{1,0:T(8,128)(2,1)S(1)} collective-permute-done((bf16[224,384]{1,0:T(8,128)(2,1)S(1)}, bf16[224,384]{1,0:T(8,128)(2,1)S(1)}, u32[]{:S(2)}, u32[]{:S(2)}) %collective-permute-start.6) | collective-permute-done | bytes 172064 | tf_op jit(solution)/shard_map/ppermute | solution.py:269
  147.4 10.9 %collective-permute-done.1 = bf16[224,192]{1,0:T(8,128)(2,1)} collective-permute-done((bf16[224,192]{1,0:T(8,128)(2,1)}, bf16[224,192]{1,0:T(8,128)(2,1)}, u32[]{:S(2)}, u32[]{:S(2)}) %collective-permute-start.1) | collective-permute-done | bytes 86048 | tf_op jit(solution)/shard_map/ppermute | solution.py:269
  158.2 6.7 collective-permute-done.3
  167.5 14.9 %attention_forward.2 = (f32[896,192]{1,0:T(8,128)S(1)}, f32[8,896]{1,0:T(8,128)S(1)}) custom-call(bf16[896,192]{1,0:T(8,128)(2,1)S(1)} %pad_maximum_fusion.9.q_ref, bf16[1792,384]{1,0:T(8,128)(2,1)S(1)} %constant_dynamic-update-slice_fusion.kv_ref, s32[1,896]{1,0:T(1,128)S(1)} %slice_bitcast_fusion.9.qid_ref, s32[1792,1]{1,0:T(8,128)S(1)} %copy.290.mark_ref), custom_call_target="tpu_custom_call" | custom-call | flops 19730006016 | bytes 4816896 | tf_op jit(solution)/shard_map/attention_forward/pallas_call | solution.py:134
  187.0 8.3 %collective-permute-done.15 = bf16[224,192]{1,0:T(8,128)(2,1)S(1)} collective-permute-done((bf16[224,192]{1,0:T(8,128)(2,1)S(1)}, bf16[224,192]{1,0:T(8,128)(2,1)S(1)}, u32[]{:S(2)}, u32[]{:S(2)}) %collective-permute-start.15) | collective-permute-done | bytes 86048 | tf_op jit(solution)/shard_map/ppermute | solution.py:269
  200.6 10.5 %multiply_convert_fusion.1 = (bf16[224,3072]{1,0:T(8,128)(2,1)S(1)}, f32[224,3072]{1,0:T(8,128)}, f32[224,3072]{1,0:T(8,128)}) fusion(f32[3072]{0:T(1024)S(1)} %copy-done.97, bf16[768,6912]{1,0:T(8,128)(2,1)} %all-gather.6.cloned.1.call-done, f32[224,768]{1,0:T(8,128)S(1)} %get-tuple-element.290, f32[768]{0:T(1024)S(1)} %copy-done.84, ...), kind=kOutput, calls=%fused_computation.51 | convolution fusion | flops 1102553088 | bytes 12308224 | tf_op jit(solution)/shard_map/dot_general | solution.py:21
  229.6 8.3 %collective-permute-done.21 = bf16[224,384]{1,0:T(8,128)(2,1)S(1)} collective-permute-done((bf16[224,384]{1,0:T(8,128)(2,1)S(1)}, bf16[224,384]{1,0:T(8,128)(2,1)S(1)}, u32[]{:S(2)}, u32[]{:S(2)}) %collective-permute-start.21) | collective-permute-done | bytes 172064 | tf_op jit(solution)/shard_map/ppermute | solution.py:269
  252.0 13.8 %collective-permute-done.18 = bf16[224,192]{1,0:T(8,128)(2,1)S(1)} collective-permute-done((bf16[224,192]{1,0:T(8,128)(2,1)}, bf16[224,192]{1,0:T(8,128)(2,1)S(1)}, u32[]{:S(2)}, u32[]{:S(2)}) %collective-permute-start.18) | collective-permute-done | bytes 86048 | tf_op jit(solution)/shard_map/ppermute | solution.py:269
  265.8 7.1 collective-permute-done.20
  274.4 14.6 %attention_forward.3 = (f32[896,192]{1,0:T(8,128)S(1)}, f32[8,896]{1,0:T(8,128)S(1)}) custom-call(bf16[896,192]{1,0:T(8,128)(2,1)S(1)} %pad_maximum_fusion.11.q_ref, bf16[1792,384]{1,0:T(8,128)(2,1)S(1)} %constant_dynamic-update-slice_fusion.6.kv_ref, s32[1,896]{1,0:T(1,128)S(1)} %slice_bitcast_fusion.9.qid_ref, s32[1792,1]{1,0:T(8,128)S(1)} %copy.290.mark_ref), custom_call_target="tpu_custom_call" | custom-call | flops 19730006016 | bytes 4816896 | tf_op jit(solution)/shard_map/attention_forward/pallas_call | solution.py:134
  295.5 9.1 %collective-permute-done.27 = bf16[224,192]{1,0:T(8,128)(2,1)S(1)} collective-permute-done((bf16[224,192]{1,0:T(8,128)(2,1)}, bf16[224,192]{1,0:T(8,128)(2,1)S(1)}, u32[]{:S(2)}, u32[]{:S(2)}) %collective-permute-start.27) | collective-permute-done | bytes 86048 | tf_op jit(solution)/shard_map/ppermute | solution.py:269
  312.8 9.0 %multiply_convert_fusion = (bf16[224,3072]{1,0:T(8,128)(2,1)S(1)}, f32[224,3072]{1,0:T(8,128)S(1)}, f32[224,3072]{1,0:T(8,128)S(1)}) fusion(f32[3072]{0:T(1024)} %add.399, bf16[768,6912]{1,0:T(8,128)(2,1)} %all-gather.8.cloned.1.call-done, f32[224,768]{1,0:T(8,128)S(1)} %get-tuple-element.295, f32[768]{0:T(1024)S(1)} %copy-done.86, ...), kind=kOutput, calls=%fused_computation.38 | convolution fusion | flops 1102553088 | bytes 12308224 | tf_op jit(solution)/shard_map/dot_general | solution.py:21
  361.4 18.4 %attention_backward.2 = (bf16[896,192]{1,0:T(8,128)(2,1)S(1)}, bf16[1792,384]{1,0:T(8,128)(2,1)S(1)}) custom-call(bf16[896,192]{1,0:T(8,128)(2,1)S(1)} %copy-done.5, bf16[1792,384]{1,0:T(8,128)(2,1)S(1)} %copy-done.13, s32[1,896]{1,0:T(1,128)S(1)} %slice_bitcast_fusion.9.qid_ref, s32[1792,1]{1,0:T(8,128)S(1)} %copy.290.mark_ref, ...), custom_call_target="tpu_custom_call" | custom-call | flops 49325015040 | bytes 4816896 | tf_op jit(solution)/shard_map/attention_backward/pallas_call | solution.py:165
  392.5 8.5 %collective-permute-done.40 = bf16[224,192]{1,0:T(8,128)(2,1)S(1)} collective-permute-done((bf16[224,192]{1,0:T(8,128)(2,1)S(1)}, bf16[224,192]{1,0:T(8,128)(2,1)S(1)}, u32[]{:S(2)}, u32[]{:S(2)}) %collective-permute-start.40) | collective-permute-done | bytes 86048 | tf_op jit(solution)/shard_map/ppermute | solution.py:269
  401.5 6.9 collective-permute-done.38
  409.3 8.3 %collective-permute-done.37 = bf16[224,384]{1,0:T(8,128)(2,1)S(1)} collective-permute-done((bf16[224,384]{1,0:T(8,128)(2,1)S(1)}, bf16[224,384]{1,0:T(8,128)(2,1)S(1)}, u32[]{:S(2)}, u32[]{:S(2)}) %collective-permute-start.37) | collective-permute-done | bytes 172064 | tf_op jit(solution)/shard_map/ppermute | solution.py:269
  426.1 4.9 fusion.152
  462.6 5.3 multiply_reduce_fusion
  486.1 18.4 %attention_backward.3 = (bf16[896,192]{1,0:T(8,128)(2,1)S(1)}, bf16[1792,384]{1,0:T(8,128)(2,1)S(1)}) custom-call(bf16[896,192]{1,0:T(8,128)(2,1)S(1)} %copy-done.3, bf16[1792,384]{1,0:T(8,128)(2,1)S(1)} %copy-done.11, s32[1,896]{1,0:T(1,128)S(1)} %slice_bitcast_fusion.9.qid_ref, s32[1792,1]{1,0:T(8,128)S(1)} %copy.290.mark_ref, f32[896,192]{1,0:T(8,128)S(1)} %copy-done.1, ...), custom_call_target="tpu_custom_call" | custom-call | flops 49325015040 | bytes 4816896 | tf_op jit(solution)/shard_map/attention_backward/pallas_call | solution.py:165
  524.8 13.7 %collective-permute-done.50 = bf16[224,192]{1,0:T(8,128)(2,1)S(1)} collective-permute-done((bf16[224,192]{1,0:T(8,128)(2,1)S(1)}, bf16[224,192]{1,0:T(8,128)(2,1)S(1)}, u32[]{:S(2)}, u32[]{:S(2)}) %collective-permute-start.50) | collective-permute-done | bytes 86048 | tf_op jit(solution)/shard_map/ppermute | solution.py:269
  538.5 7.5 %collective-permute-done.48 = bf16[224,192]{1,0:T(8,128)(2,1)S(1)} collective-permute-done((bf16[224,192]{1,0:T(8,128)(2,1)S(1)}, bf16[224,192]{1,0:T(8,128)(2,1)S(1)}, u32[]{:S(2)}, u32[]{:S(2)}) %collective-permute-start.48) | collective-permute-done | bytes 86048 | tf_op jit(solution)/shard_map/ppermute | solution.py:269
  546.2 11.0 %collective-permute-done.47 = bf16[224,384]{1,0:T(8,128)(2,1)S(1)} collective-permute-done((bf16[224,384]{1,0:T(8,128)(2,1)S(1)}, bf16[224,384]{1,0:T(8,128)(2,1)S(1)}, u32[]{:S(2)}, u32[]{:S(2)}) %collective-permute-start.47) | collective-permute-done | bytes 172064 | tf_op jit(solution)/shard_map/ppermute | solution.py:269
  557.2 10.0 %collective-permute-done.45 = bf16[224,384]{1,0:T(8,128)(2,1)S(1)} collective-permute-done((bf16[224,384]{1,0:T(8,128)(2,1)S(1)}, bf16[224,384]{1,0:T(8,128)(2,1)S(1)}, u32[]{:S(2)}, u32[]{:S(2)}) %collective-permute-start.45) | collective-permute-done | bytes 172064 | tf_op jit(solution)/shard_map/ppermute | solution.py:269
  590.1 17.1 %collective-permute-done.17 = bf16[112,768]{1,0:T(8,128)(2,1)S(1)} collective-permute-done((bf16[112,768]{1,0:T(8,128)(2,1)S(1)}, bf16[112,768]{1,0:T(8,128)(2,1)S(1)}, u32[]{:S(2)}, u32[]{:S(2)}) %collective-permute-start.17) | collective-permute-done | bytes 172064 | tf_op jit(solution)/shard_map/ppermute | solution.py:261
  608.7 24.6 %collective-permute-done.52 = f32[112,768]{1,0:T(8,128)S(1)} collective-permute-done((f32[112,768]{1,0:T(8,128)S(1)}, f32[112,768]{1,0:T(8,128)S(1)}, u32[]{:S(2)}, u32[]{:S(2)}) %collective-permute-start.52) | collective-permute-done | bytes 344096 | tf_op jit(solution)/shard_map/ppermute | solution.py:261
  634.2 19.1 %collective-permute-done.51 = f32[112,768]{1,0:T(8,128)S(1)} collective-permute-done((f32[112,768]{1,0:T(8,128)S(1)}, f32[112,768]{1,0:T(8,128)S(1)}, u32[]{:S(2)}, u32[]{:S(2)}) %collective-permute-start.51) | collective-permute-done | bytes 344096 | tf_op jit(solution)/shard_map/ppermute | solution.py:261
  667.1 17.8 %collective-permute-done.29 = bf16[2,112,768]{2,1,0:T(8,128)(2,1)S(1)} collective-permute-done((bf16[2,112,768]{2,1,0:T(8,128)(2,1)S(1)}, bf16[2,112,768]{2,1,0:T(8,128)(2,1)S(1)}, u32[]{:S(2)}, u32[]{:S(2)}) %collective-permute-start.29) | collective-permute-done | bytes 344096 | tf_op jit(solution)/shard_map/ppermute | solution.py:258
  691.3 5.1 collective-permute-done.59
  706.3 7.1 collective-permute-done.56
  (616 shorter events, 313.8 us)
Async XLA Ops:
  7.2 86.7 %all-gather.4.cloned.1.call-start = ((), (), s32[]{:S(2)}) async-start(), calls=%async_computation.3 | async-start | bytes 7704576 | tf_op jit(solution)/shard_map/all_gather | solution.py:390
  12.9 185.5 %all-gather.6.cloned.1.call-start = ((), (), s32[]{:S(2)}) async-start(), calls=%async_computation.4 | async-start | bytes 11280384 | tf_op jit(solution)/shard_map/all_gather | solution.py:392
  37.2 273.1 %all-gather.8.cloned.1.call-start = ((), (), s32[]{:S(2)}) async-start(), calls=%async_computation.5 | async-start | bytes 11280384 | tf_op jit(solution)/shard_map/all_gather | solution.py:395
  38.0 423.2 %reduce-scatter.4.cloned.1.call-start = ((), (), s32[]{:S(2)}) async-start(), calls=%async_computation.6 | async-start | bytes 10027008 | tf_op jit(solution)/shard_map/reduce_scatter | solution.py:478
  41.0 56.2 %collective-permute-start = (bf16[112,768]{1,0:T(8,128)(2,1)S(1)}, bf16[112,768]{1,0:T(8,128)(2,1)S(1)}, u32[]{:S(2)}, u32[]{:S(2)}) collective-permute-start(bf16[112,768]{1,0:T(8,128)(2,1)S(1)} %get-tuple-element.214), channel_id=1, source_target_pairs={{0,2},{1,3},{2,0},{3,1},{4,6},{5,7},{6,4},{7,5},{8,10},{9,11},{10,... | collective-permute-start | bytes 516104 | tf_op jit(solution)/shard_map/ppermute | solution.py:261
  107.6 25.5 %collective-permute-start.6 = (bf16[224,384]{1,0:T(8,128)(2,1)S(1)}, bf16[224,384]{1,0:T(8,128)(2,1)S(1)}, u32[]{:S(2)}, u32[]{:S(2)}) collective-permute-start(bf16[224,384]{1,0:T(8,128)(2,1)S(1)} %bitcast.302), channel_id=1, source_target_pairs={{0,9},{1,8},{2,11},{3,10},{4,13},{5,12},{6,15},{7,14},{8,1},{9,0},... | collective-permute-start | bytes 516104 | tf_op jit(solution)/shard_map/ppermute | solution.py:269
  134.0 32.2 %collective-permute-start.7 = (bf16[896,384]{1,0:T(8,128)(2,1)}, bf16[896,384]{1,0:T(8,128)(2,1)}, u32[]{:S(2)}, u32[]{:S(2)}) collective-permute-start(bf16[896,384]{1,0:T(8,128)(2,1)} %pad_maximum_fusion.2), channel_id=1, source_target_pairs={{0,4},{4,0},{8,12},{12,8},{1,5},{5,1},{9,13},{13,9},{2,6},{6,2},{1... | collective-permute-start | bytes 2064392 | tf_op jit(solution)/shard_map/ppermute | solution.py:272
  142.2 22.8 %collective-permute-start.3 = (bf16[224,192]{1,0:T(8,128)(2,1)}, bf16[224,192]{1,0:T(8,128)(2,1)}, u32[]{:S(2)}, u32[]{:S(2)}) collective-permute-start(bf16[224,192]{1,0:T(8,128)(2,1)} %bitcast.324), channel_id=1, source_target_pairs={{0,9},{1,8},{2,11},{3,10},{4,13},{5,12},{6,15},{7,14},{8,1},{9,0},... | collective-permute-start | bytes 258056 | tf_op jit(solution)/shard_map/ppermute | solution.py:269
  243.3 29.8 %collective-permute-start.24 = (bf16[896,384]{1,0:T(8,128)(2,1)}, bf16[896,384]{1,0:T(8,128)(2,1)}, u32[]{:S(2)}, u32[]{:S(2)}) collective-permute-start(bf16[896,384]{1,0:T(8,128)(2,1)} %pad_maximum_fusion.3), channel_id=1, source_target_pairs={{0,4},{4,0},{8,12},{12,8},{1,5},{5,1},{9,13},{13,9},{2,6},{6,2},{1... | collective-permute-start | bytes 2064392 | tf_op jit(solution)/shard_map/ppermute | solution.py:272
  249.1 23.8 %collective-permute-start.20 = (bf16[224,192]{1,0:T(8,128)(2,1)}, bf16[224,192]{1,0:T(8,128)(2,1)S(1)}, u32[]{:S(2)}, u32[]{:S(2)}) collective-permute-start(bf16[224,192]{1,0:T(8,128)(2,1)} %bitcast.328), channel_id=1, source_target_pairs={{0,9},{1,8},{2,11},{3,10},{4,13},{5,12},{6,15},{7,14},{8,1},{9,0},... | collective-permute-start | bytes 258056 | tf_op jit(solution)/shard_map/ppermute | solution.py:269
  294.1 30.0 %collective-permute-start.30 = (f32[112,768]{1,0:T(8,128)}, f32[112,768]{1,0:T(8,128)S(1)}, u32[]{:S(2)}, u32[]{:S(2)}) collective-permute-start(f32[112,768]{1,0:T(8,128)} %get-tuple-element.174), channel_id=1, source_target_pairs={{0,2},{1,3},{2,0},{3,1},{4,6},{5,7},{6,4},{7,5},{8,10},{9,11},{10,... | collective-permute-start | bytes 1032200 | tf_op jit(solution)/shard_map/ppermute | solution.py:261
  339.5 318.0 %reduce-scatter.6.cloned.1.call-start = ((), (), s32[]{:S(2)}) async-start(), calls=%async_computation.7 | async-start | bytes 15249408 | tf_op jit(solution)/shard_map/reduce_scatter | solution.py:478
  387.6 20.8 %collective-permute-start.38 = (bf16[224,192]{1,0:T(8,128)(2,1)S(1)}, bf16[224,192]{1,0:T(8,128)(2,1)S(1)}, u32[]{:S(2)}, u32[]{:S(2)}) collective-permute-start(bf16[224,192]{1,0:T(8,128)(2,1)S(1)} %get-tuple-element.236), channel_id=1, source_target_pairs={{0,1},{1,0},{2,3},{3,2},{4,5},{5,4},{6,7},{7,6},{8,9},{9,8},{10,11... | collective-permute-start | bytes 258056 | tf_op jit(solution)/shard_map/ppermute | solution.py:269
  389.2 28.4 %collective-permute-start.37 = (bf16[224,384]{1,0:T(8,128)(2,1)S(1)}, bf16[224,384]{1,0:T(8,128)(2,1)S(1)}, u32[]{:S(2)}, u32[]{:S(2)}) collective-permute-start(bf16[224,384]{1,0:T(8,128)(2,1)S(1)} %get-tuple-element.200), channel_id=1, source_target_pairs={{0,9},{1,8},{2,11},{3,10},{4,13},{5,12},{6,15},{7,14},{8,1},{9,0},... | collective-permute-start | bytes 516104 | tf_op jit(solution)/shard_map/ppermute | solution.py:269
  391.0 26.6 %collective-permute-start.36 = (bf16[224,384]{1,0:T(8,128)(2,1)S(1)}, bf16[224,384]{1,0:T(8,128)(2,1)S(1)}, u32[]{:S(2)}, u32[]{:S(2)}) collective-permute-start(bf16[224,384]{1,0:T(8,128)(2,1)S(1)} %get-tuple-element.201), channel_id=1, source_target_pairs={{0,8},{1,9},{2,10},{3,11},{4,12},{5,13},{6,14},{7,15},{8,0},{9,1},... | collective-permute-start | bytes 516104 | tf_op jit(solution)/shard_map/ppermute | solution.py:269
  401.0 21.3 %collective-permute-start.35 = (bf16[224,384]{1,0:T(8,128)(2,1)S(1)}, bf16[224,384]{1,0:T(8,128)(2,1)S(1)}, u32[]{:S(2)}, u32[]{:S(2)}) collective-permute-start(bf16[224,384]{1,0:T(8,128)(2,1)S(1)} %get-tuple-element.202), channel_id=1, source_target_pairs={{0,1},{1,0},{2,3},{3,2},{4,5},{5,4},{6,7},{7,6},{8,9},{9,8},{10,11... | collective-permute-start | bytes 516104 | tf_op jit(solution)/shard_map/ppermute | solution.py:269
  461.2 241.8 %reduce-scatter.8.cloned.1.call-start = ((), (), s32[]{:S(2)}) async-start(), calls=%async_computation.8 | async-start | bytes 1536000 | tf_op jit(solution)/shard_map/reduce_scatter | solution.py:321
  517.3 21.2 %collective-permute-start.50 = (bf16[224,192]{1,0:T(8,128)(2,1)S(1)}, bf16[224,192]{1,0:T(8,128)(2,1)S(1)}, u32[]{:S(2)}, u32[]{:S(2)}) collective-permute-start(bf16[224,192]{1,0:T(8,128)(2,1)S(1)} %get-tuple-element.226), channel_id=1, source_target_pairs={{0,9},{1,8},{2,11},{3,10},{4,13},{5,12},{6,15},{7,14},{8,1},{9,0},... | collective-permute-start | bytes 258056 | tf_op jit(solution)/shard_map/ppermute | solution.py:269
  518.6 19.9 %collective-permute-start.49 = (bf16[224,192]{1,0:T(8,128)(2,1)S(1)}, bf16[224,192]{1,0:T(8,128)(2,1)S(1)}, u32[]{:S(2)}, u32[]{:S(2)}) collective-permute-start(bf16[224,192]{1,0:T(8,128)(2,1)S(1)} %get-tuple-element.227), channel_id=1, source_target_pairs={{0,8},{1,9},{2,10},{3,11},{4,12},{5,13},{6,14},{7,15},{8,0},{9,1},... | collective-permute-start | bytes 258056 | tf_op jit(solution)/shard_map/ppermute | solution.py:269
  519.9 26.1 %collective-permute-start.48 = (bf16[224,192]{1,0:T(8,128)(2,1)S(1)}, bf16[224,192]{1,0:T(8,128)(2,1)S(1)}, u32[]{:S(2)}, u32[]{:S(2)}) collective-permute-start(bf16[224,192]{1,0:T(8,128)(2,1)S(1)} %get-tuple-element.228), channel_id=1, source_target_pairs={{0,1},{1,0},{2,3},{3,2},{4,5},{5,4},{6,7},{7,6},{8,9},{9,8},{10,11... | collective-permute-start | bytes 258056 | tf_op jit(solution)/shard_map/ppermute | solution.py:269
  522.2 35.0 %collective-permute-start.47 = (bf16[224,384]{1,0:T(8,128)(2,1)S(1)}, bf16[224,384]{1,0:T(8,128)(2,1)S(1)}, u32[]{:S(2)}, u32[]{:S(2)}) collective-permute-start(bf16[224,384]{1,0:T(8,128)(2,1)S(1)} %get-tuple-element.192), channel_id=1, source_target_pairs={{0,9},{1,8},{2,11},{3,10},{4,13},{5,12},{6,15},{7,14},{8,1},{9,0},... | collective-permute-start | bytes 516104 | tf_op jit(solution)/shard_map/ppermute | solution.py:269
  523.5 33.7 %collective-permute-start.46 = (bf16[224,384]{1,0:T(8,128)(2,1)S(1)}, bf16[224,384]{1,0:T(8,128)(2,1)S(1)}, u32[]{:S(2)}, u32[]{:S(2)}) collective-permute-start(bf16[224,384]{1,0:T(8,128)(2,1)S(1)} %get-tuple-element.193), channel_id=1, source_target_pairs={{0,8},{1,9},{2,10},{3,11},{4,12},{5,13},{6,14},{7,15},{8,0},{9,1},... | collective-permute-start | bytes 516104 | tf_op jit(solution)/shard_map/ppermute | solution.py:269
  538.5 28.7 %collective-permute-start.45 = (bf16[224,384]{1,0:T(8,128)(2,1)S(1)}, bf16[224,384]{1,0:T(8,128)(2,1)S(1)}, u32[]{:S(2)}, u32[]{:S(2)}) collective-permute-start(bf16[224,384]{1,0:T(8,128)(2,1)S(1)} %get-tuple-element.194), channel_id=1, source_target_pairs={{0,1},{1,0},{2,3},{3,2},{4,5},{5,4},{6,7},{7,6},{8,9},{9,8},{10,11... | collective-permute-start | bytes 516104 | tf_op jit(solution)/shard_map/ppermute | solution.py:269
  580.4 73.7 %collective-permute-start.55 = (bf16[1,4,48,3200]{3,2,1,0:T(8,128)(2,1)}, bf16[1,4,48,3200]{3,2,1,0:T(8,128)(2,1)}, u32[]{:S(2)}, u32[]{:S(2)}) collective-permute-start(bf16[1,4,48,3200]{3,2,1,0:T(8,128)(2,1)} %fusion.72), channel_id=1, source_target_pairs={{0,8},{4,12},{8,0},{12,4},{1,9},{5,13},{9,1},{13,5},{2,10},{6,14},... | collective-permute-start | bytes 3686408 | tf_op jit(solution)/shard_map/ppermute | solution.py:286
  582.4 24.8 %collective-permute-start.17 = (bf16[112,768]{1,0:T(8,128)(2,1)S(1)}, bf16[112,768]{1,0:T(8,128)(2,1)S(1)}, u32[]{:S(2)}, u32[]{:S(2)}) collective-permute-start(bf16[112,768]{1,0:T(8,128)(2,1)S(1)} %slice.620), channel_id=1, source_target_pairs={{0,2},{1,3},{2,0},{3,1},{4,6},{5,7},{6,4},{7,5},{8,10},{9,11},{10,... | collective-permute-start | bytes 516104 | tf_op jit(solution)/shard_map/ppermute | solution.py:261
  583.5 49.8 %collective-permute-start.52 = (f32[112,768]{1,0:T(8,128)S(1)}, f32[112,768]{1,0:T(8,128)S(1)}, u32[]{:S(2)}, u32[]{:S(2)}) collective-permute-start(f32[112,768]{1,0:T(8,128)S(1)} %slice.664), channel_id=1, source_target_pairs={{0,2},{1,3},{2,0},{3,1},{4,6},{5,7},{6,4},{7,5},{8,10},{9,11},{10,... | collective-permute-start | bytes 1032200 | tf_op jit(solution)/shard_map/ppermute | solution.py:261
  590.0 63.3 %collective-permute-start.51 = (f32[112,768]{1,0:T(8,128)S(1)}, f32[112,768]{1,0:T(8,128)S(1)}, u32[]{:S(2)}, u32[]{:S(2)}) collective-permute-start(f32[112,768]{1,0:T(8,128)S(1)} %slice.662), channel_id=1, source_target_pairs={{0,2},{1,3},{2,0},{3,1},{4,6},{5,7},{6,4},{7,5},{8,10},{9,11},{10,... | collective-permute-start | bytes 1032200 | tf_op jit(solution)/shard_map/ppermute | solution.py:261
  608.7 51.9 %collective-permute-start.28 = (bf16[112,768]{1,0:T(8,128)(2,1)}, bf16[112,768]{1,0:T(8,128)(2,1)}, u32[]{:S(2)}, u32[]{:S(2)}) collective-permute-start(bf16[112,768]{1,0:T(8,128)(2,1)} %slice.649), channel_id=1, source_target_pairs={{0,2},{1,3},{2,0},{3,1},{4,6},{5,7},{6,4},{7,5},{8,10},{9,11},{10,... | collective-permute-start | bytes 516104 | tf_op jit(solution)/shard_map/ppermute | solution.py:261
  659.1 26.7 %collective-permute-start.53 = (f32[2,112,768]{2,1,0:T(8,128)S(1)}, f32[2,112,768]{2,1,0:T(8,128)S(1)}, u32[]{:S(2)}, u32[]{:S(2)}) collective-permute-start(f32[2,112,768]{2,1,0:T(8,128)S(1)} %get-tuple-element.172), channel_id=1, source_target_pairs={{0,16},{16,0},{1,17},{17,1},{2,18},{18,2},{3,19},{19,3},{4,20},{20... | collective-permute-start | bytes 2064392 | tf_op jit(solution)/shard_map/ppermute | solution.py:258
  661.7 23.2 %collective-permute-start.29 = (bf16[2,112,768]{2,1,0:T(8,128)(2,1)S(1)}, bf16[2,112,768]{2,1,0:T(8,128)(2,1)S(1)}, u32[]{:S(2)}, u32[]{:S(2)}) collective-permute-start(bf16[2,112,768]{2,1,0:T(8,128)(2,1)S(1)} %get-tuple-element.204), channel_id=1, source_target_pairs={{0,16},{16,0},{1,17},{17,1},{2,18},{18,2},{3,19},{19,3},{4,20},{20... | collective-permute-start | bytes 1032200 | tf_op jit(solution)/shard_map/ppermute | solution.py:258
  662.3 34.1 %collective-permute-start.59 = (bf16[48,6144]{1,0:T(8,128)(2,1)S(1)}, bf16[48,6144]{1,0:T(8,128)(2,1)S(1)}, u32[]{:S(2)}, u32[]{:S(2)}) collective-permute-start(bf16[48,6144]{1,0:T(8,128)(2,1)S(1)} %copy-done.60), channel_id=1, source_target_pairs={{0,16},{1,17},{2,18},{3,19},{4,20},{5,21},{6,22},{7,23},{8,24},{9,... | collective-permute-start | bytes 1769480 | tf_op jit(solution)/shard_map/ppermute | solution.py:581
  665.8 30.8 %collective-permute-start.58 = (bf16[48,6144]{1,0:T(8,128)(2,1)S(1)}, bf16[48,6144]{1,0:T(8,128)(2,1)S(1)}, u32[]{:S(2)}, u32[]{:S(2)}) collective-permute-start(bf16[48,6144]{1,0:T(8,128)(2,1)S(1)} %slice.580), channel_id=1, source_target_pairs={{16,0},{17,1},{18,2},{19,3},{20,4},{21,5},{22,6},{23,7},{24,8},{25... | collective-permute-start | bytes 1769480 | tf_op jit(solution)/shard_map/ppermute | solution.py:580
  (142 other events, 1499.4 us)
Sparse Core Ops, SparseCore 0:
  13.1 80.8 all-gather.3
  96.8 101.4 all-gather.5
  200.6 107.1 all-gather.7
  339.6 121.4 reduce-scatter.3
  465.7 191.8 reduce-scatter.5
  659.7 29.1 reduce-scatter.7

commit v4 on v3

--- a/solution.py
+++ b/solution.py
@@ -357,7 +357,9 @@
     def split_parts(value):
         return value[0].reshape(shard, members, part_width)
 
-    pairs_local = jnp.concatenate([split_parts(w_key), split_parts(w_value)], axis=2)
+    joint_local = jnp.concatenate(
+        [split_parts(w_key), split_parts(w_value), split_parts(w_query)], axis=2
+    )
     small_local = jnp.stack(
         [
             part.reshape(shard)
@@ -370,8 +372,7 @@
     joint_width = 3 * width
     first_local = jnp.concatenate(
         [
-            pairs_local.reshape(shard, 2 * width),
-            w_query[0],
+            joint_local.reshape(shard, joint_width),
             jnp.pad(small_local, ((0, 0), (0, 128 - small_count))),
         ],
         axis=1,
@@ -428,13 +429,18 @@
             small[at] for at in range(8)
         ]
         up_shift = small[8 : 8 + chunks].reshape(hidden_width)
-        pair_shift = jnp.concatenate(
-            [jnp.zeros((members, part_width), F32), v_shift.reshape(members, part_width)], axis=1
-        )
-        joint_shift = jnp.concatenate([pair_shift.reshape(2 * width), q_shift])
-        joint_rows = (dot(layer_in, joint) + joint_shift).astype(BF16)
-        pairs = all_keys(to_heads(columns(joint_rows[:, : 2 * width], pair_width)))
-        queries = to_heads(columns(joint_rows[:, 2 * width :], part_width))
+        joint_shift = jnp.concatenate(
+            [
+                jnp.zeros((members, part_width), F32),
+                v_shift.reshape(members, part_width),
+                q_shift.reshape(members, part_width),
+            ],
+            axis=1,
+        )
+        joint_rows = (dot(layer_in, joint) + joint_shift.reshape(joint_width)).astype(BF16)
+        arrived = to_heads(columns(joint_rows, pair_width + part_width))
+        pairs = all_keys(arrived[:, :pair_width])
+        queries = arrived[:, pair_width:]
         mixed, lse = attention_forward(queries, pairs, query_ids, key_marks)
         attended = jnp.concatenate(to_tokens(mixed.astype(BF16)), axis=1)
         first_sum = layer_in.astype(F32) + dot(attended, out_weight) + out_shift
@@ -474,12 +480,29 @@
         layer_in = result.astype(BF16)
         outputs.append(layer_in)
 
+    moves = [[(1, 0)], [(0, 1)]]
+
+    def both_batches(value):
+        got = across_half(value[rows:].astype(BF16)).astype(value.dtype)
+        own = value[:rows]
+        return jnp.stack([jnp.where(low_half, own, got), jnp.where(low_half, got, own)], axis=0)
+
+    def placed(first, second):
+        first_got = lax.ppermute(first.astype(BF16), "section", moves[0]).astype(first.dtype)
+        second_got = lax.ppermute(second.astype(BF16), "section", moves[1]).astype(first.dtype)
+        return jnp.where(
+            first_section,
+            jnp.concatenate([first, first_got], axis=0),
+            jnp.concatenate([second_got, second], axis=0),
+        )
+
+    ready = [both_batches(value) for value in outputs]
+
     def reduced(value):
         return lax.psum_scatter(value, GROUP, scatter_dimension=0, tiled=True)
 
     wide_sums = [None, None]
     last_sums = [None, None]
-    grads = [None, None]
     for layer in (1, 0):
         (
             layer_in,
@@ -515,10 +538,12 @@
             for at in range(chunks)
         ]
         grad_up = dot(middle_low, grad_hidden, TN).astype(BF16)
-        parts = [grad_up] + grad_down + ([last] if layer == 0 else [])
-        grad_hidden, wide = tied(grad_hidden, jnp.concatenate(parts, axis=1))
+        parts = [grad_up] + grad_down
+        wide = jnp.concatenate(parts, axis=1)
         if layer == 0:
-            wide, wide_sums[1] = tied(wide, wide_sums[1])
+            grad_hidden, wide, wide_sums[1] = tied(grad_hidden, wide, wide_sums[1])
+        else:
+            grad_hidden, wide = tied(grad_hidden, wide)
         wide_sums[layer] = reduced(wide)
         grad_middle = grad_second + dot(grad_hidden, up_weight, NT)
         grad_first, grad_gain_one, grad_shift_one = norm_backward(
@@ -527,18 +552,22 @@
         grad_branch = grad_first.astype(BF16)
         grad_returned = dot(grad_branch, out_weight, NT).astype(BF16)
         grad_mixed = to_heads(columns(grad_returned, part_width))
+        if direct and layer == 0:
+            grad_mixed, *last_chip = tied(grad_mixed, *last_chip)
+            last_side = side_sum(last_chip)[0]
         grad_queries, grad_pairs = attention_backward(
             queries, pairs, query_ids, key_marks, mixed, lse, grad_mixed
         )
-        pair_parts = to_tokens(own_keys_sum(grad_pairs))
-        query_parts = to_tokens(grad_queries)
-        grad_joint = jnp.concatenate(pair_parts + query_parts, axis=1)
+        if direct and layer == 0:
+            grad_queries, grad_pairs, last_side = tied(grad_queries, grad_pairs, last_side)
+        grad_arrived = jnp.concatenate([own_keys_sum(grad_pairs), grad_queries], axis=1)
+        grad_joint = jnp.concatenate(to_tokens(grad_arrived), axis=1)
         grad_input = grad_first + dot(grad_joint, joint, NT)
-        joint_sum = jnp.sum(grad_joint.astype(F32), axis=0)
+        joint_sum = jnp.sum(grad_joint.astype(F32), axis=0).reshape(members, 3, part_width)
         small = jnp.stack(
             [
-                joint_sum[2 * width :],
-                joint_sum[: 2 * width].reshape(members, 2, part_width)[:, 1].reshape(width),
+                joint_sum[:, 2].reshape(width),
+                joint_sum[:, 1].reshape(width),
                 jnp.sum(grad_branch.astype(F32), axis=0),
                 grad_gain_one,
                 grad_shift_one,
@@ -551,29 +580,29 @@
         hidden_sum = jnp.sum(grad_hidden.astype(F32), axis=0).reshape(chunks, width)
         small = jnp.concatenate([small, hidden_sum], axis=0).astype(BF16)
         small = jnp.pad(small.T, ((0, 0), (0, 128 - small_count)))
-        if direct and layer == 0:
-            last_side = side_sum(
-                chip_parts(
+        if direct:
+            last_chip = chip_parts(
+                [
+                    jnp.concatenate(group, axis=1)
+                    for group in zip(
+                        weight_grad(layer_in, grad_joint),
+                        weight_grad(attended, grad_branch),
+                        halves(small, 0),
+                    )
+                ]
+            )
+        else:
+            last_sums[layer] = reduced(
+                jnp.concatenate(
                     [
-                        jnp.concatenate(group, axis=1)
-                        for group in zip(
-                            weight_grad(layer_in, grad_joint),
-                            weight_grad(attended, grad_branch),
-                            halves(small, 0),
-                        )
-                    ]
+                        dot(layer_in, grad_joint, TN).astype(BF16),
+                        dot(attended, grad_branch, TN).astype(BF16),
+                        small,
+                    ],
+                    axis=1,
                 )
-            )[0]
-        else:
-            last = jnp.concatenate(
-                [
-                    dot(layer_in, grad_joint, TN).astype(BF16),
-                    dot(attended, grad_branch, TN).astype(BF16),
-                    small,
-                ],
-                axis=1,
             )
-        grads[layer] = grad_input
+        ready.append(both_batches(grad_input))
         grad_top = grad_input.astype(BF16).astype(F32)
 
     def settle(first, second):
@@ -584,12 +613,10 @@
         ).astype(F32)
 
     if direct:
-        last_side, wide_sums[0] = tied(last_side, wide_sums[0])
-        last_sums[0] = line_sum(last_side)
-    else:
-        last_sums[0] = reduced(last)
-    last_sums[1] = wide_sums[0][:, 2 * hidden_width :]
-    wide_sums[0] = wide_sums[0][:, : 2 * hidden_width]
+        last_sides = jnp.concatenate([side_sum(last_chip)[0], last_side], axis=-1)
+        last_sides, wide_sums[0], *ready = tied(last_sides, wide_sums[0], *ready)
+        both = line_sum(last_sides)
+        last_sums = [both[:, : both.shape[1] // 2], both[:, both.shape[1] // 2 :]]
     wide = settle(wide_sums[0], wide_sums[1])
     last = settle(last_sums[0], last_sums[1])
     grad_up = (
@@ -605,30 +632,15 @@
         ],
         axis=0,
     )
-    grad_pairs = last[:, : 2 * width].reshape(shard, members, 2, part_width)
-    grad_key = grad_pairs[:, :, 0].reshape(shard, width)
-    grad_value = grad_pairs[:, :, 1].reshape(shard, width)
-    grad_query = last[:, 2 * width : 3 * width]
+    grad_joint = last[:, :joint_width].reshape(shard, members, 3, part_width)
+    grad_key, grad_value, grad_query = [
+        grad_joint[:, :, at].reshape(shard, width) for at in range(3)
+    ]
     grad_out = last[:, 3 * width : 4 * width]
     small = last[:, 4 * width :].T
 
-    def placed_rows(first, second):
-        def halves(value):
-            got = across_half(value[rows:])
-            own = value[:rows]
-            return jnp.stack([jnp.where(low_half, own, got), jnp.where(low_half, got, own)], axis=0)
-
-        first, second = halves(first), halves(second)
-        got = across_section(jnp.where(first_section, second, first))
-        kept = jnp.where(first_section, first, second)
-        return jnp.where(
-            first_section,
-            jnp.concatenate([kept, got], axis=0),
-            jnp.concatenate([got, kept], axis=0),
-        )
-
-    outputs_all = placed_rows(outputs[0], outputs[1])
-    grad_inputs = placed_rows(grads[0], grads[1])
+    outputs_all = placed(ready[0], ready[1])
+    grad_inputs = placed(ready[3], ready[2])
     return (
         outputs_all[None],
         grad_inputs[None],

time: 742 us -> 713 us (0.961)
  local copies, waits for them, and re-layouts: 88.6 us -> 60.9 us
  other arithmetic: 47 us -> 55.5 us
    ppermute x39 -> x27, waiting for transfers between devices: 182 us -> 160 us  [across_member(): return lax.ppermute(value, GROUP, pairs)]
    ppermute x7, waiting for transfers between devices: 62.3 us -> 43.2 us  [across_half(): lax.ppermute(value, 'blk', [(at, (at + half) % blk_count) for at in range...]
    ppermute x3 -> x1, waiting for transfers between devices: 34.4 us -> 16.6 us  [across_section(): return lax.ppermute(value, 'section', [(0, 1), (1, 0)])]
    ppermute x0 -> x4, waiting for transfers between devices: none -> 16 us  [the longest x2 11.9 us: placed(): lax.ppermute(second.astype(BF16), 'section', moves[1]).astype(first.dtype)]
    another operation x37 -> x33, local copies, waits for them, and re-layouts: 23.2 us -> 8.44 us
    ppermute x1 -> x2, waiting for transfers between devices: 0.01 us -> 13.2 us  [across_side(): lax.ppermute(value, 'head', [(at, at ^ 2) for at in range(head_count)])]
    all_gather x1, waiting for transfers between devices: 0.02 us -> 12.6 us  [body(): lax.all_gather(jnp.where(first_section, rest_local, rest_other), GROUP, a...]
    ppermute x39 -> x27, starting transfers between devices: 46 us -> 34.9 us  [across_member(): return lax.ppermute(value, GROUP, pairs)]
  transfers between devices with their start and end apart: 66 -> 58, of which waited for: 41 -> 39; matrix products, arithmetic and copies ran while one was open for 27% -> 24% of each run, Pallas kernels for 9% -> 9%
where the time goes in v4:
time: 713 us; the launch traced here: 706 us
  waiting for transfers between devices  337 us (47%)
  matrix products  99.1 us (14%)
  starting transfers between devices  71.2 us (10%)
  Pallas kernels  65.7 us (9%)
  local copies, waits for them, and re-layouts  60.9 us (9%)
  other arithmetic  55.5 us (8%)
  between operations  16.8 us (2%)
    ppermute x27, waiting for transfers between devices, across_member(): return lax.ppermute(value, GROUP, pairs)  160 us
    dot_general x46, matrix products, dot(): return lax.dot_general(left, right, dims, preferred_element_type=F32)  99.1 us
    all_gather x1, waiting for transfers between devices, body(): lax.all_gather(first_local, ('section',) + GROUP, axis=0, tiled=True)  52.2 us
    ppermute x7, waiting for transfers between devices, across_half(): lax.ppermute(value, 'blk', [(at, (at + half) % blk_count) for at in range...  43.2 us
    pallas_call x2, Pallas kernels, attention_backward(): pl.pallas_call(attention_backward_kernel, grid=(count // block,), in_spec...  36.5 us
    ppermute x27, starting transfers between devices, across_member(): return lax.ppermute(value, GROUP, pairs)  34.9 us
    pallas_call x2, Pallas kernels, attention_forward(): pl.pallas_call(attention_forward_kernel, grid=(count // block,), in_specs...  29.3 us
    ppermute x1, waiting for transfers between devices, across_section(): return lax.ppermute(value, 'section', [(0, 1), (1, 0)])  16.6 us
  transfers between devices with their start and end apart: 58, of which 39 were waited for; matrix products, arithmetic and copies ran while one was open for 24% of the time, Pallas kernels for 9%

profile of v4, /device:TPU:0, one launch (start us, length us, event | category | flops | bytes accessed | tf_op | source)
XLA Modules:
  0.0 705.8 jit_solution(3277163516039551107)
XLA Ops:
  19.8 16.6 %collective-permute-done.13 = bf16[48,6912]{1,0:T(8,128)(2,1)S(1)} collective-permute-done((bf16[48,6912]{1,0:T(8,128)(2,1)S(1)}, bf16[48,6912]{1,0:T(8,128)(2,1)S(1)}, u32[]{:S(2)}, u32[]{:S(2)}) %collective-permute-start.13) | collective-permute-done | bytes 663584 | tf_op jit(solution)/shard_map/ppermute | solution.py:258
  41.4 52.2 %all-gather.4.cloned.1.call-done = bf16[1536,2432]{1,0:T(8,128)(2,1)} async-done(((bf16[48,2432]{1,0:T(8,128)(2,1)}), bf16[1536,2432]{1,0:T(8,128)(2,1)}) %all-gather.4.cloned.1.call-update) | async-done | bytes 7471120 | tf_op jit(solution)/shard_map/all_gather | solution.py:391
  111.0 20.1 %collective-permute-done.3 = bf16[224,576]{1,0:T(8,128)(2,1)S(1)} collective-permute-done((bf16[224,576]{1,0:T(8,128)(2,1)S(1)}, bf16[224,576]{1,0:T(8,128)(2,1)S(1)}, u32[]{:S(2)}, u32[]{:S(2)}) %collective-permute-start.3) | collective-permute-done | bytes 258080 | tf_op jit(solution)/shard_map/ppermute | solution.py:269
  131.1 8.8 %collective-permute-done.1 = bf16[224,576]{1,0:T(8,128)(2,1)S(1)} collective-permute-done((bf16[224,576]{1,0:T(8,128)(2,1)S(1)}, bf16[224,576]{1,0:T(8,128)(2,1)S(1)}, u32[]{:S(2)}, u32[]{:S(2)}) %collective-permute-start.1) | collective-permute-done | bytes 258080 | tf_op jit(solution)/shard_map/ppermute | solution.py:269
  155.4 14.6 %attention_forward.2 = (f32[896,192]{1,0:T(8,128)S(1)}, f32[8,896]{1,0:T(8,128)S(1)}) custom-call(bf16[896,192]{1,0:T(8,128)(2,1)S(1)} %pad_maximum_fusion.19.q_ref, bf16[1792,384]{1,0:T(8,128)(2,1)S(1)} %pad_maximum_fusion.5.kv_ref, s32[1,896]{1,0:T(1,128)S(1)} %slice_bitcast_fusion.4.qid_ref, s32[1792,1]{1,0:T(8,128)S(1)} %copy.244.mark_ref), custom_call_target="tpu_custom_call" | custom-call | flops 19730006016 | bytes 4816896 | tf_op jit(solution)/shard_map/attention_forward/pallas_call | solution.py:134
  185.0 12.6 %all-gather.6.cloned.1.call-done = bf16[768,6912]{1,0:T(8,128)(2,1)} async-done(((bf16[48,6912]{1,0:T(8,128)(2,1)}), bf16[768,6912]{1,0:T(8,128)(2,1)}) %all-gather.6.cloned.1.call-update) | async-done | bytes 10616848 | tf_op jit(solution)/shard_map/all_gather | solution.py:393
  199.7 10.3 %multiply_convert_fusion.1 = (bf16[224,3072]{1,0:T(8,128)(2,1)S(1)}, f32[224,3072]{1,0:T(8,128)}, f32[224,3072]{1,0:T(8,128)}) fusion(f32[3072]{0:T(1024)S(1)} %add.394, bf16[768,6912]{1,0:T(8,128)(2,1)} %all-gather.6.cloned.1.call-done, f32[224,768]{1,0:T(8,128)S(1)} %get-tuple-element.273, f32[768]{0:T(1024)S(1)} %get-tuple-element.145, ...), kind=kOutput, calls=%fused_computation.51 | convolution fusion | flops 1102553088 | bytes 12308224 | tf_op jit(solution)/shard_map/dot_general | solution.py:21
  232.1 7.6 %collective-permute-done.16 = bf16[224,576]{1,0:T(8,128)(2,1)S(1)} collective-permute-done((bf16[224,576]{1,0:T(8,128)(2,1)S(1)}, bf16[224,576]{1,0:T(8,128)(2,1)S(1)}, u32[]{:S(2)}, u32[]{:S(2)}) %collective-permute-start.16) | collective-permute-done | bytes 258080 | tf_op jit(solution)/shard_map/ppermute | solution.py:269
  239.8 9.3 %collective-permute-done.15 = bf16[224,576]{1,0:T(8,128)(2,1)S(1)} collective-permute-done((bf16[224,576]{1,0:T(8,128)(2,1)S(1)}, bf16[224,576]{1,0:T(8,128)(2,1)S(1)}, u32[]{:S(2)}, u32[]{:S(2)}) %collective-permute-start.15) | collective-permute-done | bytes 258080 | tf_op jit(solution)/shard_map/ppermute | solution.py:269
  249.1 9.2 %collective-permute-done.14 = bf16[224,576]{1,0:T(8,128)(2,1)S(1)} collective-permute-done((bf16[224,576]{1,0:T(8,128)(2,1)S(1)}, bf16[224,576]{1,0:T(8,128)(2,1)S(1)}, u32[]{:S(2)}, u32[]{:S(2)}) %collective-permute-start.14) | collective-permute-done | bytes 258080 | tf_op jit(solution)/shard_map/ppermute | solution.py:269
  260.8 14.6 %attention_forward.3 = (f32[896,192]{1,0:T(8,128)S(1)}, f32[8,896]{1,0:T(8,128)S(1)}) custom-call(bf16[896,192]{1,0:T(8,128)(2,1)S(1)} %pad_maximum_fusion.18.q_ref, bf16[1792,384]{1,0:T(8,128)(2,1)S(1)} %pad_maximum_fusion.6.kv_ref, s32[1,896]{1,0:T(1,128)S(1)} %slice_bitcast_fusion.4.qid_ref, s32[1792,1]{1,0:T(8,128)S(1)} %copy.244.mark_ref), custom_call_target="tpu_custom_call" | custom-call | flops 19730006016 | bytes 4816896 | tf_op jit(solution)/shard_map/attention_forward/pallas_call | solution.py:134
  282.0 11.6 %collective-permute-done.20 = bf16[224,192]{1,0:T(8,128)(2,1)S(1)} collective-permute-done((bf16[224,192]{1,0:T(8,128)(2,1)}, bf16[224,192]{1,0:T(8,128)(2,1)S(1)}, u32[]{:S(2)}, u32[]{:S(2)}) %collective-permute-start.20) | collective-permute-done | bytes 86048 | tf_op jit(solution)/shard_map/ppermute | solution.py:269
  293.6 4.7 collective-permute-done.18
  302.2 9.0 %multiply_convert_fusion = (bf16[224,3072]{1,0:T(8,128)(2,1)S(1)}, f32[224,3072]{1,0:T(8,128)S(1)}, f32[224,3072]{1,0:T(8,128)S(1)}) fusion(f32[3072]{0:T(1024)S(1)} %add.419, bf16[768,6912]{1,0:T(8,128)(2,1)} %all-gather.8.cloned.1.call-done, f32[224,768]{1,0:T(8,128)S(1)} %get-tuple-element.278, f32[768]{0:T(1024)S(1)} %get-tuple-element.137, ...), kind=kOutput, calls=%fused_computation.38 | convolution fusion | flops 1102553088 | bytes 12308224 | tf_op jit(solution)/shard_map/dot_general | solution.py:21
  340.1 5.0 collective-permute-start.24
  353.8 18.2 %attention_backward.2 = (bf16[896,192]{1,0:T(8,128)(2,1)S(1)}, bf16[1792,384]{1,0:T(8,128)(2,1)S(1)}) custom-call(bf16[896,192]{1,0:T(8,128)(2,1)S(1)} %pad_maximum_fusion.18.q_ref, bf16[1792,384]{1,0:T(8,128)(2,1)S(1)} %pad_maximum_fusion.6.kv_ref, s32[1,896]{1,0:T(1,128)S(1)} %slice_bitcast_fusion.4.qid_ref, s32[1792,1]{1,0:T(8,128)S(1)} %copy-done.3, ...), custom_call_target="tpu_custom_call" | custom-call | flops 49325015040 | bytes 4816896 | tf_op jit(solution)/shard_map/attention_backward/pallas_call | solution.py:165
  386.6 20.4 %collective-permute-done.28 = bf16[224,576]{1,0:T(8,128)(2,1)S(1)} collective-permute-done((bf16[224,576]{1,0:T(8,128)(2,1)}, bf16[224,576]{1,0:T(8,128)(2,1)S(1)}, u32[]{:S(2)}, u32[]{:S(2)}) %collective-permute-start.28) | collective-permute-done | bytes 258080 | tf_op jit(solution)/shard_map/ppermute | solution.py:269
  407.0 12.0 %collective-permute-done.26 = bf16[224,576]{1,0:T(8,128)(2,1)} collective-permute-done((bf16[224,576]{1,0:T(8,128)(2,1)S(1)}, bf16[224,576]{1,0:T(8,128)(2,1)}, u32[]{:S(2)}, u32[]{:S(2)}) %collective-permute-start.26) | collective-permute-done | bytes 258080 | tf_op jit(solution)/shard_map/ppermute | solution.py:269
  425.6 4.8 fusion.160
  457.5 5.3 multiply_reduce_fusion
  481.8 18.2 %attention_backward.3 = (bf16[896,192]{1,0:T(8,128)(2,1)S(1)}, bf16[1792,384]{1,0:T(8,128)(2,1)S(1)}) custom-call(bf16[896,192]{1,0:T(8,128)(2,1)S(1)} %copy-done.10, bf16[1792,384]{1,0:T(8,128)(2,1)S(1)} %copy-done.1, s32[1,896]{1,0:T(1,128)S(1)} %slice_bitcast_fusion.4.qid_ref, s32[1792,1]{1,0:T(8,128)S(1)} %copy-done.4, f32[896,192]{1,0:T(8,128)S(1)} %copy-done.6, ...), custom_call_target="tpu_custom_call" | custom-call | flops 49325015040 | bytes 4816896 | tf_op jit(solution)/shard_map/attention_backward/pallas_call | solution.py:165
  500.1 8.4 %collective-permute-done.33 = bf16[1,4,48,3200]{3,2,1,0:T(8,128)(2,1)S(1)} collective-permute-done((bf16[1,4,48,3200]{3,2,1,0:T(8,128)(2,1)S(1)}, bf16[1,4,48,3200]{3,2,1,0:T(8,128)(2,1)S(1)}, u32[]{:S(2)}, u32[]{:S(2)}) %collective-permute-start.33) | collective-permute-done | bytes 1228832 | tf_op jit(solution)/shard_map/ppermute | solution.py:286
  522.4 20.7 %collective-permute-done.37 = bf16[224,576]{1,0:T(8,128)(2,1)S(1)} collective-permute-done((bf16[224,576]{1,0:T(8,128)(2,1)}, bf16[224,576]{1,0:T(8,128)(2,1)S(1)}, u32[]{:S(2)}, u32[]{:S(2)}) %collective-permute-start.37) | collective-permute-done | bytes 258080 | tf_op jit(solution)/shard_map/ppermute | solution.py:269
  543.1 16.6 %collective-permute-done.35 = bf16[224,576]{1,0:T(8,128)(2,1)S(1)} collective-permute-done((bf16[224,576]{1,0:T(8,128)(2,1)S(1)}, bf16[224,576]{1,0:T(8,128)(2,1)S(1)}, u32[]{:S(2)}, u32[]{:S(2)}) %collective-permute-start.35) | collective-permute-done | bytes 258080 | tf_op jit(solution)/shard_map/ppermute | solution.py:269
  568.8 11.4 %collective-permute-done.40 = bf16[112,768]{1,0:T(8,128)(2,1)S(1)} collective-permute-done((bf16[112,768]{1,0:T(8,128)(2,1)S(1)}, bf16[112,768]{1,0:T(8,128)(2,1)S(1)}, u32[]{:S(2)}, u32[]{:S(2)}) %collective-permute-start.40) | collective-permute-done | bytes 172064 | tf_op jit(solution)/shard_map/ppermute | solution.py:261
  580.2 10.7 %collective-permute-done.41 = bf16[112,768]{1,0:T(8,128)(2,1)S(1)} collective-permute-done((bf16[112,768]{1,0:T(8,128)(2,1)S(1)}, bf16[112,768]{1,0:T(8,128)(2,1)S(1)}, u32[]{:S(2)}, u32[]{:S(2)}) %collective-permute-start.41) | collective-permute-done | bytes 172064 | tf_op jit(solution)/shard_map/ppermute | solution.py:261
  600.4 13.6 %collective-permute-done.42 = bf16[112,768]{1,0:T(8,128)(2,1)S(1)} collective-permute-done((bf16[112,768]{1,0:T(8,128)(2,1)S(1)}, bf16[112,768]{1,0:T(8,128)(2,1)S(1)}, u32[]{:S(2)}, u32[]{:S(2)}) %collective-permute-start.42) | collective-permute-done | bytes 172064 | tf_op jit(solution)/shard_map/ppermute | solution.py:261
  617.7 4.7 collective-permute-done.39
  627.3 4.6 collective-permute-start.45
  633.3 4.9 collective-permute-start.51
  646.0 11.9 %collective-permute-done.47 = bf16[2,112,768]{2,1,0:T(8,128)(2,1)S(1)} collective-permute-done((bf16[2,112,768]{2,1,0:T(8,128)(2,1)S(1)}, bf16[2,112,768]{2,1,0:T(8,128)(2,1)S(1)}, u32[]{:S(2)}, u32[]{:S(2)}) %collective-permute-start.47) | collective-permute-done | bytes 344096 | tf_op jit(solution)/shard_map/ppermute | solution.py:492
  664.6 9.7 %reduce-scatter.8.cloned.1.call-done = bf16[1,48,6400]{2,1,0:T(8,128)(2,1)} async-done(((bf16[4,48,6400]{2,1,0:T(8,128)(2,1)}), bf16[1,48,6400]{2,1,0:T(8,128)(2,1)}) %reduce-scatter.8.cloned.1.call-update) | async-done | bytes 614416 | tf_op jit(solution)/shard_map/reduce_scatter | solution.py:321
  (551 shorter events, 286.5 us)
Async XLA Ops:
  7.2 86.5 %all-gather.4.cloned.1.call-start = ((), (), s32[]{:S(2)}) async-start(), calls=%async_computation.3 | async-start | bytes 7704576 | tf_op jit(solution)/shard_map/all_gather | solution.py:391
  13.3 184.3 %all-gather.6.cloned.1.call-start = ((), (), s32[]{:S(2)}) async-start(), calls=%async_computation.4 | async-start | bytes 11280384 | tf_op jit(solution)/shard_map/all_gather | solution.py:393
  16.8 19.6 %collective-permute-start.13 = (bf16[48,6912]{1,0:T(8,128)(2,1)S(1)}, bf16[48,6912]{1,0:T(8,128)(2,1)S(1)}, u32[]{:S(2)}, u32[]{:S(2)}) collective-permute-start(bf16[48,6912]{1,0:T(8,128)(2,1)S(1)} %bitcast_dynamic-update-slice_fusion), channel_id=1, source_target_pairs={{0,16},{16,0},{1,17},{17,1},{2,18},{18,2},{3,19},{19,3},{4,20},{20... | collective-permute-start | bytes 1990664 | tf_op jit(solution)/shard_map/ppermute | solution.py:258
  37.7 262.3 %all-gather.8.cloned.1.call-start = ((), (), s32[]{:S(2)}) async-start(), calls=%async_computation.5 | async-start | bytes 11280384 | tf_op jit(solution)/shard_map/all_gather | solution.py:396
  38.4 419.1 %reduce-scatter.4.cloned.1.call-start = ((), (), s32[]{:S(2)}) async-start(), calls=%async_computation.6 | async-start | bytes 10027008 | tf_op jit(solution)/shard_map/reduce_scatter | solution.py:502
  38.5 60.7 %collective-permute-start = (bf16[112,768]{1,0:T(8,128)(2,1)S(1)}, bf16[112,768]{1,0:T(8,128)(2,1)S(1)}, u32[]{:S(2)}, u32[]{:S(2)}) collective-permute-start(bf16[112,768]{1,0:T(8,128)(2,1)S(1)} %get-tuple-element.213), channel_id=1, source_target_pairs={{0,2},{1,3},{2,0},{3,1},{4,6},{5,7},{6,4},{7,5},{8,10},{9,11},{10,... | collective-permute-start | bytes 516104 | tf_op jit(solution)/shard_map/ppermute | solution.py:261
  107.2 23.9 %collective-permute-start.3 = (bf16[224,576]{1,0:T(8,128)(2,1)S(1)}, bf16[224,576]{1,0:T(8,128)(2,1)S(1)}, u32[]{:S(2)}, u32[]{:S(2)}) collective-permute-start(bf16[224,576]{1,0:T(8,128)(2,1)S(1)} %bitcast.316), channel_id=1, source_target_pairs={{0,9},{1,8},{2,11},{3,10},{4,13},{5,12},{6,15},{7,14},{8,1},{9,0},... | collective-permute-start | bytes 774152 | tf_op jit(solution)/shard_map/ppermute | solution.py:269
  109.7 21.4 %collective-permute-start.2 = (bf16[224,576]{1,0:T(8,128)(2,1)S(1)}, bf16[224,576]{1,0:T(8,128)(2,1)S(1)}, u32[]{:S(2)}, u32[]{:S(2)}) collective-permute-start(bf16[224,576]{1,0:T(8,128)(2,1)S(1)} %bitcast.318), channel_id=1, source_target_pairs={{0,8},{1,9},{2,10},{3,11},{4,12},{5,13},{6,14},{7,15},{8,0},{9,1},... | collective-permute-start | bytes 774152 | tf_op jit(solution)/shard_map/ppermute | solution.py:269
  110.4 29.6 %collective-permute-start.1 = (bf16[224,576]{1,0:T(8,128)(2,1)S(1)}, bf16[224,576]{1,0:T(8,128)(2,1)S(1)}, u32[]{:S(2)}, u32[]{:S(2)}) collective-permute-start(bf16[224,576]{1,0:T(8,128)(2,1)S(1)} %bitcast.320), channel_id=1, source_target_pairs={{0,1},{1,0},{2,3},{3,2},{4,5},{5,4},{6,7},{7,6},{8,9},{9,8},{10,11... | collective-permute-start | bytes 774152 | tf_op jit(solution)/shard_map/ppermute | solution.py:269
  230.5 18.6 %collective-permute-start.15 = (bf16[224,576]{1,0:T(8,128)(2,1)S(1)}, bf16[224,576]{1,0:T(8,128)(2,1)S(1)}, u32[]{:S(2)}, u32[]{:S(2)}) collective-permute-start(bf16[224,576]{1,0:T(8,128)(2,1)S(1)} %bitcast.319), channel_id=1, source_target_pairs={{0,8},{1,9},{2,10},{3,11},{4,12},{5,13},{6,14},{7,15},{8,0},{9,1},... | collective-permute-start | bytes 774152 | tf_op jit(solution)/shard_map/ppermute | solution.py:269
  232.0 26.3 %collective-permute-start.14 = (bf16[224,576]{1,0:T(8,128)(2,1)S(1)}, bf16[224,576]{1,0:T(8,128)(2,1)S(1)}, u32[]{:S(2)}, u32[]{:S(2)}) collective-permute-start(bf16[224,576]{1,0:T(8,128)(2,1)S(1)} %bitcast.321), channel_id=1, source_target_pairs={{0,1},{1,0},{2,3},{3,2},{4,5},{5,4},{6,7},{7,6},{8,9},{9,8},{10,11... | collective-permute-start | bytes 774152 | tf_op jit(solution)/shard_map/ppermute | solution.py:269
  277.1 16.5 %collective-permute-start.20 = (bf16[224,192]{1,0:T(8,128)(2,1)}, bf16[224,192]{1,0:T(8,128)(2,1)S(1)}, u32[]{:S(2)}, u32[]{:S(2)}) collective-permute-start(bf16[224,192]{1,0:T(8,128)(2,1)} %get-tuple-element.225), channel_id=1, source_target_pairs={{0,9},{1,8},{2,11},{3,10},{4,13},{5,12},{6,15},{7,14},{8,1},{9,0},... | collective-permute-start | bytes 258056 | tf_op jit(solution)/shard_map/ppermute | solution.py:269
  278.6 19.7 %collective-permute-start.18 = (bf16[224,192]{1,0:T(8,128)(2,1)S(1)}, bf16[224,192]{1,0:T(8,128)(2,1)}, u32[]{:S(2)}, u32[]{:S(2)}) collective-permute-start(bf16[224,192]{1,0:T(8,128)(2,1)S(1)} %get-tuple-element.227), channel_id=1, source_target_pairs={{0,1},{1,0},{2,3},{3,2},{4,5},{5,4},{6,7},{7,6},{8,9},{9,8},{10,11... | collective-permute-start | bytes 258056 | tf_op jit(solution)/shard_map/ppermute | solution.py:269
  281.5 32.0 %collective-permute-start.21 = (f32[112,768]{1,0:T(8,128)}, f32[112,768]{1,0:T(8,128)}, u32[]{:S(2)}, u32[]{:S(2)}) collective-permute-start(f32[112,768]{1,0:T(8,128)} %get-tuple-element.175), channel_id=1, source_target_pairs={{0,2},{1,3},{2,0},{3,1},{4,6},{5,7},{6,4},{7,5},{8,10},{9,11},{10,... | collective-permute-start | bytes 1032200 | tf_op jit(solution)/shard_map/ppermute | solution.py:261
  330.9 295.0 %reduce-scatter.6.cloned.1.call-start = ((), (), s32[]{:S(2)}) async-start(), calls=%async_computation.7 | async-start | bytes 10027008 | tf_op jit(solution)/shard_map/reduce_scatter | solution.py:502
  380.0 27.0 %collective-permute-start.28 = (bf16[224,576]{1,0:T(8,128)(2,1)}, bf16[224,576]{1,0:T(8,128)(2,1)S(1)}, u32[]{:S(2)}, u32[]{:S(2)}) collective-permute-start(bf16[224,576]{1,0:T(8,128)(2,1)} %get-tuple-element.197), channel_id=1, source_target_pairs={{0,9},{1,8},{2,11},{3,10},{4,13},{5,12},{6,15},{7,14},{8,1},{9,0},... | collective-permute-start | bytes 774152 | tf_op jit(solution)/shard_map/ppermute | solution.py:269
  381.9 25.1 %collective-permute-start.27 = (bf16[224,576]{1,0:T(8,128)(2,1)S(1)}, bf16[224,576]{1,0:T(8,128)(2,1)S(1)}, u32[]{:S(2)}, u32[]{:S(2)}) collective-permute-start(bf16[224,576]{1,0:T(8,128)(2,1)S(1)} %get-tuple-element.198), channel_id=1, source_target_pairs={{0,8},{1,9},{2,10},{3,11},{4,12},{5,13},{6,14},{7,15},{8,0},{9,1},... | collective-permute-start | bytes 774152 | tf_op jit(solution)/shard_map/ppermute | solution.py:269
  383.3 35.7 %collective-permute-start.26 = (bf16[224,576]{1,0:T(8,128)(2,1)S(1)}, bf16[224,576]{1,0:T(8,128)(2,1)}, u32[]{:S(2)}, u32[]{:S(2)}) collective-permute-start(bf16[224,576]{1,0:T(8,128)(2,1)S(1)} %get-tuple-element.196), channel_id=1, source_target_pairs={{0,1},{1,0},{2,3},{3,2},{4,5},{5,4},{6,7},{7,6},{8,9},{9,8},{10,11... | collective-permute-start | bytes 774152 | tf_op jit(solution)/shard_map/ppermute | solution.py:269
  425.6 52.7 %collective-permute-start.32 = (bf16[384,3200]{1,0:T(8,128)(2,1)}, bf16[384,3200]{1,0:T(8,128)(2,1)}, u32[]{:S(2)}, u32[]{:S(2)}) collective-permute-start(bf16[384,3200]{1,0:T(8,128)(2,1)} %pad_maximum_fusion.1), channel_id=1, source_target_pairs={{0,4},{4,0},{8,12},{12,8},{1,5},{5,1},{9,13},{13,9},{2,6},{6,2},{1... | collective-permute-start | bytes 7372808 | tf_op jit(solution)/shard_map/ppermute | solution.py:272
  476.3 197.9 %reduce-scatter.8.cloned.1.call-start = ((), (), s32[]{:S(2)}) async-start(), calls=%async_computation.8 | async-start | bytes 3072000 | tf_op jit(solution)/shard_map/reduce_scatter | solution.py:321
  480.2 28.3 %collective-permute-start.33 = (bf16[1,4,48,3200]{3,2,1,0:T(8,128)(2,1)S(1)}, bf16[1,4,48,3200]{3,2,1,0:T(8,128)(2,1)S(1)}, u32[]{:S(2)}, u32[]{:S(2)}) collective-permute-start(bf16[1,4,48,3200]{3,2,1,0:T(8,128)(2,1)S(1)} %fusion.71), channel_id=1, source_target_pairs={{0,8},{4,12},{8,0},{12,4},{1,9},{5,13},{9,1},{13,5},{2,10},{6,14},... | collective-permute-start | bytes 3686408 | tf_op jit(solution)/shard_map/ppermute | solution.py:286
  516.2 27.0 %collective-permute-start.37 = (bf16[224,576]{1,0:T(8,128)(2,1)}, bf16[224,576]{1,0:T(8,128)(2,1)S(1)}, u32[]{:S(2)}, u32[]{:S(2)}) collective-permute-start(bf16[224,576]{1,0:T(8,128)(2,1)} %get-tuple-element.189), channel_id=1, source_target_pairs={{0,9},{1,8},{2,11},{3,10},{4,13},{5,12},{6,15},{7,14},{8,1},{9,0},... | collective-permute-start | bytes 774152 | tf_op jit(solution)/shard_map/ppermute | solution.py:269
  517.5 25.6 %collective-permute-start.36 = (bf16[224,576]{1,0:T(8,128)(2,1)}, bf16[224,576]{1,0:T(8,128)(2,1)S(1)}, u32[]{:S(2)}, u32[]{:S(2)}) collective-permute-start(bf16[224,576]{1,0:T(8,128)(2,1)} %get-tuple-element.190), channel_id=1, source_target_pairs={{0,8},{1,9},{2,10},{3,11},{4,12},{5,13},{6,14},{7,15},{8,0},{9,1},... | collective-permute-start | bytes 774152 | tf_op jit(solution)/shard_map/ppermute | solution.py:269
  519.3 40.4 %collective-permute-start.35 = (bf16[224,576]{1,0:T(8,128)(2,1)S(1)}, bf16[224,576]{1,0:T(8,128)(2,1)S(1)}, u32[]{:S(2)}, u32[]{:S(2)}) collective-permute-start(bf16[224,576]{1,0:T(8,128)(2,1)S(1)} %get-tuple-element.188), channel_id=1, source_target_pairs={{0,1},{1,0},{2,3},{3,2},{4,5},{5,4},{6,7},{7,6},{8,9},{9,8},{10,11... | collective-permute-start | bytes 774152 | tf_op jit(solution)/shard_map/ppermute | solution.py:269
  565.5 26.7 %collective-permute-start.38 = (bf16[384,3200]{1,0:T(8,128)(2,1)}, bf16[384,3200]{1,0:T(8,128)(2,1)}, u32[]{:S(2)}, u32[]{:S(2)}) collective-permute-start(bf16[384,3200]{1,0:T(8,128)(2,1)} %pad_maximum_fusion.3), channel_id=1, source_target_pairs={{0,4},{4,0},{8,12},{12,8},{1,5},{5,1},{9,13},{13,9},{2,6},{6,2},{1... | collective-permute-start | bytes 7372808 | tf_op jit(solution)/shard_map/ppermute | solution.py:272
  565.9 25.0 %collective-permute-start.41 = (bf16[112,768]{1,0:T(8,128)(2,1)S(1)}, bf16[112,768]{1,0:T(8,128)(2,1)S(1)}, u32[]{:S(2)}, u32[]{:S(2)}) collective-permute-start(bf16[112,768]{1,0:T(8,128)(2,1)S(1)} %slice.627), channel_id=1, source_target_pairs={{0,2},{1,3},{2,0},{3,1},{4,6},{5,7},{6,4},{7,5},{8,10},{9,11},{10,... | collective-permute-start | bytes 516104 | tf_op jit(solution)/shard_map/ppermute | solution.py:261
  593.8 28.6 %collective-permute-start.39 = (bf16[1,4,48,3200]{3,2,1,0:T(8,128)(2,1)S(1)}, bf16[1,4,48,3200]{3,2,1,0:T(8,128)(2,1)S(1)}, u32[]{:S(2)}, u32[]{:S(2)}) collective-permute-start(bf16[1,4,48,3200]{3,2,1,0:T(8,128)(2,1)S(1)} %fusion.72), channel_id=1, source_target_pairs={{0,8},{4,12},{8,0},{12,4},{1,9},{5,13},{9,1},{13,5},{2,10},{6,14},... | collective-permute-start | bytes 3686408 | tf_op jit(solution)/shard_map/ppermute | solution.py:286
  594.0 20.0 %collective-permute-start.42 = (bf16[112,768]{1,0:T(8,128)(2,1)S(1)}, bf16[112,768]{1,0:T(8,128)(2,1)S(1)}, u32[]{:S(2)}, u32[]{:S(2)}) collective-permute-start(bf16[112,768]{1,0:T(8,128)(2,1)S(1)} %slice.629), channel_id=1, source_target_pairs={{0,2},{1,3},{2,0},{3,1},{4,6},{5,7},{6,4},{7,5},{8,10},{9,11},{10,... | collective-permute-start | bytes 516104 | tf_op jit(solution)/shard_map/ppermute | solution.py:261
  597.5 20.2 %collective-permute-start.43 = (bf16[112,768]{1,0:T(8,128)(2,1)S(1)}, bf16[112,768]{1,0:T(8,128)(2,1)S(1)}, u32[]{:S(2)}, u32[]{:S(2)}) collective-permute-start(bf16[112,768]{1,0:T(8,128)(2,1)S(1)} %slice.883), channel_id=1, source_target_pairs={{0,2},{1,3},{2,0},{3,1},{4,6},{5,7},{6,4},{7,5},{8,10},{9,11},{10,... | collective-permute-start | bytes 516104 | tf_op jit(solution)/shard_map/ppermute | solution.py:261
  633.3 25.9 %collective-permute-start.51 = (bf16[48,6144]{1,0:T(8,128)(2,1)S(1)}, bf16[48,6144]{1,0:T(8,128)(2,1)S(1)}, u32[]{:S(2)}, u32[]{:S(2)}) collective-permute-start(bf16[48,6144]{1,0:T(8,128)(2,1)S(1)} %copy-done.54), channel_id=1, source_target_pairs={{0,16},{1,17},{2,18},{3,19},{4,20},{5,21},{6,22},{7,23},{8,24},{9,... | collective-permute-start | bytes 1769480 | tf_op jit(solution)/shard_map/ppermute | solution.py:610
  638.2 19.7 %collective-permute-start.47 = (bf16[2,112,768]{2,1,0:T(8,128)(2,1)S(1)}, bf16[2,112,768]{2,1,0:T(8,128)(2,1)S(1)}, u32[]{:S(2)}, u32[]{:S(2)}) collective-permute-start(bf16[2,112,768]{2,1,0:T(8,128)(2,1)S(1)} %convert_element_type.418), channel_id=1, source_target_pairs={{0,16},{1,17},{2,18},{3,19},{4,20},{5,21},{6,22},{7,23},{8,24},{9,... | collective-permute-start | bytes 1032200 | tf_op jit(solution)/shard_map/ppermute | solution.py:492
  639.5 19.7 %collective-permute-start.50 = (bf16[48,6144]{1,0:T(8,128)(2,1)S(1)}, bf16[48,6144]{1,0:T(8,128)(2,1)S(1)}, u32[]{:S(2)}, u32[]{:S(2)}) collective-permute-start(bf16[48,6144]{1,0:T(8,128)(2,1)S(1)} %copy-done.55), channel_id=1, source_target_pairs={{16,0},{17,1},{18,2},{19,3},{20,4},{21,5},{22,6},{23,7},{24,8},{25... | collective-permute-start | bytes 1769480 | tf_op jit(solution)/shard_map/ppermute | solution.py:609
  (114 other events, 1251.4 us)
Sparse Core Ops, SparseCore 0:
  13.4 80.1 all-gather.3
  96.5 101.0 all-gather.5
  199.9 99.9 all-gather.7
  331.0 126.4 reduce-scatter.3
  476.4 138.1 reduce-scatter.5
  626.0 48.1 reduce-scatter.7

commit v5 on v4

--- a/solution.py
+++ b/solution.py
@@ -120,7 +120,7 @@
 
 def attention_cost(rows, count, width, products):
     return pl.CostEstimate(
-        flops=16 * products * 2 * rows * count * width,
+        flops=products * 2 * rows * count * width,
         bytes_accessed=rows * width * 12 + count * width * 8,
         transcendentals=rows * count * (width // HEAD_DIM),
     )
@@ -152,7 +152,7 @@
             pltpu.VMEM((8, rows), F32),
         ],
         compiler_params=pltpu.CompilerParams(vmem_limit_bytes=VMEM_LIMIT),
-        cost_estimate=attention_cost(rows, count, width, 2),
+        cost_estimate=attention_cost(rows, count, width, 28),
         name="attention_forward",
     )(queries, pairs, query_ids, marks)
 
@@ -189,7 +189,7 @@
             pltpu.VMEM((8, rows), F32),
         ],
         compiler_params=pltpu.CompilerParams(vmem_limit_bytes=VMEM_LIMIT),
-        cost_estimate=attention_cost(rows, count, width, 5),
+        cost_estimate=attention_cost(rows, count, width, 34),
         name="attention_backward",
     )(queries, pairs, query_ids, marks, out, lse, grad_out)
 
@@ -447,7 +447,7 @@
         middle, unit_one, inverse_one = norm_forward(first_sum, gain_one, shift_one)
         middle_low = middle.astype(BF16)
         hidden = dot(middle_low, up_weight) + up_shift
-        share = 0.5 * lax.erfc(hidden * (-(0.5**0.5)))
+        share = 0.5 + 0.5 * lax.erf(hidden * 0.5**0.5)
         slope = share + hidden * jnp.exp(hidden * hidden * -0.5) * 0.3989422804014327
         active = (hidden * share).astype(BF16)
         second = middle + down_shift
@@ -614,7 +614,7 @@
 
     if direct:
         last_sides = jnp.concatenate([side_sum(last_chip)[0], last_side], axis=-1)
-        last_sides, wide_sums[0], *ready = tied(last_sides, wide_sums[0], *ready)
+        last_sides, wide_sums[0], *ready[:3] = tied(last_sides, wide_sums[0], *ready[:3])
         both = line_sum(last_sides)
         last_sums = [both[:, : both.shape[1] // 2], both[:, both.shape[1] // 2 :]]
     wide = settle(wide_sums[0], wide_sums[1])

time: 713 us -> 710 us (level)
  waiting for transfers between devices: 337 us -> 296 us
  local copies, waits for them, and re-layouts: 60.9 us -> 97.6 us
  matrix products: 99.1 us -> 90 us
  other arithmetic: 55.5 us -> 63.9 us
    ppermute x27, waiting for transfers between devices: 160 us -> 115 us  [across_member(): return lax.ppermute(value, GROUP, pairs)]
    ppermute x7, waiting for transfers between devices: 43.2 us -> 60.6 us  [across_half(): lax.ppermute(value, 'blk', [(at, (at + half) % blk_count) for at in range...]
    another operation x15, local copies, waits for them, and re-layouts: 7.08 us -> 16.8 us
    reduce_scatter x1, waiting for transfers between devices: 9.65 us -> 0.01 us  [line_sum(): return lax.psum_scatter(value, 'blk', scatter_dimension=0, tiled=True)[0]]
    dot_general x46, matrix products: 99.1 us -> 90 us  [dot(): return lax.dot_general(left, right, dims, preferred_element_type=F32)]
    unnamed x202 -> x248, local copies, waits for them, and re-layouts: 15 us -> 23.9 us
    ppermute x2, waiting for transfers between devices: 11.9 us -> 4.61 us  [placed(): lax.ppermute(second.astype(BF16), 'section', moves[1]).astype(first.dtype)]
  transfers between devices with their start and end apart: 58 -> 58, of which waited for: 39 -> 41; matrix products, arithmetic and copies ran while one was open for 24% -> 28% of each run, Pallas kernels for 9% -> 10%
where the time goes in v5:
time: 710 us; the launch traced here: 696 us
  waiting for transfers between devices  296 us (42%)
  local copies, waits for them, and re-layouts  97.6 us (14%)
  matrix products  90 us (13%)
  Pallas kernels  67 us (9%)
  starting transfers between devices  65.1 us (9%)
  other arithmetic  63.9 us (9%)
  between operations  16.5 us (2%)
    ppermute x27, waiting for transfers between devices, across_member(): return lax.ppermute(value, GROUP, pairs)  115 us
    dot_general x46, matrix products, dot(): return lax.dot_general(left, right, dims, preferred_element_type=F32)  90 us
    ppermute x7, waiting for transfers between devices, across_half(): lax.ppermute(value, 'blk', [(at, (at + half) % blk_count) for at in range...  60.6 us
    all_gather x1, waiting for transfers between devices, body(): lax.all_gather(first_local, ('section',) + GROUP, axis=0, tiled=True)  51.8 us
    pallas_call x2, Pallas kernels, attention_backward(): pl.pallas_call(attention_backward_kernel, grid=(count // block,), in_spec...  37.1 us
    ppermute x27, starting transfers between devices, across_member(): return lax.ppermute(value, GROUP, pairs)  31.9 us
    pallas_call x2, Pallas kernels, attention_forward(): pl.pallas_call(attention_forward_kernel, grid=(count // block,), in_specs...  29.9 us
    unnamed x248, local copies, waits for them, and re-layouts  23.9 us
  transfers between devices with their start and end apart: 58, of which 41 were waited for; matrix products, arithmetic and copies ran while one was open for 28% of the time, Pallas kernels for 10%

profile of v5, /device:TPU:0, one launch (start us, length us, event | category | flops | bytes accessed | tf_op | source)
XLA Modules:
  0.0 696.2 jit_solution(7240914891645873081)
XLA Ops:
  18.9 16.6 %collective-permute-done.13 = bf16[48,6912]{1,0:T(8,128)(2,1)S(1)} collective-permute-done((bf16[48,6912]{1,0:T(8,128)(2,1)S(1)}, bf16[48,6912]{1,0:T(8,128)(2,1)S(1)}, u32[]{:S(2)}, u32[]{:S(2)}) %collective-permute-start.13) | collective-permute-done | bytes 663584 | tf_op jit(solution)/shard_map/ppermute | solution.py:258
  40.6 51.8 %all-gather.4.cloned.1.call-done = bf16[1536,2432]{1,0:T(8,128)(2,1)} async-done(((bf16[48,2432]{1,0:T(8,128)(2,1)}), bf16[1536,2432]{1,0:T(8,128)(2,1)}) %all-gather.4.cloned.1.call-update) | async-done | bytes 7471120 | tf_op jit(solution)/shard_map/all_gather | solution.py:391
  110.2 19.9 %collective-permute-done.3 = bf16[224,576]{1,0:T(8,128)(2,1)S(1)} collective-permute-done((bf16[224,576]{1,0:T(8,128)(2,1)S(1)}, bf16[224,576]{1,0:T(8,128)(2,1)S(1)}, u32[]{:S(2)}, u32[]{:S(2)}) %collective-permute-start.3) | collective-permute-done | bytes 258080 | tf_op jit(solution)/shard_map/ppermute | solution.py:269
  130.1 8.6 %collective-permute-done.1 = bf16[224,576]{1,0:T(8,128)(2,1)S(1)} collective-permute-done((bf16[224,576]{1,0:T(8,128)(2,1)S(1)}, bf16[224,576]{1,0:T(8,128)(2,1)S(1)}, u32[]{:S(2)}, u32[]{:S(2)}) %collective-permute-start.1) | collective-permute-done | bytes 258080 | tf_op jit(solution)/shard_map/ppermute | solution.py:269
  154.0 14.8 %attention_forward.2 = (f32[896,192]{1,0:T(8,128)S(1)}, f32[8,896]{1,0:T(8,128)S(1)}) custom-call(bf16[896,192]{1,0:T(8,128)(2,1)S(1)} %pad_maximum_fusion.18.q_ref, bf16[1792,384]{1,0:T(8,128)(2,1)S(1)} %pad_maximum_fusion.5.kv_ref, s32[1,896]{1,0:T(1,128)S(1)} %slice_bitcast_fusion.4.qid_ref, s32[1792,1]{1,0:T(8,128)S(1)} %copy.244.mark_ref), custom_call_target="tpu_custom_call" | custom-call | flops 17263755264 | bytes 4816896 | tf_op jit(solution)/shard_map/attention_forward/pallas_call | solution.py:134
  174.5 5.7 collective-permute-done.12
  180.2 6.1 collective-permute-done.10
  187.9 8.5 %all-gather.6.cloned.1.call-done = bf16[768,6912]{1,0:T(8,128)(2,1)} async-done(((bf16[48,6912]{1,0:T(8,128)(2,1)}), bf16[768,6912]{1,0:T(8,128)(2,1)}) %all-gather.6.cloned.1.call-update) | async-done | bytes 10616848 | tf_op jit(solution)/shard_map/all_gather | solution.py:393
  198.5 5.6 multiply_convert_fusion.1
  220.3 5.0 constant_dynamic-slice_fusion.17
  229.2 9.5 %collective-permute-done.16 = bf16[224,576]{1,0:T(8,128)(2,1)S(1)} collective-permute-done((bf16[224,576]{1,0:T(8,128)(2,1)S(1)}, bf16[224,576]{1,0:T(8,128)(2,1)S(1)}, u32[]{:S(2)}, u32[]{:S(2)}) %collective-permute-start.16) | collective-permute-done | bytes 258080 | tf_op jit(solution)/shard_map/ppermute | solution.py:269
  238.7 5.2 collective-permute-done.15
  243.8 5.6 collective-permute-done.14
  251.8 15.0 %attention_forward.3 = (f32[896,192]{1,0:T(8,128)S(1)}, f32[8,896]{1,0:T(8,128)S(1)}) custom-call(bf16[896,192]{1,0:T(8,128)(2,1)S(1)} %pad_maximum_fusion.17.q_ref, bf16[1792,384]{1,0:T(8,128)(2,1)S(1)} %pad_maximum_fusion.6.kv_ref, s32[1,896]{1,0:T(1,128)S(1)} %slice_bitcast_fusion.4.qid_ref, s32[1792,1]{1,0:T(8,128)S(1)} %copy-done.3), custom_call_target="tpu_custom_call" | custom-call | flops 17263755264 | bytes 4816896 | tf_op jit(solution)/shard_map/attention_forward/pallas_call | solution.py:134
  276.7 8.9 %collective-permute-done.20 = bf16[224,192]{1,0:T(8,128)(2,1)} collective-permute-done((bf16[224,192]{1,0:T(8,128)(2,1)}, bf16[224,192]{1,0:T(8,128)(2,1)}, u32[]{:S(2)}, u32[]{:S(2)}) %collective-permute-start.20) | collective-permute-done | bytes 86048 | tf_op jit(solution)/shard_map/ppermute | solution.py:269
  285.7 5.5 collective-permute-done.18
  297.1 5.9 all-gather.8.cloned.1.call-done
  332.1 5.6 multiply_reduce_fusion.2
  361.8 18.4 %attention_backward.2 = (bf16[896,192]{1,0:T(8,128)(2,1)S(1)}, bf16[1792,384]{1,0:T(8,128)(2,1)S(1)}) custom-call(bf16[896,192]{1,0:T(8,128)(2,1)S(1)} %copy-done.11, bf16[1792,384]{1,0:T(8,128)(2,1)S(1)} %pad_maximum_fusion.6.kv_ref, s32[1,896]{1,0:T(1,128)S(1)} %slice_bitcast_fusion.4.qid_ref, s32[1792,1]{1,0:T(8,128)S(1)} %copy-done.4, ...), custom_call_target="tpu_custom_call" | custom-call | flops 20963131392 | bytes 4816896 | tf_op jit(solution)/shard_map/attention_backward/pallas_call | solution.py:165
  399.0 11.3 %collective-permute-done.28 = bf16[224,576]{1,0:T(8,128)(2,1)} collective-permute-done((bf16[224,576]{1,0:T(8,128)(2,1)}, bf16[224,576]{1,0:T(8,128)(2,1)}, u32[]{:S(2)}, u32[]{:S(2)}) %collective-permute-start.28) | collective-permute-done | bytes 258080 | tf_op jit(solution)/shard_map/ppermute | solution.py:269
  429.1 4.7 fusion.148
  456.0 5.4 multiply_reduce_fusion
  482.0 18.8 %attention_backward.3 = (bf16[896,192]{1,0:T(8,128)(2,1)S(1)}, bf16[1792,384]{1,0:T(8,128)(2,1)S(1)}) custom-call(bf16[896,192]{1,0:T(8,128)(2,1)S(1)} %pad_maximum_fusion.18.q_ref, bf16[1792,384]{1,0:T(8,128)(2,1)S(1)} %pad_maximum_fusion.5.kv_ref, s32[1,896]{1,0:T(1,128)S(1)} %slice_bitcast_fusion.4.qid_ref, s32[1792,1]{1,0:T(8,128)S(1)} %copy-done.5, ...), custom_call_target="tpu_custom_call" | custom-call | flops 20963131392 | bytes 4816896 | tf_op jit(solution)/shard_map/attention_backward/pallas_call | solution.py:165
  500.8 18.8 %collective-permute-done.33 = bf16[1,4,48,3200]{3,2,1,0:T(8,128)(2,1)S(1)} collective-permute-done((bf16[1,4,48,3200]{3,2,1,0:T(8,128)(2,1)S(1)}, bf16[1,4,48,3200]{3,2,1,0:T(8,128)(2,1)S(1)}, u32[]{:S(2)}, u32[]{:S(2)}) %collective-permute-start.33) | collective-permute-done | bytes 1228832 | tf_op jit(solution)/shard_map/ppermute | solution.py:286
  534.2 8.9 %collective-permute-done.37 = bf16[224,576]{1,0:T(8,128)(2,1)S(1)} collective-permute-done((bf16[224,576]{1,0:T(8,128)(2,1)}, bf16[224,576]{1,0:T(8,128)(2,1)S(1)}, u32[]{:S(2)}, u32[]{:S(2)}) %collective-permute-start.37) | collective-permute-done | bytes 258080 | tf_op jit(solution)/shard_map/ppermute | solution.py:269
  543.1 7.7 %collective-permute-done.36 = bf16[224,576]{1,0:T(8,128)(2,1)} collective-permute-done((bf16[224,576]{1,0:T(8,128)(2,1)S(1)}, bf16[224,576]{1,0:T(8,128)(2,1)}, u32[]{:S(2)}, u32[]{:S(2)}) %collective-permute-start.36) | collective-permute-done | bytes 258080 | tf_op jit(solution)/shard_map/ppermute | solution.py:269
  566.4 21.1 %collective-permute-done.40 = bf16[112,768]{1,0:T(8,128)(2,1)} collective-permute-done((bf16[112,768]{1,0:T(8,128)(2,1)}, bf16[112,768]{1,0:T(8,128)(2,1)}, u32[]{:S(2)}, u32[]{:S(2)}) %collective-permute-start.40) | collective-permute-done | bytes 172064 | tf_op jit(solution)/shard_map/ppermute | solution.py:261
  587.4 9.8 %collective-permute-done.41 = bf16[112,768]{1,0:T(8,128)(2,1)} collective-permute-done((bf16[112,768]{1,0:T(8,128)(2,1)}, bf16[112,768]{1,0:T(8,128)(2,1)}, u32[]{:S(2)}, u32[]{:S(2)}) %collective-permute-start.41) | collective-permute-done | bytes 172064 | tf_op jit(solution)/shard_map/ppermute | solution.py:261
  601.1 8.5 %collective-permute-done.42 = bf16[112,768]{1,0:T(8,128)(2,1)S(1)} collective-permute-done((bf16[112,768]{1,0:T(8,128)(2,1)S(1)}, bf16[112,768]{1,0:T(8,128)(2,1)S(1)}, u32[]{:S(2)}, u32[]{:S(2)}) %collective-permute-start.42) | collective-permute-done | bytes 172064 | tf_op jit(solution)/shard_map/ppermute | solution.py:261
  618.7 17.3 %collective-permute-done.45 = bf16[112,768]{1,0:T(8,128)(2,1)S(1)} collective-permute-done((bf16[112,768]{1,0:T(8,128)(2,1)S(1)}, bf16[112,768]{1,0:T(8,128)(2,1)S(1)}, u32[]{:S(2)}, u32[]{:S(2)}) %collective-permute-start.45) | collective-permute-done | bytes 172064 | tf_op jit(solution)/shard_map/ppermute | solution.py:261
  637.4 4.6 collective-permute-start.51
  643.3 4.6 collective-permute-start.44
  (596 shorter events, 316.2 us)
Async XLA Ops:
  7.2 85.2 %all-gather.4.cloned.1.call-start = ((), (), s32[]{:S(2)}) async-start(), calls=%async_computation.3 | async-start | bytes 7704576 | tf_op jit(solution)/shard_map/all_gather | solution.py:391
  13.3 183.0 %all-gather.6.cloned.1.call-start = ((), (), s32[]{:S(2)}) async-start(), calls=%async_computation.4 | async-start | bytes 11280384 | tf_op jit(solution)/shard_map/all_gather | solution.py:393
  15.9 19.6 %collective-permute-start.13 = (bf16[48,6912]{1,0:T(8,128)(2,1)S(1)}, bf16[48,6912]{1,0:T(8,128)(2,1)S(1)}, u32[]{:S(2)}, u32[]{:S(2)}) collective-permute-start(bf16[48,6912]{1,0:T(8,128)(2,1)S(1)} %bitcast_dynamic-update-slice_fusion), channel_id=1, source_target_pairs={{0,16},{16,0},{1,17},{17,1},{2,18},{18,2},{3,19},{19,3},{4,20},{20... | collective-permute-start | bytes 1990664 | tf_op jit(solution)/shard_map/ppermute | solution.py:258
  36.6 266.4 %all-gather.8.cloned.1.call-start = ((), (), s32[]{:S(2)}) async-start(), calls=%async_computation.5 | async-start | bytes 11280384 | tf_op jit(solution)/shard_map/all_gather | solution.py:396
  37.4 418.5 %reduce-scatter.4.cloned.1.call-start = ((), (), s32[]{:S(2)}) async-start(), calls=%async_computation.6 | async-start | bytes 10027008 | tf_op jit(solution)/shard_map/reduce_scatter | solution.py:502
  37.7 61.0 %collective-permute-start = (bf16[112,768]{1,0:T(8,128)(2,1)S(1)}, bf16[112,768]{1,0:T(8,128)(2,1)S(1)}, u32[]{:S(2)}, u32[]{:S(2)}) collective-permute-start(bf16[112,768]{1,0:T(8,128)(2,1)S(1)} %get-tuple-element.209), channel_id=1, source_target_pairs={{0,2},{1,3},{2,0},{3,1},{4,6},{5,7},{6,4},{7,5},{8,10},{9,11},{10,... | collective-permute-start | bytes 516104 | tf_op jit(solution)/shard_map/ppermute | solution.py:261
  106.4 23.7 %collective-permute-start.3 = (bf16[224,576]{1,0:T(8,128)(2,1)S(1)}, bf16[224,576]{1,0:T(8,128)(2,1)S(1)}, u32[]{:S(2)}, u32[]{:S(2)}) collective-permute-start(bf16[224,576]{1,0:T(8,128)(2,1)S(1)} %bitcast.314), channel_id=1, source_target_pairs={{0,9},{1,8},{2,11},{3,10},{4,13},{5,12},{6,15},{7,14},{8,1},{9,0},... | collective-permute-start | bytes 774152 | tf_op jit(solution)/shard_map/ppermute | solution.py:269
  108.7 21.3 %collective-permute-start.2 = (bf16[224,576]{1,0:T(8,128)(2,1)S(1)}, bf16[224,576]{1,0:T(8,128)(2,1)S(1)}, u32[]{:S(2)}, u32[]{:S(2)}) collective-permute-start(bf16[224,576]{1,0:T(8,128)(2,1)S(1)} %bitcast.316), channel_id=1, source_target_pairs={{0,8},{1,9},{2,10},{3,11},{4,12},{5,13},{6,14},{7,15},{8,0},{9,1},... | collective-permute-start | bytes 774152 | tf_op jit(solution)/shard_map/ppermute | solution.py:269
  109.5 29.2 %collective-permute-start.1 = (bf16[224,576]{1,0:T(8,128)(2,1)S(1)}, bf16[224,576]{1,0:T(8,128)(2,1)S(1)}, u32[]{:S(2)}, u32[]{:S(2)}) collective-permute-start(bf16[224,576]{1,0:T(8,128)(2,1)S(1)} %bitcast.318), channel_id=1, source_target_pairs={{0,1},{1,0},{2,3},{3,2},{4,5},{5,4},{6,7},{7,6},{8,9},{9,8},{10,11... | collective-permute-start | bytes 774152 | tf_op jit(solution)/shard_map/ppermute | solution.py:269
  138.8 13.8 %collective-permute-start.4 = (bf16[896,384]{1,0:T(8,128)(2,1)S(1)}, bf16[896,384]{1,0:T(8,128)(2,1)}, u32[]{:S(2)}, u32[]{:S(2)}) collective-permute-start(bf16[896,384]{1,0:T(8,128)(2,1)S(1)} %pad_maximum_fusion.12), channel_id=1, source_target_pairs={{0,4},{4,0},{8,12},{12,8},{1,5},{5,1},{9,13},{13,9},{2,6},{6,2},{1... | collective-permute-start | bytes 2064392 | tf_op jit(solution)/shard_map/ppermute | solution.py:272
  225.3 13.3 %collective-permute-start.16 = (bf16[224,576]{1,0:T(8,128)(2,1)S(1)}, bf16[224,576]{1,0:T(8,128)(2,1)S(1)}, u32[]{:S(2)}, u32[]{:S(2)}) collective-permute-start(bf16[224,576]{1,0:T(8,128)(2,1)S(1)} %bitcast.315), channel_id=1, source_target_pairs={{0,9},{1,8},{2,11},{3,10},{4,13},{5,12},{6,15},{7,14},{8,1},{9,0},... | collective-permute-start | bytes 774152 | tf_op jit(solution)/shard_map/ppermute | solution.py:269
  228.2 15.7 %collective-permute-start.15 = (bf16[224,576]{1,0:T(8,128)(2,1)S(1)}, bf16[224,576]{1,0:T(8,128)(2,1)S(1)}, u32[]{:S(2)}, u32[]{:S(2)}) collective-permute-start(bf16[224,576]{1,0:T(8,128)(2,1)S(1)} %bitcast.317), channel_id=1, source_target_pairs={{0,8},{1,9},{2,10},{3,11},{4,12},{5,13},{6,14},{7,15},{8,0},{9,1},... | collective-permute-start | bytes 774152 | tf_op jit(solution)/shard_map/ppermute | solution.py:269
  228.8 20.5 %collective-permute-start.14 = (bf16[224,576]{1,0:T(8,128)(2,1)S(1)}, bf16[224,576]{1,0:T(8,128)(2,1)S(1)}, u32[]{:S(2)}, u32[]{:S(2)}) collective-permute-start(bf16[224,576]{1,0:T(8,128)(2,1)S(1)} %bitcast.319), channel_id=1, source_target_pairs={{0,1},{1,0},{2,3},{3,2},{4,5},{5,4},{6,7},{7,6},{8,9},{9,8},{10,11... | collective-permute-start | bytes 774152 | tf_op jit(solution)/shard_map/ppermute | solution.py:269
  268.6 17.0 %collective-permute-start.20 = (bf16[224,192]{1,0:T(8,128)(2,1)}, bf16[224,192]{1,0:T(8,128)(2,1)}, u32[]{:S(2)}, u32[]{:S(2)}) collective-permute-start(bf16[224,192]{1,0:T(8,128)(2,1)} %get-tuple-element.221), channel_id=1, source_target_pairs={{0,9},{1,8},{2,11},{3,10},{4,13},{5,12},{6,15},{7,14},{8,1},{9,0},... | collective-permute-start | bytes 258056 | tf_op jit(solution)/shard_map/ppermute | solution.py:269
  268.6 17.0 %collective-permute-start.19 = (bf16[224,192]{1,0:T(8,128)(2,1)}, bf16[224,192]{1,0:T(8,128)(2,1)}, u32[]{:S(2)}, u32[]{:S(2)}) collective-permute-start(bf16[224,192]{1,0:T(8,128)(2,1)} %get-tuple-element.222), channel_id=1, source_target_pairs={{0,8},{1,9},{2,10},{3,11},{4,12},{5,13},{6,14},{7,15},{8,0},{9,1},... | collective-permute-start | bytes 258056 | tf_op jit(solution)/shard_map/ppermute | solution.py:269
  270.5 20.6 %collective-permute-start.18 = (bf16[224,192]{1,0:T(8,128)(2,1)S(1)}, bf16[224,192]{1,0:T(8,128)(2,1)}, u32[]{:S(2)}, u32[]{:S(2)}) collective-permute-start(bf16[224,192]{1,0:T(8,128)(2,1)S(1)} %get-tuple-element.223), channel_id=1, source_target_pairs={{0,1},{1,0},{2,3},{3,2},{4,5},{5,4},{6,7},{7,6},{8,9},{9,8},{10,11... | collective-permute-start | bytes 258056 | tf_op jit(solution)/shard_map/ppermute | solution.py:269
  273.6 39.5 %collective-permute-start.21 = (f32[112,768]{1,0:T(8,128)}, f32[112,768]{1,0:T(8,128)}, u32[]{:S(2)}, u32[]{:S(2)}) collective-permute-start(f32[112,768]{1,0:T(8,128)} %get-tuple-element.169), channel_id=1, source_target_pairs={{0,2},{1,3},{2,0},{3,1},{4,6},{5,7},{6,4},{7,5},{8,10},{9,11},{10,... | collective-permute-start | bytes 1032200 | tf_op jit(solution)/shard_map/ppermute | solution.py:261
  332.0 282.1 %reduce-scatter.6.cloned.1.call-start = ((), (), s32[]{:S(2)}) async-start(), calls=%async_computation.7 | async-start | bytes 10027008 | tf_op jit(solution)/shard_map/reduce_scatter | solution.py:502
  391.8 18.5 %collective-permute-start.28 = (bf16[224,576]{1,0:T(8,128)(2,1)}, bf16[224,576]{1,0:T(8,128)(2,1)}, u32[]{:S(2)}, u32[]{:S(2)}) collective-permute-start(bf16[224,576]{1,0:T(8,128)(2,1)} %get-tuple-element.191), channel_id=1, source_target_pairs={{0,9},{1,8},{2,11},{3,10},{4,13},{5,12},{6,15},{7,14},{8,1},{9,0},... | collective-permute-start | bytes 774152 | tf_op jit(solution)/shard_map/ppermute | solution.py:269
  393.3 20.8 %collective-permute-start.27 = (bf16[224,576]{1,0:T(8,128)(2,1)}, bf16[224,576]{1,0:T(8,128)(2,1)}, u32[]{:S(2)}, u32[]{:S(2)}) collective-permute-start(bf16[224,576]{1,0:T(8,128)(2,1)} %get-tuple-element.192), channel_id=1, source_target_pairs={{0,8},{1,9},{2,10},{3,11},{4,12},{5,13},{6,14},{7,15},{8,0},{9,1},... | collective-permute-start | bytes 774152 | tf_op jit(solution)/shard_map/ppermute | solution.py:269
  395.1 20.4 %collective-permute-start.26 = (bf16[224,576]{1,0:T(8,128)(2,1)}, bf16[224,576]{1,0:T(8,128)(2,1)}, u32[]{:S(2)}, u32[]{:S(2)}) collective-permute-start(bf16[224,576]{1,0:T(8,128)(2,1)} %get-tuple-element.190), channel_id=1, source_target_pairs={{0,1},{1,0},{2,3},{3,2},{4,5},{5,4},{6,7},{7,6},{8,9},{9,8},{10,11... | collective-permute-start | bytes 774152 | tf_op jit(solution)/shard_map/ppermute | solution.py:269
  428.5 47.3 %collective-permute-start.32 = (bf16[384,3200]{1,0:T(8,128)(2,1)}, bf16[384,3200]{1,0:T(8,128)(2,1)}, u32[]{:S(2)}, u32[]{:S(2)}) collective-permute-start(bf16[384,3200]{1,0:T(8,128)(2,1)} %pad_maximum_fusion.1), channel_id=1, source_target_pairs={{0,4},{4,0},{8,12},{12,8},{1,5},{5,1},{9,13},{13,9},{2,6},{6,2},{1... | collective-permute-start | bytes 7372808 | tf_op jit(solution)/shard_map/ppermute | solution.py:272
  455.9 210.6 %reduce-scatter.8.cloned.1.call-start = ((), (), s32[]{:S(2)}) async-start(), calls=%async_computation.8 | async-start | bytes 3072000 | tf_op jit(solution)/shard_map/reduce_scatter | solution.py:321
  478.0 41.6 %collective-permute-start.33 = (bf16[1,4,48,3200]{3,2,1,0:T(8,128)(2,1)S(1)}, bf16[1,4,48,3200]{3,2,1,0:T(8,128)(2,1)S(1)}, u32[]{:S(2)}, u32[]{:S(2)}) collective-permute-start(bf16[1,4,48,3200]{3,2,1,0:T(8,128)(2,1)S(1)} %fusion.55), channel_id=1, source_target_pairs={{0,8},{4,12},{8,0},{12,4},{1,9},{5,13},{9,1},{13,5},{2,10},{6,14},... | collective-permute-start | bytes 3686408 | tf_op jit(solution)/shard_map/ppermute | solution.py:286
  528.0 15.1 %collective-permute-start.37 = (bf16[224,576]{1,0:T(8,128)(2,1)}, bf16[224,576]{1,0:T(8,128)(2,1)S(1)}, u32[]{:S(2)}, u32[]{:S(2)}) collective-permute-start(bf16[224,576]{1,0:T(8,128)(2,1)} %get-tuple-element.183), channel_id=1, source_target_pairs={{0,9},{1,8},{2,11},{3,10},{4,13},{5,12},{6,15},{7,14},{8,1},{9,0},... | collective-permute-start | bytes 774152 | tf_op jit(solution)/shard_map/ppermute | solution.py:269
  529.7 21.1 %collective-permute-start.36 = (bf16[224,576]{1,0:T(8,128)(2,1)S(1)}, bf16[224,576]{1,0:T(8,128)(2,1)}, u32[]{:S(2)}, u32[]{:S(2)}) collective-permute-start(bf16[224,576]{1,0:T(8,128)(2,1)S(1)} %get-tuple-element.184), channel_id=1, source_target_pairs={{0,8},{1,9},{2,10},{3,11},{4,12},{5,13},{6,14},{7,15},{8,0},{9,1},... | collective-permute-start | bytes 774152 | tf_op jit(solution)/shard_map/ppermute | solution.py:269
  530.0 20.8 %collective-permute-start.35 = (bf16[224,576]{1,0:T(8,128)(2,1)S(1)}, bf16[224,576]{1,0:T(8,128)(2,1)}, u32[]{:S(2)}, u32[]{:S(2)}) collective-permute-start(bf16[224,576]{1,0:T(8,128)(2,1)S(1)} %get-tuple-element.182), channel_id=1, source_target_pairs={{0,1},{1,0},{2,3},{3,2},{4,5},{5,4},{6,7},{7,6},{8,9},{9,8},{10,11... | collective-permute-start | bytes 774152 | tf_op jit(solution)/shard_map/ppermute | solution.py:269
  561.6 49.0 %collective-permute-start.39 = (bf16[1,4,48,3200]{3,2,1,0:T(8,128)(2,1)}, bf16[1,4,48,3200]{3,2,1,0:T(8,128)(2,1)}, u32[]{:S(2)}, u32[]{:S(2)}) collective-permute-start(bf16[1,4,48,3200]{3,2,1,0:T(8,128)(2,1)} %fusion.56), channel_id=1, source_target_pairs={{0,8},{4,12},{8,0},{12,4},{1,9},{5,13},{9,1},{13,5},{2,10},{6,14},... | collective-permute-start | bytes 3686408 | tf_op jit(solution)/shard_map/ppermute | solution.py:286
  562.7 24.7 %collective-permute-start.40 = (bf16[112,768]{1,0:T(8,128)(2,1)}, bf16[112,768]{1,0:T(8,128)(2,1)}, u32[]{:S(2)}, u32[]{:S(2)}) collective-permute-start(bf16[112,768]{1,0:T(8,128)(2,1)} %slice.624), channel_id=1, source_target_pairs={{0,2},{1,3},{2,0},{3,1},{4,6},{5,7},{6,4},{7,5},{8,10},{9,11},{10,... | collective-permute-start | bytes 516104 | tf_op jit(solution)/shard_map/ppermute | solution.py:261
  565.4 31.8 %collective-permute-start.41 = (bf16[112,768]{1,0:T(8,128)(2,1)}, bf16[112,768]{1,0:T(8,128)(2,1)}, u32[]{:S(2)}, u32[]{:S(2)}) collective-permute-start(bf16[112,768]{1,0:T(8,128)(2,1)} %slice.627), channel_id=1, source_target_pairs={{0,2},{1,3},{2,0},{3,1},{4,6},{5,7},{6,4},{7,5},{8,10},{9,11},{10,... | collective-permute-start | bytes 516104 | tf_op jit(solution)/shard_map/ppermute | solution.py:261
  618.6 17.4 %collective-permute-start.45 = (bf16[112,768]{1,0:T(8,128)(2,1)S(1)}, bf16[112,768]{1,0:T(8,128)(2,1)S(1)}, u32[]{:S(2)}, u32[]{:S(2)}) collective-permute-start(bf16[112,768]{1,0:T(8,128)(2,1)S(1)} %slice.895), channel_id=1, source_target_pairs={{0,2},{1,3},{2,0},{3,1},{4,6},{5,7},{6,4},{7,5},{8,10},{9,11},{10,... | collective-permute-start | bytes 516104 | tf_op jit(solution)/shard_map/ppermute | solution.py:261
  637.4 20.6 %collective-permute-start.51 = (bf16[48,6144]{1,0:T(8,128)(2,1)S(1)}, bf16[48,6144]{1,0:T(8,128)(2,1)S(1)}, u32[]{:S(2)}, u32[]{:S(2)}) collective-permute-start(bf16[48,6144]{1,0:T(8,128)(2,1)S(1)} %copy-done.63), channel_id=1, source_target_pairs={{0,16},{1,17},{2,18},{3,19},{4,20},{5,21},{6,22},{7,23},{8,24},{9,... | collective-permute-start | bytes 1769480 | tf_op jit(solution)/shard_map/ppermute | solution.py:610
  (137 other events, 1376.5 us)
Sparse Core Ops, SparseCore 0:
  13.4 78.9 all-gather.3
  95.3 101.0 all-gather.5
  198.6 104.3 all-gather.7
  332.1 121.9 reduce-scatter.3
  458.6 142.9 reduce-scatter.5
  614.3 49.1 reduce-scatter.7

commit v6 on v5

--- a/solution.py
+++ b/solution.py
@@ -618,7 +618,8 @@
         both = line_sum(last_sides)
         last_sums = [both[:, : both.shape[1] // 2], both[:, both.shape[1] // 2 :]]
     wide = settle(wide_sums[0], wide_sums[1])
-    last = settle(last_sums[0], last_sums[1])
+    last_other = across_section(jnp.where(first_section, last_sums[1], last_sums[0]))
+    last = jnp.where(first_section, last_sums[0], last_sums[1]).astype(F32) + last_other.astype(F32)
     grad_up = (
         wide[:, :hidden_width]
         .reshape(shard, chunks, head_count * blk_count, shard)

time: 710 us -> 707 us (level)
    ppermute x1 -> x2, waiting for transfers between devices: 16.6 us -> 22.5 us  [across_section(): return lax.ppermute(value, 'section', [(0, 1), (1, 0)])]
  transfers between devices with their start and end apart: 58 -> 57, of which waited for: 41 -> 40; matrix products, arithmetic and copies ran while one was open for 28% -> 28% of each run, Pallas kernels for 10% -> 10%
where the time goes in v6:
time: 707 us; the launch traced here: 693 us
  waiting for transfers between devices  299 us (42%)
  local copies, waits for them, and re-layouts  96.5 us (14%)
  matrix products  90.2 us (13%)
  Pallas kernels  67 us (9%)
  other arithmetic  65 us (9%)
  starting transfers between devices  59 us (8%)
  between operations  16.5 us (2%)
    ppermute x27, waiting for transfers between devices, across_member(): return lax.ppermute(value, GROUP, pairs)  114 us
    dot_general x46, matrix products, dot(): return lax.dot_general(left, right, dims, preferred_element_type=F32)  90.2 us
    ppermute x7, waiting for transfers between devices, across_half(): lax.ppermute(value, 'blk', [(at, (at + half) % blk_count) for at in range...  60.6 us
    all_gather x1, waiting for transfers between devices, body(): lax.all_gather(first_local, ('section',) + GROUP, axis=0, tiled=True)  51.8 us
    pallas_call x2, Pallas kernels, attention_backward(): pl.pallas_call(attention_backward_kernel, grid=(count // block,), in_spec...  37.1 us
    ppermute x27, starting transfers between devices, across_member(): return lax.ppermute(value, GROUP, pairs)  31.9 us
    pallas_call x2, Pallas kernels, attention_forward(): pl.pallas_call(attention_forward_kernel, grid=(count // block,), in_specs...  29.9 us
    unnamed x248, local copies, waits for them, and re-layouts  23.9 us
  transfers between devices with their start and end apart: 57, of which 40 were waited for; matrix products, arithmetic and copies ran while one was open for 28% of the time, Pallas kernels for 10%

profile of v6, /device:TPU:0, one launch (start us, length us, event | category | flops | bytes accessed | tf_op | source)
XLA Modules:
  0.0 693.0 jit_solution(13342445553170400816)
XLA Ops:
  18.9 16.6 %collective-permute-done.13 = bf16[48,6912]{1,0:T(8,128)(2,1)S(1)} collective-permute-done((bf16[48,6912]{1,0:T(8,128)(2,1)S(1)}, bf16[48,6912]{1,0:T(8,128)(2,1)S(1)}, u32[]{:S(2)}, u32[]{:S(2)}) %collective-permute-start.13) | collective-permute-done | bytes 663584 | tf_op jit(solution)/shard_map/ppermute | solution.py:258
  40.6 51.8 %all-gather.4.cloned.1.call-done = bf16[1536,2432]{1,0:T(8,128)(2,1)} async-done(((bf16[48,2432]{1,0:T(8,128)(2,1)}), bf16[1536,2432]{1,0:T(8,128)(2,1)}) %all-gather.4.cloned.1.call-update) | async-done | bytes 7471120 | tf_op jit(solution)/shard_map/all_gather | solution.py:391
  110.2 19.9 %collective-permute-done.3 = bf16[224,576]{1,0:T(8,128)(2,1)S(1)} collective-permute-done((bf16[224,576]{1,0:T(8,128)(2,1)S(1)}, bf16[224,576]{1,0:T(8,128)(2,1)S(1)}, u32[]{:S(2)}, u32[]{:S(2)}) %collective-permute-start.3) | collective-permute-done | bytes 258080 | tf_op jit(solution)/shard_map/ppermute | solution.py:269
  130.1 8.6 %collective-permute-done.1 = bf16[224,576]{1,0:T(8,128)(2,1)S(1)} collective-permute-done((bf16[224,576]{1,0:T(8,128)(2,1)S(1)}, bf16[224,576]{1,0:T(8,128)(2,1)S(1)}, u32[]{:S(2)}, u32[]{:S(2)}) %collective-permute-start.1) | collective-permute-done | bytes 258080 | tf_op jit(solution)/shard_map/ppermute | solution.py:269
  154.0 14.9 %attention_forward.2 = (f32[896,192]{1,0:T(8,128)S(1)}, f32[8,896]{1,0:T(8,128)S(1)}) custom-call(bf16[896,192]{1,0:T(8,128)(2,1)S(1)} %pad_maximum_fusion.18.q_ref, bf16[1792,384]{1,0:T(8,128)(2,1)S(1)} %pad_maximum_fusion.5.kv_ref, s32[1,896]{1,0:T(1,128)S(1)} %slice_bitcast_fusion.4.qid_ref, s32[1792,1]{1,0:T(8,128)S(1)} %copy.244.mark_ref), custom_call_target="tpu_custom_call" | custom-call | flops 17263755264 | bytes 4816896 | tf_op jit(solution)/shard_map/attention_forward/pallas_call | solution.py:134
  174.5 5.7 collective-permute-done.12
  180.2 6.1 collective-permute-done.10
  187.9 8.5 %all-gather.6.cloned.1.call-done = bf16[768,6912]{1,0:T(8,128)(2,1)} async-done(((bf16[48,6912]{1,0:T(8,128)(2,1)}), bf16[768,6912]{1,0:T(8,128)(2,1)}) %all-gather.6.cloned.1.call-update) | async-done | bytes 10616848 | tf_op jit(solution)/shard_map/all_gather | solution.py:393
  198.5 5.6 multiply_convert_fusion.1
  220.3 5.0 constant_dynamic-slice_fusion.17
  229.2 9.5 %collective-permute-done.16 = bf16[224,576]{1,0:T(8,128)(2,1)S(1)} collective-permute-done((bf16[224,576]{1,0:T(8,128)(2,1)S(1)}, bf16[224,576]{1,0:T(8,128)(2,1)S(1)}, u32[]{:S(2)}, u32[]{:S(2)}) %collective-permute-start.16) | collective-permute-done | bytes 258080 | tf_op jit(solution)/shard_map/ppermute | solution.py:269
  238.7 5.2 collective-permute-done.15
  243.9 5.5 collective-permute-done.14
  251.8 15.0 %attention_forward.3 = (f32[896,192]{1,0:T(8,128)S(1)}, f32[8,896]{1,0:T(8,128)S(1)}) custom-call(bf16[896,192]{1,0:T(8,128)(2,1)S(1)} %pad_maximum_fusion.17.q_ref, bf16[1792,384]{1,0:T(8,128)(2,1)S(1)} %pad_maximum_fusion.6.kv_ref, s32[1,896]{1,0:T(1,128)S(1)} %slice_bitcast_fusion.4.qid_ref, s32[1792,1]{1,0:T(8,128)S(1)} %copy-done.3), custom_call_target="tpu_custom_call" | custom-call | flops 17263755264 | bytes 4816896 | tf_op jit(solution)/shard_map/attention_forward/pallas_call | solution.py:134
  276.8 8.9 %collective-permute-done.20 = bf16[224,192]{1,0:T(8,128)(2,1)} collective-permute-done((bf16[224,192]{1,0:T(8,128)(2,1)}, bf16[224,192]{1,0:T(8,128)(2,1)}, u32[]{:S(2)}, u32[]{:S(2)}) %collective-permute-start.20) | collective-permute-done | bytes 86048 | tf_op jit(solution)/shard_map/ppermute | solution.py:269
  285.7 5.5 collective-permute-done.18
  297.1 5.9 all-gather.8.cloned.1.call-done
  332.1 5.6 multiply_reduce_fusion.2
  361.8 18.4 %attention_backward.2 = (bf16[896,192]{1,0:T(8,128)(2,1)S(1)}, bf16[1792,384]{1,0:T(8,128)(2,1)S(1)}) custom-call(bf16[896,192]{1,0:T(8,128)(2,1)S(1)} %copy-done.11, bf16[1792,384]{1,0:T(8,128)(2,1)S(1)} %pad_maximum_fusion.6.kv_ref, s32[1,896]{1,0:T(1,128)S(1)} %slice_bitcast_fusion.4.qid_ref, s32[1792,1]{1,0:T(8,128)S(1)} %copy-done.4, ...), custom_call_target="tpu_custom_call" | custom-call | flops 20963131392 | bytes 4816896 | tf_op jit(solution)/shard_map/attention_backward/pallas_call | solution.py:165
  399.1 11.2 %collective-permute-done.28 = bf16[224,576]{1,0:T(8,128)(2,1)} collective-permute-done((bf16[224,576]{1,0:T(8,128)(2,1)}, bf16[224,576]{1,0:T(8,128)(2,1)}, u32[]{:S(2)}, u32[]{:S(2)}) %collective-permute-start.28) | collective-permute-done | bytes 258080 | tf_op jit(solution)/shard_map/ppermute | solution.py:269
  429.1 4.7 fusion.148
  456.1 5.4 multiply_reduce_fusion
  482.1 18.8 %attention_backward.3 = (bf16[896,192]{1,0:T(8,128)(2,1)S(1)}, bf16[1792,384]{1,0:T(8,128)(2,1)S(1)}) custom-call(bf16[896,192]{1,0:T(8,128)(2,1)S(1)} %pad_maximum_fusion.18.q_ref, bf16[1792,384]{1,0:T(8,128)(2,1)S(1)} %pad_maximum_fusion.5.kv_ref, s32[1,896]{1,0:T(1,128)S(1)} %slice_bitcast_fusion.4.qid_ref, s32[1792,1]{1,0:T(8,128)S(1)} %copy-done.5, ...), custom_call_target="tpu_custom_call" | custom-call | flops 20963131392 | bytes 4816896 | tf_op jit(solution)/shard_map/attention_backward/pallas_call | solution.py:165
  500.9 19.0 %collective-permute-done.33 = bf16[1,4,48,3200]{3,2,1,0:T(8,128)(2,1)S(1)} collective-permute-done((bf16[1,4,48,3200]{3,2,1,0:T(8,128)(2,1)S(1)}, bf16[1,4,48,3200]{3,2,1,0:T(8,128)(2,1)S(1)}, u32[]{:S(2)}, u32[]{:S(2)}) %collective-permute-start.33) | collective-permute-done | bytes 1228832 | tf_op jit(solution)/shard_map/ppermute | solution.py:286
  534.4 8.8 %collective-permute-done.37 = bf16[224,576]{1,0:T(8,128)(2,1)S(1)} collective-permute-done((bf16[224,576]{1,0:T(8,128)(2,1)}, bf16[224,576]{1,0:T(8,128)(2,1)S(1)}, u32[]{:S(2)}, u32[]{:S(2)}) %collective-permute-start.37) | collective-permute-done | bytes 258080 | tf_op jit(solution)/shard_map/ppermute | solution.py:269
  543.2 7.9 %collective-permute-done.36 = bf16[224,576]{1,0:T(8,128)(2,1)} collective-permute-done((bf16[224,576]{1,0:T(8,128)(2,1)S(1)}, bf16[224,576]{1,0:T(8,128)(2,1)}, u32[]{:S(2)}, u32[]{:S(2)}) %collective-permute-start.36) | collective-permute-done | bytes 258080 | tf_op jit(solution)/shard_map/ppermute | solution.py:269
  566.5 21.4 %collective-permute-done.40 = bf16[112,768]{1,0:T(8,128)(2,1)} collective-permute-done((bf16[112,768]{1,0:T(8,128)(2,1)}, bf16[112,768]{1,0:T(8,128)(2,1)}, u32[]{:S(2)}, u32[]{:S(2)}) %collective-permute-start.40) | collective-permute-done | bytes 172064 | tf_op jit(solution)/shard_map/ppermute | solution.py:261
  587.9 9.4 %collective-permute-done.41 = bf16[112,768]{1,0:T(8,128)(2,1)} collective-permute-done((bf16[112,768]{1,0:T(8,128)(2,1)}, bf16[112,768]{1,0:T(8,128)(2,1)}, u32[]{:S(2)}, u32[]{:S(2)}) %collective-permute-start.41) | collective-permute-done | bytes 172064 | tf_op jit(solution)/shard_map/ppermute | solution.py:261
  601.3 8.5 %collective-permute-done.42 = bf16[112,768]{1,0:T(8,128)(2,1)S(1)} collective-permute-done((bf16[112,768]{1,0:T(8,128)(2,1)S(1)}, bf16[112,768]{1,0:T(8,128)(2,1)S(1)}, u32[]{:S(2)}, u32[]{:S(2)}) %collective-permute-start.42) | collective-permute-done | bytes 172064 | tf_op jit(solution)/shard_map/ppermute | solution.py:261
  618.8 17.3 %collective-permute-done.45 = bf16[112,768]{1,0:T(8,128)(2,1)S(1)} collective-permute-done((bf16[112,768]{1,0:T(8,128)(2,1)S(1)}, bf16[112,768]{1,0:T(8,128)(2,1)S(1)}, u32[]{:S(2)}, u32[]{:S(2)}) %collective-permute-start.45) | collective-permute-done | bytes 172064 | tf_op jit(solution)/shard_map/ppermute | solution.py:261
  637.5 4.6 collective-permute-start.50
  668.9 5.9 collective-permute-done.48
  (594 shorter events, 311.5 us)
Async XLA Ops:
  7.2 85.2 %all-gather.4.cloned.1.call-start = ((), (), s32[]{:S(2)}) async-start(), calls=%async_computation.3 | async-start | bytes 7704576 | tf_op jit(solution)/shard_map/all_gather | solution.py:391
  13.3 183.0 %all-gather.6.cloned.1.call-start = ((), (), s32[]{:S(2)}) async-start(), calls=%async_computation.4 | async-start | bytes 11280384 | tf_op jit(solution)/shard_map/all_gather | solution.py:393
  15.9 19.6 %collective-permute-start.13 = (bf16[48,6912]{1,0:T(8,128)(2,1)S(1)}, bf16[48,6912]{1,0:T(8,128)(2,1)S(1)}, u32[]{:S(2)}, u32[]{:S(2)}) collective-permute-start(bf16[48,6912]{1,0:T(8,128)(2,1)S(1)} %bitcast_dynamic-update-slice_fusion), channel_id=1, source_target_pairs={{0,16},{16,0},{1,17},{17,1},{2,18},{18,2},{3,19},{19,3},{4,20},{20... | collective-permute-start | bytes 1990664 | tf_op jit(solution)/shard_map/ppermute | solution.py:258
  36.7 266.4 %all-gather.8.cloned.1.call-start = ((), (), s32[]{:S(2)}) async-start(), calls=%async_computation.5 | async-start | bytes 11280384 | tf_op jit(solution)/shard_map/all_gather | solution.py:396
  37.4 418.7 %reduce-scatter.4.cloned.1.call-start = ((), (), s32[]{:S(2)}) async-start(), calls=%async_computation.6 | async-start | bytes 10027008 | tf_op jit(solution)/shard_map/reduce_scatter | solution.py:502
  37.7 61.0 %collective-permute-start = (bf16[112,768]{1,0:T(8,128)(2,1)S(1)}, bf16[112,768]{1,0:T(8,128)(2,1)S(1)}, u32[]{:S(2)}, u32[]{:S(2)}) collective-permute-start(bf16[112,768]{1,0:T(8,128)(2,1)S(1)} %get-tuple-element.209), channel_id=1, source_target_pairs={{0,2},{1,3},{2,0},{3,1},{4,6},{5,7},{6,4},{7,5},{8,10},{9,11},{10,... | collective-permute-start | bytes 516104 | tf_op jit(solution)/shard_map/ppermute | solution.py:261
  106.4 23.7 %collective-permute-start.3 = (bf16[224,576]{1,0:T(8,128)(2,1)S(1)}, bf16[224,576]{1,0:T(8,128)(2,1)S(1)}, u32[]{:S(2)}, u32[]{:S(2)}) collective-permute-start(bf16[224,576]{1,0:T(8,128)(2,1)S(1)} %bitcast.314), channel_id=1, source_target_pairs={{0,9},{1,8},{2,11},{3,10},{4,13},{5,12},{6,15},{7,14},{8,1},{9,0},... | collective-permute-start | bytes 774152 | tf_op jit(solution)/shard_map/ppermute | solution.py:269
  108.7 21.3 %collective-permute-start.2 = (bf16[224,576]{1,0:T(8,128)(2,1)S(1)}, bf16[224,576]{1,0:T(8,128)(2,1)S(1)}, u32[]{:S(2)}, u32[]{:S(2)}) collective-permute-start(bf16[224,576]{1,0:T(8,128)(2,1)S(1)} %bitcast.316), channel_id=1, source_target_pairs={{0,8},{1,9},{2,10},{3,11},{4,12},{5,13},{6,14},{7,15},{8,0},{9,1},... | collective-permute-start | bytes 774152 | tf_op jit(solution)/shard_map/ppermute | solution.py:269
  109.5 29.2 %collective-permute-start.1 = (bf16[224,576]{1,0:T(8,128)(2,1)S(1)}, bf16[224,576]{1,0:T(8,128)(2,1)S(1)}, u32[]{:S(2)}, u32[]{:S(2)}) collective-permute-start(bf16[224,576]{1,0:T(8,128)(2,1)S(1)} %bitcast.318), channel_id=1, source_target_pairs={{0,1},{1,0},{2,3},{3,2},{4,5},{5,4},{6,7},{7,6},{8,9},{9,8},{10,11... | collective-permute-start | bytes 774152 | tf_op jit(solution)/shard_map/ppermute | solution.py:269
  138.8 13.8 %collective-permute-start.4 = (bf16[896,384]{1,0:T(8,128)(2,1)S(1)}, bf16[896,384]{1,0:T(8,128)(2,1)}, u32[]{:S(2)}, u32[]{:S(2)}) collective-permute-start(bf16[896,384]{1,0:T(8,128)(2,1)S(1)} %pad_maximum_fusion.12), channel_id=1, source_target_pairs={{0,4},{4,0},{8,12},{12,8},{1,5},{5,1},{9,13},{13,9},{2,6},{6,2},{1... | collective-permute-start | bytes 2064392 | tf_op jit(solution)/shard_map/ppermute | solution.py:272
  225.4 13.3 %collective-permute-start.16 = (bf16[224,576]{1,0:T(8,128)(2,1)S(1)}, bf16[224,576]{1,0:T(8,128)(2,1)S(1)}, u32[]{:S(2)}, u32[]{:S(2)}) collective-permute-start(bf16[224,576]{1,0:T(8,128)(2,1)S(1)} %bitcast.315), channel_id=1, source_target_pairs={{0,9},{1,8},{2,11},{3,10},{4,13},{5,12},{6,15},{7,14},{8,1},{9,0},... | collective-permute-start | bytes 774152 | tf_op jit(solution)/shard_map/ppermute | solution.py:269
  228.2 15.7 %collective-permute-start.15 = (bf16[224,576]{1,0:T(8,128)(2,1)S(1)}, bf16[224,576]{1,0:T(8,128)(2,1)S(1)}, u32[]{:S(2)}, u32[]{:S(2)}) collective-permute-start(bf16[224,576]{1,0:T(8,128)(2,1)S(1)} %bitcast.317), channel_id=1, source_target_pairs={{0,8},{1,9},{2,10},{3,11},{4,12},{5,13},{6,14},{7,15},{8,0},{9,1},... | collective-permute-start | bytes 774152 | tf_op jit(solution)/shard_map/ppermute | solution.py:269
  228.9 20.5 %collective-permute-start.14 = (bf16[224,576]{1,0:T(8,128)(2,1)S(1)}, bf16[224,576]{1,0:T(8,128)(2,1)S(1)}, u32[]{:S(2)}, u32[]{:S(2)}) collective-permute-start(bf16[224,576]{1,0:T(8,128)(2,1)S(1)} %bitcast.319), channel_id=1, source_target_pairs={{0,1},{1,0},{2,3},{3,2},{4,5},{5,4},{6,7},{7,6},{8,9},{9,8},{10,11... | collective-permute-start | bytes 774152 | tf_op jit(solution)/shard_map/ppermute | solution.py:269
  268.7 17.0 %collective-permute-start.20 = (bf16[224,192]{1,0:T(8,128)(2,1)}, bf16[224,192]{1,0:T(8,128)(2,1)}, u32[]{:S(2)}, u32[]{:S(2)}) collective-permute-start(bf16[224,192]{1,0:T(8,128)(2,1)} %get-tuple-element.219), channel_id=1, source_target_pairs={{0,9},{1,8},{2,11},{3,10},{4,13},{5,12},{6,15},{7,14},{8,1},{9,0},... | collective-permute-start | bytes 258056 | tf_op jit(solution)/shard_map/ppermute | solution.py:269
  268.7 17.0 %collective-permute-start.19 = (bf16[224,192]{1,0:T(8,128)(2,1)}, bf16[224,192]{1,0:T(8,128)(2,1)}, u32[]{:S(2)}, u32[]{:S(2)}) collective-permute-start(bf16[224,192]{1,0:T(8,128)(2,1)} %get-tuple-element.220), channel_id=1, source_target_pairs={{0,8},{1,9},{2,10},{3,11},{4,12},{5,13},{6,14},{7,15},{8,0},{9,1},... | collective-permute-start | bytes 258056 | tf_op jit(solution)/shard_map/ppermute | solution.py:269
  270.5 20.6 %collective-permute-start.18 = (bf16[224,192]{1,0:T(8,128)(2,1)S(1)}, bf16[224,192]{1,0:T(8,128)(2,1)}, u32[]{:S(2)}, u32[]{:S(2)}) collective-permute-start(bf16[224,192]{1,0:T(8,128)(2,1)S(1)} %get-tuple-element.221), channel_id=1, source_target_pairs={{0,1},{1,0},{2,3},{3,2},{4,5},{5,4},{6,7},{7,6},{8,9},{9,8},{10,11... | collective-permute-start | bytes 258056 | tf_op jit(solution)/shard_map/ppermute | solution.py:269
  273.6 39.5 %collective-permute-start.21 = (f32[112,768]{1,0:T(8,128)}, f32[112,768]{1,0:T(8,128)}, u32[]{:S(2)}, u32[]{:S(2)}) collective-permute-start(f32[112,768]{1,0:T(8,128)} %get-tuple-element.169), channel_id=1, source_target_pairs={{0,2},{1,3},{2,0},{3,1},{4,6},{5,7},{6,4},{7,5},{8,10},{9,11},{10,... | collective-permute-start | bytes 1032200 | tf_op jit(solution)/shard_map/ppermute | solution.py:261
  332.0 282.2 %reduce-scatter.6.cloned.1.call-start = ((), (), s32[]{:S(2)}) async-start(), calls=%async_computation.7 | async-start | bytes 10027008 | tf_op jit(solution)/shard_map/reduce_scatter | solution.py:502
  391.9 18.4 %collective-permute-start.28 = (bf16[224,576]{1,0:T(8,128)(2,1)}, bf16[224,576]{1,0:T(8,128)(2,1)}, u32[]{:S(2)}, u32[]{:S(2)}) collective-permute-start(bf16[224,576]{1,0:T(8,128)(2,1)} %get-tuple-element.191), channel_id=1, source_target_pairs={{0,9},{1,8},{2,11},{3,10},{4,13},{5,12},{6,15},{7,14},{8,1},{9,0},... | collective-permute-start | bytes 774152 | tf_op jit(solution)/shard_map/ppermute | solution.py:269
  393.3 20.8 %collective-permute-start.27 = (bf16[224,576]{1,0:T(8,128)(2,1)}, bf16[224,576]{1,0:T(8,128)(2,1)}, u32[]{:S(2)}, u32[]{:S(2)}) collective-permute-start(bf16[224,576]{1,0:T(8,128)(2,1)} %get-tuple-element.192), channel_id=1, source_target_pairs={{0,8},{1,9},{2,10},{3,11},{4,12},{5,13},{6,14},{7,15},{8,0},{9,1},... | collective-permute-start | bytes 774152 | tf_op jit(solution)/shard_map/ppermute | solution.py:269
  395.1 20.4 %collective-permute-start.26 = (bf16[224,576]{1,0:T(8,128)(2,1)}, bf16[224,576]{1,0:T(8,128)(2,1)}, u32[]{:S(2)}, u32[]{:S(2)}) collective-permute-start(bf16[224,576]{1,0:T(8,128)(2,1)} %get-tuple-element.190), channel_id=1, source_target_pairs={{0,1},{1,0},{2,3},{3,2},{4,5},{5,4},{6,7},{7,6},{8,9},{9,8},{10,11... | collective-permute-start | bytes 774152 | tf_op jit(solution)/shard_map/ppermute | solution.py:269
  428.5 47.5 %collective-permute-start.32 = (bf16[384,3200]{1,0:T(8,128)(2,1)}, bf16[384,3200]{1,0:T(8,128)(2,1)}, u32[]{:S(2)}, u32[]{:S(2)}) collective-permute-start(bf16[384,3200]{1,0:T(8,128)(2,1)} %pad_maximum_fusion.1), channel_id=1, source_target_pairs={{0,4},{4,0},{8,12},{12,8},{1,5},{5,1},{9,13},{13,9},{2,6},{6,2},{1... | collective-permute-start | bytes 7372808 | tf_op jit(solution)/shard_map/ppermute | solution.py:272
  456.1 210.6 %reduce-scatter.8.cloned.1.call-start = ((), (), s32[]{:S(2)}) async-start(), calls=%async_computation.8 | async-start | bytes 3072000 | tf_op jit(solution)/shard_map/reduce_scatter | solution.py:321
  478.2 41.6 %collective-permute-start.33 = (bf16[1,4,48,3200]{3,2,1,0:T(8,128)(2,1)S(1)}, bf16[1,4,48,3200]{3,2,1,0:T(8,128)(2,1)S(1)}, u32[]{:S(2)}, u32[]{:S(2)}) collective-permute-start(bf16[1,4,48,3200]{3,2,1,0:T(8,128)(2,1)S(1)} %fusion.55), channel_id=1, source_target_pairs={{0,8},{4,12},{8,0},{12,4},{1,9},{5,13},{9,1},{13,5},{2,10},{6,14},... | collective-permute-start | bytes 3686408 | tf_op jit(solution)/shard_map/ppermute | solution.py:286
  528.3 14.9 %collective-permute-start.37 = (bf16[224,576]{1,0:T(8,128)(2,1)}, bf16[224,576]{1,0:T(8,128)(2,1)S(1)}, u32[]{:S(2)}, u32[]{:S(2)}) collective-permute-start(bf16[224,576]{1,0:T(8,128)(2,1)} %get-tuple-element.183), channel_id=1, source_target_pairs={{0,9},{1,8},{2,11},{3,10},{4,13},{5,12},{6,15},{7,14},{8,1},{9,0},... | collective-permute-start | bytes 774152 | tf_op jit(solution)/shard_map/ppermute | solution.py:269
  529.9 21.2 %collective-permute-start.36 = (bf16[224,576]{1,0:T(8,128)(2,1)S(1)}, bf16[224,576]{1,0:T(8,128)(2,1)}, u32[]{:S(2)}, u32[]{:S(2)}) collective-permute-start(bf16[224,576]{1,0:T(8,128)(2,1)S(1)} %get-tuple-element.184), channel_id=1, source_target_pairs={{0,8},{1,9},{2,10},{3,11},{4,12},{5,13},{6,14},{7,15},{8,0},{9,1},... | collective-permute-start | bytes 774152 | tf_op jit(solution)/shard_map/ppermute | solution.py:269
  530.1 20.9 %collective-permute-start.35 = (bf16[224,576]{1,0:T(8,128)(2,1)S(1)}, bf16[224,576]{1,0:T(8,128)(2,1)}, u32[]{:S(2)}, u32[]{:S(2)}) collective-permute-start(bf16[224,576]{1,0:T(8,128)(2,1)S(1)} %get-tuple-element.182), channel_id=1, source_target_pairs={{0,1},{1,0},{2,3},{3,2},{4,5},{5,4},{6,7},{7,6},{8,9},{9,8},{10,11... | collective-permute-start | bytes 774152 | tf_op jit(solution)/shard_map/ppermute | solution.py:269
  561.9 48.8 %collective-permute-start.39 = (bf16[1,4,48,3200]{3,2,1,0:T(8,128)(2,1)}, bf16[1,4,48,3200]{3,2,1,0:T(8,128)(2,1)}, u32[]{:S(2)}, u32[]{:S(2)}) collective-permute-start(bf16[1,4,48,3200]{3,2,1,0:T(8,128)(2,1)} %fusion.56), channel_id=1, source_target_pairs={{0,8},{4,12},{8,0},{12,4},{1,9},{5,13},{9,1},{13,5},{2,10},{6,14},... | collective-permute-start | bytes 3686408 | tf_op jit(solution)/shard_map/ppermute | solution.py:286
  562.9 25.0 %collective-permute-start.40 = (bf16[112,768]{1,0:T(8,128)(2,1)}, bf16[112,768]{1,0:T(8,128)(2,1)}, u32[]{:S(2)}, u32[]{:S(2)}) collective-permute-start(bf16[112,768]{1,0:T(8,128)(2,1)} %slice.624), channel_id=1, source_target_pairs={{0,2},{1,3},{2,0},{3,1},{4,6},{5,7},{6,4},{7,5},{8,10},{9,11},{10,... | collective-permute-start | bytes 516104 | tf_op jit(solution)/shard_map/ppermute | solution.py:261
  565.7 31.6 %collective-permute-start.41 = (bf16[112,768]{1,0:T(8,128)(2,1)}, bf16[112,768]{1,0:T(8,128)(2,1)}, u32[]{:S(2)}, u32[]{:S(2)}) collective-permute-start(bf16[112,768]{1,0:T(8,128)(2,1)} %slice.627), channel_id=1, source_target_pairs={{0,2},{1,3},{2,0},{3,1},{4,6},{5,7},{6,4},{7,5},{8,10},{9,11},{10,... | collective-permute-start | bytes 516104 | tf_op jit(solution)/shard_map/ppermute | solution.py:261
  618.7 17.4 %collective-permute-start.45 = (bf16[112,768]{1,0:T(8,128)(2,1)S(1)}, bf16[112,768]{1,0:T(8,128)(2,1)S(1)}, u32[]{:S(2)}, u32[]{:S(2)}) collective-permute-start(bf16[112,768]{1,0:T(8,128)(2,1)S(1)} %slice.897), channel_id=1, source_target_pairs={{0,2},{1,3},{2,0},{3,1},{4,6},{5,7},{6,4},{7,5},{8,10},{9,11},{10,... | collective-permute-start | bytes 516104 | tf_op jit(solution)/shard_map/ppermute | solution.py:261
  637.5 20.6 %collective-permute-start.50 = (bf16[48,6144]{1,0:T(8,128)(2,1)S(1)}, bf16[48,6144]{1,0:T(8,128)(2,1)S(1)}, u32[]{:S(2)}, u32[]{:S(2)}) collective-permute-start(bf16[48,6144]{1,0:T(8,128)(2,1)S(1)} %copy-done.63), channel_id=1, source_target_pairs={{0,16},{1,17},{2,18},{3,19},{4,20},{5,21},{6,22},{7,23},{8,24},{9,... | collective-permute-start | bytes 1769480 | tf_op jit(solution)/shard_map/ppermute | solution.py:610
  (136 other events, 1357.6 us)
Sparse Core Ops, SparseCore 0:
  13.4 78.9 all-gather.3
  95.3 101.0 all-gather.5
  198.7 104.3 all-gather.7
  332.1 121.9 reduce-scatter.3
  458.6 143.2 reduce-scatter.5
  614.4 49.3 reduce-scatter.7
